TPU v7x, 512 devices: a whole 4x4x16 slice. The times are simulated.
512 devices in a mesh: azim: 64 (over z_lo, y, core), block: 8 (over x, z_hi).
Axes of the slice: x: 4, y: 4, z: 16 (z_hi: 2, z_lo: 8; z = z_hi * 8 + z_lo), core: 2. Of those that a mesh axis runs over, the one named last changes fastest.
Arguments:
- flow_state: float32 [5, 512, 256, 128], P(None, 'azim', 'block'), may hold values from -4 to 4
- cotangent: float32 [5, 512, 256, 128], P(None, 'azim', 'block'), may hold values from -6 to 6
- mix_theta: float32 [5, 5], replicated, may hold values from -2.5 to 2.5
- mix_axial: float32 [5, 5], replicated, may hold values from -2.5 to 2.5
- mix_radial: float32 [5, 5], replicated, may hold values from -2.5 to 2.5
- intersection_slot: int32 [512, 3], replicated, may hold values from 0 to 15
- intersection_code: int32 [512, 3], replicated, may hold values from 0 to 7
Outputs:
- advanced: float32 [5, 512, 256, 128], P(None, 'azim', 'block')
- sensitivity: float32 [5, 512, 256, 128], P(None, 'azim', 'block')
Inputs may be any that keep to these rules, and one draw needn't show every extreme that they name: `intersection_slot`: A slot below 8 names a rotor cell of the previous sector, else one of the own sector.
All inputs are finite; a program needn't handle non-finite values.
Results may differ from a plain program's by a relative error of at most 0.00005.
Values sent between devices are 32-bit elements; how exact they have to be, the bound alone decides.
No kernel may reach another device: no remote copies, remote signals or barrier semaphores. Data moves between devices by JAX's collectives and lax.ppermute only.
A program may use at most 64 MiB of HBM per device.

v0:
```python
import jax
import jax.numpy as jnp
from jax import lax
from jax.sharding import PartitionSpec as P

nonlinear_gain = 0.4
time_step = 0.25
forward_rates = (0.55, 0.15, 0.5, 0.2, 0.35, 0.35)
reverse_rates = (0.15, 0.55, 0.2, 0.5, 0.35, 0.35)


def padded(cells, sides, width, closed):
    for axis, dim in sides:
        count = lax.axis_size(axis)
        ends = count if closed else count - 1
        head = lax.slice_in_dim(cells, 0, width, axis=dim)
        tail = lax.slice_in_dim(cells, cells.shape[dim] - width, cells.shape[dim], axis=dim)
        cells = jnp.concatenate(
            [
                lax.ppermute(tail, axis, [(i, (i + 1) % count) for i in range(ends)]),
                cells,
                lax.ppermute(head, axis, [((i + 1) % count, i) for i in range(ends)]),
            ],
            axis=dim,
        )
    return cells


def from_behind(block, axis, distance):
    devices = range(lax.axis_size(axis))
    route = [((i - distance) % len(devices), i) for i in devices]
    return lax.ppermute(block, axis, route)


def mixing(matrix, values_in):
    return jnp.einsum("gf,ftar->gtar", matrix, values_in, precision=lax.Precision.HIGHEST)


def sector_matrix(slot_list, code_list, sector_cells):
    columns = jnp.arange(2 * sector_cells, dtype=jnp.int32)
    matches = (slot_list[:, :, None] == columns[None, None, :]).astype(jnp.float32)
    weights = (code_list.astype(jnp.float32) + 1.0) / 12.0
    return jnp.sum(matches * weights[:, :, None], axis=1)


def shards(
    flow_state, cotangent, mix_theta, mix_axial, mix_radial, intersection_slot, intersection_code
):
    sector_cells = flow_state.shape[1]
    sector_index = lax.axis_index("azim")
    n_sector = lax.axis_size("azim")
    block_index = lax.axis_index("block")
    n_block = lax.axis_size("block")
    own_start = sector_index * sector_cells
    next_start = (sector_index + 1) % n_sector * sector_cells
    own_matrix = sector_matrix(
        lax.dynamic_slice_in_dim(intersection_slot, own_start, sector_cells, 0),
        lax.dynamic_slice_in_dim(intersection_code, own_start, sector_cells, 0),
        sector_cells,
    )
    next_matrix = sector_matrix(
        lax.dynamic_slice_in_dim(intersection_slot, next_start, sector_cells, 0),
        lax.dynamic_slice_in_dim(intersection_code, next_start, sector_cells, 0),
        sector_cells,
    )
    is_stator = block_index == n_block // 2
    is_rotor = block_index == n_block // 2 - 1
    forward_mixers = (mix_theta, mix_axial, mix_radial)
    reverse_mixers = (mix_theta.T, mix_axial.T, mix_radial.T)

    def neighbours(values_in):
        theta_pad = padded(values_in, (("azim", 1),), 1, True)
        axial_pad = padded(values_in, (("block", 2),), 1, False)
        rotor_low = axial_pad[:, :, 0]
        stator_up = axial_pad[:, :, -1]
        prior_rim = from_behind(rotor_low, "azim", 1)
        later_rim = from_behind(stator_up, "azim", -1)
        window = jnp.concatenate([prior_rim, rotor_low], axis=1)
        from_rotor = jnp.einsum("tj,fjr->ftr", own_matrix, window, precision=lax.Precision.HIGHEST)
        to_rotor = jnp.einsum(
            "jt,fjr->ftr", own_matrix[:, sector_cells:], stator_up, precision=lax.Precision.HIGHEST
        )
        to_rotor = to_rotor + jnp.einsum(
            "jt,fjr->ftr", next_matrix[:, :sector_cells], later_rim, precision=lax.Precision.HIGHEST
        )
        lower_side = jnp.concatenate(
            [jnp.where(is_stator, from_rotor, rotor_low)[:, :, None], axial_pad[:, :, 1:-2]], axis=2
        )
        upper_side = jnp.concatenate(
            [axial_pad[:, :, 2:-1], jnp.where(is_rotor, to_rotor, stator_up)[:, :, None]], axis=2
        )
        return (theta_pad, lower_side, upper_side)

    def combine(values_in, theta_pad, lower_side, upper_side, coefficients, mixers):
        theta_low, theta_high, axial_low, axial_high, radial_low, radial_high = coefficients
        theta_term = (
            theta_low * theta_pad[:, :-2]
            + theta_high * theta_pad[:, 2:]
            - (theta_low + theta_high) * values_in
        )
        axial_term = (
            axial_low * lower_side + axial_high * upper_side - (axial_low + axial_high) * values_in
        )
        radial_pad = jnp.pad(values_in, ((0, 0), (0, 0), (0, 0), (1, 1)))
        radial_term = (
            radial_low * radial_pad[..., :-2]
            + radial_high * radial_pad[..., 2:]
            - (radial_low + radial_high) * values_in
        )
        return (
            mixing(mixers[0], theta_term)
            + mixing(mixers[1], axial_term)
            + mixing(mixers[2], radial_term)
        )

    def operator(values_in, coefficients, mixers):
        theta_pad, lower_side, upper_side = neighbours(values_in)
        return combine(values_in, theta_pad, lower_side, upper_side, coefficients, mixers)

    def shaping(values_in):
        return values_in + 0.5 * nonlinear_gain * values_in * values_in

    first_residual = operator(shaping(flow_state), forward_rates, forward_mixers)
    reverse_raw = None
    section_one = flow_state + time_step * first_residual
    advanced = 0.5 * flow_state + 0.5 * (
        section_one + time_step * operator(shaping(section_one), forward_rates, forward_mixers)
    )
    reverse_raw = operator(cotangent, reverse_rates, reverse_mixers)
    adjoint_one = (
        0.5 * cotangent + 0.5 * time_step * (1.0 + nonlinear_gain * section_one) * reverse_raw
    )
    sensitivity = (
        0.5 * cotangent
        + adjoint_one
        + time_step
        * (1.0 + nonlinear_gain * flow_state)
        * operator(adjoint_one, reverse_rates, reverse_mixers)
    )
    return (advanced, sensitivity)


def solution(mesh):
    placed = (
        P(None, "azim", "block", None),
        P(None, "azim", "block", None),
        P(),
        P(),
        P(),
        P(),
        P(),
    )
    return jax.shard_map(
        shards,
        mesh=mesh,
        in_specs=placed,
        out_specs=(P(None, "azim", "block", None), P(None, "azim", "block", None)),
        check_vma=False,
    )
```

profile of v0, /device:TPU:3, one launch (start us, length us, event | category | flops | bytes accessed | tf_op | source)
XLA Modules:
  0.0 203.8 jit_solution(10938870480812573110)
XLA Ops:
  0.7 1.0 fusion.147
  1.7 0.7 copy.217
  2.4 2.6 %collective-permute-start.13 = (f32[5,1,32,128]{3,1,0,2:T(1,128)}, f32[5,1,32,128]{3,1,0,2:T(1,128)S(1)}, u32[]{:S(2)}, u32[]{:S(2)}) collective-permute-start(f32[5,1,32,128]{3,1,0,2:T(1,128)} %copy.217), channel_id=1, source_target_pairs={{8,0},{16,8},{24,16},{32,24},{40,32},{48,40},{56,48},{64,56},{72,6... | collective-permute-start | bytes 245768 | tf_op jit(solution)/shard_map/ppermute | solution.py:22
  5.0 0.7 copy.215
  5.7 3.1 %collective-permute-start.12 = (f32[5,1,32,128]{3,1,0,2:T(1,128)}, f32[5,1,32,128]{3,1,0,2:T(1,128)S(1)}, u32[]{:S(2)}, u32[]{:S(2)}) collective-permute-start(f32[5,1,32,128]{3,1,0,2:T(1,128)} %copy.215), channel_id=1, source_target_pairs={{0,8},{8,16},{16,24},{24,32},{32,40},{40,48},{48,56},{56,64},{64,7... | collective-permute-start | bytes 245768 | tf_op jit(solution)/shard_map/ppermute | solution.py:20
  8.8 1.5 multiply_add_fusion.1
  10.3 15.4 %collective-permute-start.4 = (f32[5,8,1,128]{3,1,0,2:T(8,128)S(1)}, f32[5,8,1,128]{3,1,0,2:T(8,128)}, u32[]{:S(2)}, u32[]{:S(2)}) collective-permute-start(f32[5,8,1,128]{3,1,0,2:T(8,128)S(1)} %get-tuple-element.38), channel_id=1, source_target_pairs={{1,0},{2,1},{3,2},{4,3},{5,4},{6,5},{7,6},{9,8},{10,9},{11,10},{12... | collective-permute-start | bytes 61448 | tf_op jit(solution)/shard_map/ppermute | solution.py:22
  25.7 0.4 copy.214
  26.1 0.6 fusion.149
  26.7 2.7 %collective-permute-start.16 = (f32[5,8,1,128]{3,1,0,2:T(8,128)}, f32[5,8,1,128]{3,1,0,2:T(8,128)}, u32[]{:S(2)}, u32[]{:S(2)}) collective-permute-start(f32[5,8,1,128]{3,1,0,2:T(8,128)} %get-tuple-element.46), channel_id=1, source_target_pairs={{1,0},{2,1},{3,2},{4,3},{5,4},{6,5},{7,6},{9,8},{10,9},{11,10},{12... | collective-permute-start | bytes 61448 | tf_op jit(solution)/shard_map/ppermute | solution.py:22
  29.5 11.2 %collective-permute-start.14 = (f32[5,8,1,128]{3,1,0,2:T(8,128)}, f32[5,8,1,128]{3,1,0,2:T(8,128)S(1)}, u32[]{:S(2)}, u32[]{:S(2)}) collective-permute-start(f32[5,8,1,128]{3,1,0,2:T(8,128)} %get-tuple-element.47), channel_id=1, source_target_pairs={{0,1},{1,2},{2,3},{3,4},{4,5},{5,6},{6,7},{8,9},{9,10},{10,11},{11... | collective-permute-start | bytes 61448 | tf_op jit(solution)/shard_map/ppermute | solution.py:20
  40.8 0.7 fusion.144
  41.5 1.1 fusion.148
  42.7 0.8 constant_dynamic-slice_fusion
  43.5 0.8 add_multiply_fusion
  44.5 7.2 %collective-permute-start.17 = (f32[5,8,128]{2,1,0:T(8,128)}, f32[5,8,128]{2,1,0:T(8,128)}, u32[]{:S(2)}, u32[]{:S(2)}) collective-permute-start(f32[5,8,128]{2,1,0:T(8,128)} %bitcast.30), channel_id=1, source_target_pairs={{8,0},{16,8},{24,16},{32,24},{40,32},{48,40},{56,48},{64,56},{72,6... | collective-permute-start | bytes 61448 | tf_op jit(solution)/shard_map/ppermute | solution.py:32
  51.8 7.0 %collective-permute-start.2 = (f32[5,8,1,128]{3,1,0,2:T(8,128)S(1)}, f32[5,8,1,128]{3,1,0,2:T(8,128)S(1)}, u32[]{:S(2)}, u32[]{:S(2)}) collective-permute-start(f32[5,8,1,128]{3,1,0,2:T(8,128)S(1)} %get-tuple-element.39), channel_id=1, source_target_pairs={{0,1},{1,2},{2,3},{3,4},{4,5},{5,6},{6,7},{8,9},{9,10},{10,11},{11... | collective-permute-start | bytes 61448 | tf_op jit(solution)/shard_map/ppermute | solution.py:20
  58.8 1.9 collective-permute-start.15
  60.7 0.9 fusion.96
  61.7 1.1 fusion.7
  62.8 1.9 collective-permute-start
  64.7 6.4 %collective-permute-done.15 = f32[5,8,128]{2,1,0:T(8,128)S(1)} collective-permute-done((f32[5,8,128]{2,1,0:T(8,128)S(1)}, f32[5,8,128]{2,1,0:T(8,128)S(1)}, u32[]{:S(2)}, u32[]{:S(2)}) %collective-permute-start.15) | collective-permute-done | bytes 20512 | tf_op jit(solution)/shard_map/ppermute | solution.py:32
  71.1 13.1 %collective-permute-start.5 = (f32[5,8,128]{2,1,0:T(8,128)}, f32[5,8,128]{2,1,0:T(8,128)S(1)}, u32[]{:S(2)}, u32[]{:S(2)}) collective-permute-start(f32[5,8,128]{2,1,0:T(8,128)} %bitcast.6), channel_id=1, source_target_pairs={{8,0},{16,8},{24,16},{32,24},{40,32},{48,40},{56,48},{64,56},{72,6... | collective-permute-start | bytes 61448 | tf_op jit(solution)/shard_map/ppermute | solution.py:32
  84.4 1.8 fusion.72
  86.2 1.1 fusion.27
  87.3 4.5 %collective-permute-start.1 = (f32[5,1,32,128]{3,1,0,2:T(1,128)S(1)}, f32[5,1,32,128]{3,1,0,2:T(1,128)S(1)}, u32[]{:S(2)}, u32[]{:S(2)}) collective-permute-start(f32[5,1,32,128]{3,1,0,2:T(1,128)S(1)} %get-tuple-element.35), channel_id=1, source_target_pairs={{8,0},{16,8},{24,16},{32,24},{40,32},{48,40},{56,48},{64,56},{72,6... | collective-permute-start | bytes 245768 | tf_op jit(solution)/shard_map/ppermute | solution.py:22
  91.9 2.1 %collective-permute-start.3 = (f32[5,8,128]{2,1,0:T(8,128)S(1)}, f32[5,8,128]{2,1,0:T(8,128)S(1)}, u32[]{:S(2)}, u32[]{:S(2)}) collective-permute-start(f32[5,8,128]{2,1,0:T(8,128)S(1)} %bitcast.177), channel_id=1, source_target_pairs={{504,0},{0,8},{8,16},{16,24},{24,32},{32,40},{40,48},{48,56},{56,6... | collective-permute-start | bytes 61448 | tf_op jit(solution)/shard_map/ppermute | solution.py:32
  94.2 1.1 fusion.16
  95.5 0.5 fusion.68
  96.0 1.1 fusion.39
  97.2 0.5 fusion.57
  97.8 1.1 fusion.29
  99.0 0.5 fusion.65
  99.5 1.1 fusion.41
  100.6 1.1 fusion.25
  101.7 1.1 fusion.37
  102.8 3.3 %fusion.74 = (f32[5,8,32,128]{3,1,0,2:T(8,128)S(1)}, f32[5,8,32,128]{3,1,0,2:T(8,128)S(1)}) fusion(f32[8,32,128,5]{2,3,1,0:T(8,128)S(1)} %fusion.25, f32[8,32,128,5]{2,3,1,0:T(8,128)S(1)} %fusion.27, f32[8,32,128,5]{2,3,1,0:T(8,128)S(1)} %fusion.29, f32[5,8,32,128]{3,2,1,0:T(8,128)S(1)} %copy-done.1, f32[8,32,128,5]{2,3,1,0:T(8,128)S(1)} %fusion.37, ...), kind=kLoop, calls=%fused_computation.110 | loop fusion | flops 1966080 | bytes 6553600 | tf_op jit(solution)/shard_map/add | solution.py:131
  106.5 7.9 %collective-permute-start.8 = (f32[5,8,1,128]{3,1,0,2:T(8,128)S(1)}, f32[5,8,1,128]{3,1,0,2:T(8,128)S(1)}, u32[]{:S(2)}, u32[]{:S(2)}) collective-permute-start(f32[5,8,1,128]{3,1,0,2:T(8,128)S(1)} %get-tuple-element.28), channel_id=1, source_target_pairs={{0,1},{1,2},{2,3},{3,4},{4,5},{5,6},{6,7},{8,9},{9,10},{10,11},{11... | collective-permute-start | bytes 61448 | tf_op jit(solution)/shard_map/ppermute | solution.py:20
  114.6 7.0 %collective-permute-start.10 = (f32[5,8,1,128]{3,1,0,2:T(8,128)S(1)}, f32[5,8,1,128]{3,1,0,2:T(8,128)S(1)}, u32[]{:S(2)}, u32[]{:S(2)}) collective-permute-start(f32[5,8,1,128]{3,1,0,2:T(8,128)S(1)} %get-tuple-element.29), channel_id=1, source_target_pairs={{1,0},{2,1},{3,2},{4,3},{5,4},{6,5},{7,6},{9,8},{10,9},{11,10},{12... | collective-permute-start | bytes 61448 | tf_op jit(solution)/shard_map/ppermute | solution.py:22
  121.6 4.1 %collective-permute-start.9 = (f32[5,8,128]{2,1,0:T(8,128)S(1)}, f32[5,8,128]{2,1,0:T(8,128)S(1)}, u32[]{:S(2)}, u32[]{:S(2)}) collective-permute-start(f32[5,8,128]{2,1,0:T(8,128)S(1)} %bitcast.179), channel_id=1, source_target_pairs={{504,0},{0,8},{8,16},{16,24},{24,32},{32,40},{40,48},{48,56},{56,6... | collective-permute-start | bytes 61448 | tf_op jit(solution)/shard_map/ppermute | solution.py:32
  125.7 7.0 %collective-permute-start.20 = (f32[5,8,1,128]{3,1,0,2:T(8,128)S(1)}, f32[5,8,1,128]{3,1,0,2:T(8,128)S(1)}, u32[]{:S(2)}, u32[]{:S(2)}) collective-permute-start(f32[5,8,1,128]{3,1,0,2:T(8,128)S(1)} %get-tuple-element.18), channel_id=1, source_target_pairs={{0,1},{1,2},{2,3},{3,4},{4,5},{5,6},{6,7},{8,9},{9,10},{10,11},{11... | collective-permute-start | bytes 61448 | tf_op jit(solution)/shard_map/ppermute | solution.py:20
  132.8 7.9 %collective-permute-start.22 = (f32[5,8,1,128]{3,1,0,2:T(8,128)S(1)}, f32[5,8,1,128]{3,1,0,2:T(8,128)S(1)}, u32[]{:S(2)}, u32[]{:S(2)}) collective-permute-start(f32[5,8,1,128]{3,1,0,2:T(8,128)S(1)} %get-tuple-element.19), channel_id=1, source_target_pairs={{1,0},{2,1},{3,2},{4,3},{5,4},{6,5},{7,6},{9,8},{10,9},{11,10},{12... | collective-permute-start | bytes 61448 | tf_op jit(solution)/shard_map/ppermute | solution.py:22
  140.6 2.5 %collective-permute-start.18 = (f32[5,1,32,128]{3,1,0,2:T(1,128)S(1)}, f32[5,1,32,128]{3,1,0,2:T(1,128)S(1)}, u32[]{:S(2)}, u32[]{:S(2)}) collective-permute-start(f32[5,1,32,128]{3,1,0,2:T(1,128)S(1)} %get-tuple-element.16), channel_id=1, source_target_pairs={{0,8},{8,16},{16,24},{24,32},{32,40},{40,48},{48,56},{56,64},{64,7... | collective-permute-start | bytes 245768 | tf_op jit(solution)/shard_map/ppermute | solution.py:20
  143.3 11.3 %collective-permute-start.19 = (f32[5,1,32,128]{3,1,0,2:T(1,128)S(1)}, f32[5,1,32,128]{3,1,0,2:T(1,128)S(1)}, u32[]{:S(2)}, u32[]{:S(2)}) collective-permute-start(f32[5,1,32,128]{3,1,0,2:T(1,128)S(1)} %get-tuple-element.17), channel_id=1, source_target_pairs={{8,0},{16,8},{24,16},{32,24},{40,32},{48,40},{56,48},{64,56},{72,6... | collective-permute-start | bytes 245768 | tf_op jit(solution)/shard_map/ppermute | solution.py:22
  154.6 12.4 %collective-permute-start.11 = (f32[5,8,128]{2,1,0:T(8,128)S(1)}, f32[5,8,128]{2,1,0:T(8,128)S(1)}, u32[]{:S(2)}, u32[]{:S(2)}) collective-permute-start(f32[5,8,128]{2,1,0:T(8,128)S(1)} %bitcast.182), channel_id=1, source_target_pairs={{8,0},{16,8},{24,16},{32,24},{40,32},{48,40},{56,48},{64,56},{72,6... | collective-permute-start | bytes 61448 | tf_op jit(solution)/shard_map/ppermute | solution.py:32
  167.2 1.9 collective-permute-start.6
  169.1 1.9 collective-permute-start.21
  171.3 0.3 fusion.11
  171.6 0.3 copy_multiply_fusion.4
  171.9 1.4 fusion.33
  173.3 2.4 %collective-permute-start.7 = (f32[5,1,32,128]{3,1,0,2:T(1,128)S(1)}, f32[5,1,32,128]{3,1,0,2:T(1,128)S(1)}, u32[]{:S(2)}, u32[]{:S(2)}) collective-permute-start(f32[5,1,32,128]{3,1,0,2:T(1,128)S(1)} %get-tuple-element.27), channel_id=1, source_target_pairs={{8,0},{16,8},{24,16},{32,24},{40,32},{48,40},{56,48},{64,56},{72,6... | collective-permute-start | bytes 245768 | tf_op jit(solution)/shard_map/ppermute | solution.py:22
  175.7 12.6 %collective-permute-start.23 = (f32[5,8,128]{2,1,0:T(8,128)S(1)}, f32[5,8,128]{2,1,0:T(8,128)S(1)}, u32[]{:S(2)}, u32[]{:S(2)}) collective-permute-start(f32[5,8,128]{2,1,0:T(8,128)S(1)} %bitcast.181), channel_id=1, source_target_pairs={{8,0},{16,8},{24,16},{32,24},{40,32},{48,40},{56,48},{64,56},{72,6... | collective-permute-start | bytes 61448 | tf_op jit(solution)/shard_map/ppermute | solution.py:32
  188.5 0.4 collective-permute-done.23
  189.5 0.4 copy_multiply_fusion.2
  189.8 1.4 fusion.21
  191.2 0.9 fusion.61
  192.5 1.4 fusion.31
  193.8 1.1 fusion.35
  194.9 0.9 fusion.53
  195.9 1.1 fusion.23
  197.3 1.4 fusion.19
  198.7 3.2 %fusion.73 = (f32[5,8,32,128]{3,1,0,2:T(8,128)S(1)}, f32[5,8,32,128]{3,1,0,2:T(8,128)S(1)}) fusion(f32[8,32,128,5]{2,3,1,0:T(8,128)S(1)} %fusion.19, f32[8,32,128,5]{2,3,1,0:T(8,128)S(1)} %fusion.21, f32[8,32,128,5]{2,3,1,0:T(8,128)S(1)} %fusion.23, f32[5,8,32,128]{3,1,0,2:T(8,128)S(1)} %get-tuple-element.8, f32[5,8,32,128]{3,2,1,0:T(8,128)S(1)} %copy-done.2, ...), kind=kLoop, calls=%fused_computation.108 | loop fusion | flops 2457600 | bytes 7864320 | tf_op jit(solution)/shard_map/add | solution.py:134
  201.8 1.0 copy.253
  202.8 1.0 copy.252
  (57 shorter events, 3.3 us)
Async XLA Ops:
  0.6 85.6 %copy-start = (f32[5,5]{1,0:T(8,128)S(1)}, f32[5,5]{1,0:T(8,128)}, u32[]{:S(2)}) copy-start(f32[5,5]{1,0:T(8,128)} %param.10) | copy-start | bytes 304
  0.6 25.1 %copy-start.1 = (f32[5,8,32,128]{3,2,1,0:T(8,128)S(1)}, f32[5,8,32,128]{3,2,1,0:T(8,128)}, u32[]{:S(2)}) copy-start(f32[5,8,32,128]{3,2,1,0:T(8,128)} %param.8) | copy-start | bytes 1966084
  2.4 94.8 %collective-permute-start.13 = (f32[5,1,32,128]{3,1,0,2:T(1,128)}, f32[5,1,32,128]{3,1,0,2:T(1,128)S(1)}, u32[]{:S(2)}, u32[]{:S(2)}) collective-permute-start(f32[5,1,32,128]{3,1,0,2:T(1,128)} %copy.217), channel_id=1, source_target_pairs={{8,0},{16,8},{24,16},{32,24},{40,32},{48,40},{56,48},{64,56},{72,6... | collective-permute-start | bytes 245768 | tf_op jit(solution)/shard_map/ppermute | solution.py:22
  5.7 91.5 %collective-permute-start.12 = (f32[5,1,32,128]{3,1,0,2:T(1,128)}, f32[5,1,32,128]{3,1,0,2:T(1,128)S(1)}, u32[]{:S(2)}, u32[]{:S(2)}) collective-permute-start(f32[5,1,32,128]{3,1,0,2:T(1,128)} %copy.215), channel_id=1, source_target_pairs={{0,8},{8,16},{16,24},{24,32},{32,40},{40,48},{48,56},{56,64},{64,7... | collective-permute-start | bytes 245768 | tf_op jit(solution)/shard_map/ppermute | solution.py:20
  10.3 52.5 %collective-permute-start.4 = (f32[5,8,1,128]{3,1,0,2:T(8,128)S(1)}, f32[5,8,1,128]{3,1,0,2:T(8,128)}, u32[]{:S(2)}, u32[]{:S(2)}) collective-permute-start(f32[5,8,1,128]{3,1,0,2:T(8,128)S(1)} %get-tuple-element.38), channel_id=1, source_target_pairs={{1,0},{2,1},{3,2},{4,3},{5,4},{6,5},{7,6},{9,8},{10,9},{11,10},{12... | collective-permute-start | bytes 61448 | tf_op jit(solution)/shard_map/ppermute | solution.py:22
  26.7 17.7 %collective-permute-start.16 = (f32[5,8,1,128]{3,1,0,2:T(8,128)}, f32[5,8,1,128]{3,1,0,2:T(8,128)}, u32[]{:S(2)}, u32[]{:S(2)}) collective-permute-start(f32[5,8,1,128]{3,1,0,2:T(8,128)} %get-tuple-element.46), channel_id=1, source_target_pairs={{1,0},{2,1},{3,2},{4,3},{5,4},{6,5},{7,6},{9,8},{10,9},{11,10},{12... | collective-permute-start | bytes 61448 | tf_op jit(solution)/shard_map/ppermute | solution.py:22
  29.5 22.3 %collective-permute-start.14 = (f32[5,8,1,128]{3,1,0,2:T(8,128)}, f32[5,8,1,128]{3,1,0,2:T(8,128)S(1)}, u32[]{:S(2)}, u32[]{:S(2)}) collective-permute-start(f32[5,8,1,128]{3,1,0,2:T(8,128)} %get-tuple-element.47), channel_id=1, source_target_pairs={{0,1},{1,2},{2,3},{3,4},{4,5},{5,6},{6,7},{8,9},{9,10},{10,11},{11... | collective-permute-start | bytes 61448 | tf_op jit(solution)/shard_map/ppermute | solution.py:20
  44.5 14.3 %collective-permute-start.17 = (f32[5,8,128]{2,1,0:T(8,128)}, f32[5,8,128]{2,1,0:T(8,128)}, u32[]{:S(2)}, u32[]{:S(2)}) collective-permute-start(f32[5,8,128]{2,1,0:T(8,128)} %bitcast.30), channel_id=1, source_target_pairs={{8,0},{16,8},{24,16},{32,24},{40,32},{48,40},{56,48},{64,56},{72,6... | collective-permute-start | bytes 61448 | tf_op jit(solution)/shard_map/ppermute | solution.py:32
  51.8 35.6 %collective-permute-start.2 = (f32[5,8,1,128]{3,1,0,2:T(8,128)S(1)}, f32[5,8,1,128]{3,1,0,2:T(8,128)S(1)}, u32[]{:S(2)}, u32[]{:S(2)}) collective-permute-start(f32[5,8,1,128]{3,1,0,2:T(8,128)S(1)} %get-tuple-element.39), channel_id=1, source_target_pairs={{0,1},{1,2},{2,3},{3,4},{4,5},{5,6},{6,7},{8,9},{9,10},{10,11},{11... | collective-permute-start | bytes 61448 | tf_op jit(solution)/shard_map/ppermute | solution.py:20
  58.8 12.4 %collective-permute-start.15 = (f32[5,8,128]{2,1,0:T(8,128)S(1)}, f32[5,8,128]{2,1,0:T(8,128)S(1)}, u32[]{:S(2)}, u32[]{:S(2)}) collective-permute-start(f32[5,8,128]{2,1,0:T(8,128)S(1)} %bitcast.173), channel_id=1, source_target_pairs={{504,0},{0,8},{8,16},{16,24},{24,32},{32,40},{40,48},{48,56},{56,6... | collective-permute-start | bytes 61448 | tf_op jit(solution)/shard_map/ppermute | solution.py:32
  62.8 36.2 %collective-permute-start = (f32[5,1,32,128]{3,1,0,2:T(1,128)}, f32[5,1,32,128]{3,1,0,2:T(1,128)S(1)}, u32[]{:S(2)}, u32[]{:S(2)}) collective-permute-start(f32[5,1,32,128]{3,1,0,2:T(1,128)} %get-tuple-element.34), channel_id=1, source_target_pairs={{0,8},{8,16},{16,24},{24,32},{32,40},{40,48},{48,56},{56,64},{64,7... | collective-permute-start | bytes 245768 | tf_op jit(solution)/shard_map/ppermute | solution.py:20
  71.1 20.7 %collective-permute-start.5 = (f32[5,8,128]{2,1,0:T(8,128)}, f32[5,8,128]{2,1,0:T(8,128)S(1)}, u32[]{:S(2)}, u32[]{:S(2)}) collective-permute-start(f32[5,8,128]{2,1,0:T(8,128)} %bitcast.6), channel_id=1, source_target_pairs={{8,0},{16,8},{24,16},{32,24},{40,32},{48,40},{56,48},{64,56},{72,6... | collective-permute-start | bytes 61448 | tf_op jit(solution)/shard_map/ppermute | solution.py:32
  86.2 9.3 %copy-start.2 = (f32[5,8,32,128]{3,2,1,0:T(8,128)S(1)}, f32[5,8,32,128]{3,2,1,0:T(8,128)}, u32[]{:S(2)}) copy-start(f32[5,8,32,128]{3,2,1,0:T(8,128)} %param.7) | copy-start | bytes 1966084
  87.3 11.6 %collective-permute-start.1 = (f32[5,1,32,128]{3,1,0,2:T(1,128)S(1)}, f32[5,1,32,128]{3,1,0,2:T(1,128)S(1)}, u32[]{:S(2)}, u32[]{:S(2)}) collective-permute-start(f32[5,1,32,128]{3,1,0,2:T(1,128)S(1)} %get-tuple-element.35), channel_id=1, source_target_pairs={{8,0},{16,8},{24,16},{32,24},{40,32},{48,40},{56,48},{64,56},{72,6... | collective-permute-start | bytes 245768 | tf_op jit(solution)/shard_map/ppermute | solution.py:22
  91.9 3.4 %collective-permute-start.3 = (f32[5,8,128]{2,1,0:T(8,128)S(1)}, f32[5,8,128]{2,1,0:T(8,128)S(1)}, u32[]{:S(2)}, u32[]{:S(2)}) collective-permute-start(f32[5,8,128]{2,1,0:T(8,128)S(1)} %bitcast.177), channel_id=1, source_target_pairs={{504,0},{0,8},{8,16},{16,24},{24,32},{32,40},{40,48},{48,56},{56,6... | collective-permute-start | bytes 61448 | tf_op jit(solution)/shard_map/ppermute | solution.py:32
  97.1 0.7 copy-start.3
  99.5 1.1 copy-start.4
  106.5 15.0 %collective-permute-start.8 = (f32[5,8,1,128]{3,1,0,2:T(8,128)S(1)}, f32[5,8,1,128]{3,1,0,2:T(8,128)S(1)}, u32[]{:S(2)}, u32[]{:S(2)}) collective-permute-start(f32[5,8,1,128]{3,1,0,2:T(8,128)S(1)} %get-tuple-element.28), channel_id=1, source_target_pairs={{0,1},{1,2},{2,3},{3,4},{4,5},{5,6},{6,7},{8,9},{9,10},{10,11},{11... | collective-permute-start | bytes 61448 | tf_op jit(solution)/shard_map/ppermute | solution.py:20
  114.6 28.7 %collective-permute-start.10 = (f32[5,8,1,128]{3,1,0,2:T(8,128)S(1)}, f32[5,8,1,128]{3,1,0,2:T(8,128)S(1)}, u32[]{:S(2)}, u32[]{:S(2)}) collective-permute-start(f32[5,8,1,128]{3,1,0,2:T(8,128)S(1)} %get-tuple-element.29), channel_id=1, source_target_pairs={{1,0},{2,1},{3,2},{4,3},{5,4},{6,5},{7,6},{9,8},{10,9},{11,10},{12... | collective-permute-start | bytes 61448 | tf_op jit(solution)/shard_map/ppermute | solution.py:22
  121.6 33.0 %collective-permute-start.9 = (f32[5,8,128]{2,1,0:T(8,128)S(1)}, f32[5,8,128]{2,1,0:T(8,128)S(1)}, u32[]{:S(2)}, u32[]{:S(2)}) collective-permute-start(f32[5,8,128]{2,1,0:T(8,128)S(1)} %bitcast.179), channel_id=1, source_target_pairs={{504,0},{0,8},{8,16},{16,24},{24,32},{32,40},{40,48},{48,56},{56,6... | collective-permute-start | bytes 61448 | tf_op jit(solution)/shard_map/ppermute | solution.py:32
  125.7 41.4 %collective-permute-start.20 = (f32[5,8,1,128]{3,1,0,2:T(8,128)S(1)}, f32[5,8,1,128]{3,1,0,2:T(8,128)S(1)}, u32[]{:S(2)}, u32[]{:S(2)}) collective-permute-start(f32[5,8,1,128]{3,1,0,2:T(8,128)S(1)} %get-tuple-element.18), channel_id=1, source_target_pairs={{0,1},{1,2},{2,3},{3,4},{4,5},{5,6},{6,7},{8,9},{9,10},{10,11},{11... | collective-permute-start | bytes 61448 | tf_op jit(solution)/shard_map/ppermute | solution.py:20
  132.8 40.5 %collective-permute-start.22 = (f32[5,8,1,128]{3,1,0,2:T(8,128)S(1)}, f32[5,8,1,128]{3,1,0,2:T(8,128)S(1)}, u32[]{:S(2)}, u32[]{:S(2)}) collective-permute-start(f32[5,8,1,128]{3,1,0,2:T(8,128)S(1)} %get-tuple-element.19), channel_id=1, source_target_pairs={{1,0},{2,1},{3,2},{4,3},{5,4},{6,5},{7,6},{9,8},{10,9},{11,10},{12... | collective-permute-start | bytes 61448 | tf_op jit(solution)/shard_map/ppermute | solution.py:22
  140.6 54.3 %collective-permute-start.18 = (f32[5,1,32,128]{3,1,0,2:T(1,128)S(1)}, f32[5,1,32,128]{3,1,0,2:T(1,128)S(1)}, u32[]{:S(2)}, u32[]{:S(2)}) collective-permute-start(f32[5,1,32,128]{3,1,0,2:T(1,128)S(1)} %get-tuple-element.16), channel_id=1, source_target_pairs={{0,8},{8,16},{16,24},{24,32},{32,40},{40,48},{48,56},{56,64},{64,7... | collective-permute-start | bytes 245768 | tf_op jit(solution)/shard_map/ppermute | solution.py:20
  143.3 51.7 %collective-permute-start.19 = (f32[5,1,32,128]{3,1,0,2:T(1,128)S(1)}, f32[5,1,32,128]{3,1,0,2:T(1,128)S(1)}, u32[]{:S(2)}, u32[]{:S(2)}) collective-permute-start(f32[5,1,32,128]{3,1,0,2:T(1,128)S(1)} %get-tuple-element.17), channel_id=1, source_target_pairs={{8,0},{16,8},{24,16},{32,24},{40,32},{48,40},{56,48},{64,56},{72,6... | collective-permute-start | bytes 245768 | tf_op jit(solution)/shard_map/ppermute | solution.py:22
  154.6 14.5 %collective-permute-start.11 = (f32[5,8,128]{2,1,0:T(8,128)S(1)}, f32[5,8,128]{2,1,0:T(8,128)S(1)}, u32[]{:S(2)}, u32[]{:S(2)}) collective-permute-start(f32[5,8,128]{2,1,0:T(8,128)S(1)} %bitcast.182), channel_id=1, source_target_pairs={{8,0},{16,8},{24,16},{32,24},{40,32},{48,40},{56,48},{64,56},{72,6... | collective-permute-start | bytes 61448 | tf_op jit(solution)/shard_map/ppermute | solution.py:32
  167.2 24.1 %collective-permute-start.6 = (f32[5,1,32,128]{3,1,0,2:T(1,128)S(1)}, f32[5,1,32,128]{3,1,0,2:T(1,128)S(1)}, u32[]{:S(2)}, u32[]{:S(2)}) collective-permute-start(f32[5,1,32,128]{3,1,0,2:T(1,128)S(1)} %get-tuple-element.26), channel_id=1, source_target_pairs={{0,8},{8,16},{16,24},{24,32},{32,40},{40,48},{48,56},{56,64},{64,7... | collective-permute-start | bytes 245768 | tf_op jit(solution)/shard_map/ppermute | solution.py:20
  169.1 6.6 %collective-permute-start.21 = (f32[5,8,128]{2,1,0:T(8,128)S(1)}, f32[5,8,128]{2,1,0:T(8,128)S(1)}, u32[]{:S(2)}, u32[]{:S(2)}) collective-permute-start(f32[5,8,128]{2,1,0:T(8,128)S(1)} %bitcast.175), channel_id=1, source_target_pairs={{504,0},{0,8},{8,16},{16,24},{24,32},{32,40},{40,48},{48,56},{56,6... | collective-permute-start | bytes 61448 | tf_op jit(solution)/shard_map/ppermute | solution.py:32
  173.3 18.0 %collective-permute-start.7 = (f32[5,1,32,128]{3,1,0,2:T(1,128)S(1)}, f32[5,1,32,128]{3,1,0,2:T(1,128)S(1)}, u32[]{:S(2)}, u32[]{:S(2)}) collective-permute-start(f32[5,1,32,128]{3,1,0,2:T(1,128)S(1)} %get-tuple-element.27), channel_id=1, source_target_pairs={{8,0},{16,8},{24,16},{32,24},{40,32},{48,40},{56,48},{64,56},{72,6... | collective-permute-start | bytes 245768 | tf_op jit(solution)/shard_map/ppermute | solution.py:22
  175.7 13.2 %collective-permute-start.23 = (f32[5,8,128]{2,1,0:T(8,128)S(1)}, f32[5,8,128]{2,1,0:T(8,128)S(1)}, u32[]{:S(2)}, u32[]{:S(2)}) collective-permute-start(f32[5,8,128]{2,1,0:T(8,128)S(1)} %bitcast.181), channel_id=1, source_target_pairs={{8,0},{16,8},{24,16},{32,24},{40,32},{48,40},{56,48},{64,56},{72,6... | collective-permute-start | bytes 61448 | tf_op jit(solution)/shard_map/ppermute | solution.py:32
where the time goes:
time: 205 us; the launch traced here: 204 us
  starting transfers between devices  152 us (74%)
  matrix products  19.3 us (9%)
  other arithmetic  15.6 us (8%)
  local copies, waits for them, and re-layouts  8.84 us (4%)
  waiting for transfers between devices  6.86 us (3%)
    ppermute x8, starting transfers between devices, from_behind(): return lax.ppermute(block, axis, route)  55.3 us
    ppermute x8, starting transfers between devices, padded(): lax.ppermute(head, axis, [((i + 1) % count, i) for i in range(ends)])  53.7 us
    ppermute x8, starting transfers between devices, padded(): lax.ppermute(tail, axis, [(i, (i + 1) % count) for i in range(ends)])  42.6 us
    dot_general x12, matrix products, mixing(): jnp.einsum('gf,ftar->gtar', matrix, values_in, precision=lax.Precision.HI...  14.3 us
    ppermute x8, waiting for transfers between devices, from_behind(): return lax.ppermute(block, axis, route)  6.82 us
  transfers between devices with their start and end apart: 24, of which 2 were waited for; matrix products, arithmetic and copies ran while one was open for 13% of the time, Pallas kernels for 0%

commit v1 on v0

v1 whole, which is shorter than its diff:
```python
import functools

import jax
import jax.numpy as jnp
from jax import lax
from jax.experimental import pallas as pl
from jax.experimental.pallas import tpu as pltpu
from jax.sharding import PartitionSpec as P

nonlinear_gain = 0.4
time_step = 0.25
forward_rates = (0.55, 0.15, 0.5, 0.2, 0.35, 0.35)
reverse_rates = (0.15, 0.55, 0.2, 0.5, 0.35, 0.35)
HALF, EVEN, BLOCK4, BLOCK3, GIVER = range(5)

VMEM = pl.BlockSpec(memory_space=pltpu.VMEM)
SMEM = pl.BlockSpec(memory_space=pltpu.SMEM)
f32 = jnp.float32


def shaping(v):
    return v + 0.5 * nonlinear_gain * v * v


def identity(v):
    return v


def call(kernel, ins, outs, scratch=(), flops=0, name=None):
    small = lambda x: x.dtype == jnp.int32 or x.ndim < 3
    moved = 4 * (sum(x.size for x in ins) + sum(x.size for x in outs))
    return pl.pallas_call(
        kernel,
        out_shape=outs,
        in_specs=[SMEM if small(x) else VMEM for x in ins],
        out_specs=[VMEM] * len(outs),
        scratch_shapes=list(scratch),
        compiler_params=pltpu.CompilerParams(vmem_limit_bytes=24 * 2**20),
        cost_estimate=pl.CostEstimate(flops=flops, bytes_accessed=moved, transcendentals=0),
        name=name,
    )(*ins)


def local_part(source, shaped, rates, mixers, transposed, finish):
    theta_low, theta_high, axial_low, axial_high, radial_low, radial_high = rates
    fields, columns, layers, radii = source.shape
    row = lax.broadcasted_iota(jnp.int32, (layers, radii), 0)
    lane = lax.broadcasted_iota(jnp.int32, (layers, radii), 1)

    def column(t, _):
        before = jnp.where(t > 0, theta_low, 0.0).astype(f32)
        after = jnp.where(t < columns - 1, theta_high, 0.0).astype(f32)
        totals = [None] * fields
        for f in range(fields):
            v = shaped(source[f, t])
            prior = shaped(source[f, jnp.maximum(t - 1, 0)])
            later = shaped(source[f, jnp.minimum(t + 1, columns - 1)])
            theta = before * prior + after * later - (theta_low + theta_high) * v
            lower = jnp.where(row == 0, 0.0, pltpu.roll(v, 1, 0))
            upper = jnp.where(row == layers - 1, 0.0, pltpu.roll(v, layers - 1, 0))
            axial = axial_low * lower + axial_high * upper - (axial_low + axial_high) * v
            inner = jnp.where(lane == 0, 0.0, pltpu.roll(v, 1, 1))
            outer = jnp.where(lane == radii - 1, 0.0, pltpu.roll(v, radii - 1, 1))
            radial = radial_low * inner + radial_high * outer - (radial_low + radial_high) * v
            for g in range(fields):
                at = (f, g) if transposed else (g, f)
                part = mixers[0][at] * theta + mixers[1][at] * axial + mixers[2][at] * radial
                totals[g] = part if totals[g] is None else totals[g] + part
        for g in range(fields):
            finish(g, t, totals[g])
        return 0

    lax.fori_loop(0, columns, column, 0)


def mixed(matrix, transposed, rate, values):
    fields = len(values)
    out = []
    for g in range(fields):
        total = None
        for f in range(fields):
            part = (rate * matrix[(f, g) if transposed else (g, f)]) * values[f]
            total = part if total is None else total + part
        out.append(total)
    return out


def pack_into(sources, shapes, place, xsend, own, send_a, send_b):
    columns, layers = sources[0].shape[1:3]
    half = place[HALF]
    even = place[EVEN]
    first = jnp.where(even == 1, columns - 1, 0)
    other = columns - 1 - first
    for n, (source, shaped) in enumerate(zip(sources, shapes)):
        for f in range(source.shape[0]):
            send_a[n, f] = shaped(source[f, first])
            send_b[n, f] = shaped(source[f, other])
            for t in range(columns):
                low = source[f, t, 0:1, :]
                high = source[f, t, layers - 1 : layers, :]
                xsend[n, f, t : t + 1, :] = shaped(jnp.where(half == 1, high, low))
                own[n, f, t : t + 1, :] = shaped(jnp.where(half == 1, low, high))


def pack_kernel(place, flow, cotangent, xsend, own, send_a, send_b):
    pack_into((flow, cotangent), (shaping, identity), place, xsend, own, send_a, send_b)


def applied(weights, face):
    total = weights[0] * face[0:1, :]
    for j in range(1, face.shape[0]):
        total = total + weights[j] * face[j : j + 1, :]
    return total


def payload_kernel(place, arrived, own, across, weights, send):
    half = place[HALF]
    scale = place[GIVER].astype(f32)
    for n in range(2):
        for f in range(own.shape[1]):
            face = applied(weights[0], arrived[n, f]) + scale * applied(weights[1], across[n, f])
            send[1 - half, n, f] = face
            send[half, n, f] = own[n, f]


def halo_parts(place, got_a, got_b, faces, across, weights, mixers, add_column, add_face):
    even = place[EVEN]
    fields, columns = faces.shape[2:4]
    first = jnp.where(even == 1, columns - 1, 0)
    other = columns - 1 - first
    scales = (place[BLOCK4].astype(f32), place[BLOCK3].astype(f32))
    for n, rates in enumerate((forward_rates, reverse_rates)):
        theta_low, theta_high, axial_low, axial_high = rates[:4]
        rate_a = jnp.where(even == 1, theta_high, theta_low).astype(f32)
        rate_b = jnp.where(even == 1, theta_low, theta_high).astype(f32)
        for at, rate, got in ((first, rate_a, got_a), (other, rate_b, got_b)):
            parts = mixed(mixers[0], n == 1, rate, [got[n, f] for f in range(fields)])
            for g in range(fields):
                add_column(n, g, at, parts[g])
        extra = [applied(weights[1], across[n, f]) for f in range(fields)]
        for side, rate in enumerate((axial_low, axial_high)):
            values = [faces[side, n, f] + scales[side] * extra[f] for f in range(fields)]
            parts = mixed(mixers[1], n == 1, rate, values)
            for g in range(fields):
                for t in range(columns):
                    add_face(n, g, t, side, parts[g][t : t + 1, :])


def first_local_kernel(mix_t, mix_a, mix_r, flow, cotangent, section, reverse):
    mixers = (mix_t, mix_a, mix_r)

    def section_at(g, t, total):
        section[g, t] = flow[g, t] + time_step * total

    def reverse_at(g, t, total):
        reverse[g, t] = total

    local_part(flow, shaping, forward_rates, mixers, False, section_at)
    local_part(cotangent, identity, reverse_rates, mixers, True, reverse_at)


def first_halo_kernel(
    place, mix_t, mix_a, mix_r, cotangent, section_local, reverse_local, got_a, got_b, faces, across, weights,
    section, adjoint, xsend, own, send_a, send_b, reverse,
):
    fields, columns, layers, _ = section.shape
    section[...] = section_local[...]
    reverse[...] = reverse_local[...]

    def add_column(n, g, t, part):
        if n == 0:
            section[g, t] += time_step * part
        else:
            reverse[g, t] += part

    def add_face(n, g, t, side, part):
        rows = slice(layers - 1, layers) if side else slice(0, 1)
        if n == 0:
            section[g, t, rows, :] += time_step * part
        else:
            reverse[g, t, rows, :] += part

    halo_parts(place, got_a, got_b, faces, across, weights, (mix_t, mix_a, mix_r), add_column, add_face)

    def column(t, _):
        for g in range(fields):
            adjoint[g, t] = 0.5 * cotangent[g, t] + 0.5 * time_step * (
                1.0 + nonlinear_gain * section[g, t]
            ) * reverse[g, t]
        return 0

    lax.fori_loop(0, columns, column, 0)
    pack_into((section, adjoint), (shaping, identity), place, xsend, own, send_a, send_b)


def second_local_kernel(mix_t, mix_a, mix_r, flow, cotangent, section, adjoint, advanced, sensitivity):
    mixers = (mix_t, mix_a, mix_r)

    def advanced_at(g, t, total):
        advanced[g, t] = 0.5 * flow[g, t] + 0.5 * (section[g, t] + time_step * total)

    def sensitivity_at(g, t, total):
        sensitivity[g, t] = (
            0.5 * cotangent[g, t]
            + adjoint[g, t]
            + time_step * (1.0 + nonlinear_gain * flow[g, t]) * total
        )

    local_part(section, shaping, forward_rates, mixers, False, advanced_at)
    local_part(adjoint, identity, reverse_rates, mixers, True, sensitivity_at)


def second_halo_kernel(
    place, mix_t, mix_a, mix_r, flow, advanced_local, sensitivity_local, got_a, got_b, faces, across, weights,
    advanced, sensitivity,
):
    layers = flow.shape[2]
    advanced[...] = advanced_local[...]
    sensitivity[...] = sensitivity_local[...]

    def add_column(n, g, t, part):
        if n == 0:
            advanced[g, t] += 0.5 * time_step * part
        else:
            sensitivity[g, t] += time_step * (1.0 + nonlinear_gain * flow[g, t]) * part

    def add_face(n, g, t, side, part):
        rows = slice(layers - 1, layers) if side else slice(0, 1)
        if n == 0:
            advanced[g, t, rows, :] += 0.5 * time_step * part
        else:
            scale = time_step * (1.0 + nonlinear_gain * flow[g, t, rows, :])
            sensitivity[g, t, rows, :] += scale * part

    halo_parts(place, got_a, got_b, faces, across, weights, (mix_t, mix_a, mix_r), add_column, add_face)


def sector_matrix(slot_list, code_list, sector_cells):
    columns = jnp.arange(2 * sector_cells, dtype=jnp.int32)
    matches = (slot_list[:, :, None] == columns[None, None, :]).astype(jnp.float32)
    weights = (code_list.astype(jnp.float32) + 1.0) / 12.0
    return jnp.sum(matches * weights[:, :, None], axis=1)


def interface_weights(intersection_slot, intersection_code, sector_cells, sector, n_sector, block, middle, lanes):
    own_start = sector * sector_cells
    next_start = (sector + 1) % n_sector * sector_cells

    def matrix(start):
        return sector_matrix(
            lax.dynamic_slice_in_dim(intersection_slot, start, sector_cells, 0),
            lax.dynamic_slice_in_dim(intersection_code, start, sector_cells, 0),
            sector_cells,
        )

    own, later = matrix(own_start), matrix(next_start)
    rising = (block == middle) | (block == middle + 1)
    here = jnp.where(block == middle + 1, own[:, sector_cells:].T, own[:, sector_cells:])
    here = jnp.where((block == middle + 1) | (block == middle - 2), here, jnp.eye(sector_cells, dtype=f32))
    there = jnp.where(rising, own[:, :sector_cells].T, later[:, :sector_cells])
    there = jnp.stack([here, there])
    return jnp.broadcast_to(there[..., None], (2, sector_cells, sector_cells, lanes))


def shards(
    flow_state, cotangent, mix_theta, mix_axial, mix_radial, intersection_slot, intersection_code
):
    fields, columns, layers, radii = flow_state.shape
    sector, block = lax.axis_index("azim"), lax.axis_index("block")
    n_sector, n_block = lax.axis_size("azim"), lax.axis_size("block")
    middle = n_block // 2

    pairs_a = [(i, i ^ 1) for i in range(n_sector)]
    pairs_b = [(i, (i + 1 if i % 2 else i - 1) % n_sector) for i in range(n_sector)]
    pairs_x = [(b, b - 2) for b in range(2, n_block, 2)] + [(b, b + 2) for b in range(1, n_block - 2, 2)]
    pairs_long = [(b, b ^ 1) for b in range(n_block)]
    at = lambda s, b: s * n_block + b
    pairs_face = []
    for s in range(n_sector):
        last, zero = s == n_sector - 1, s == 0
        pairs_face.append(
            (at(s, middle - 1), at(0, middle) if last else at(s + 1, middle + 1))
        )
        pairs_face.append(
            (at(s, middle), at(n_sector - 1, middle - 1) if zero else at(s - 1, middle - 2))
        )

    place = jnp.stack(
        [
            block % 2,
            1 - sector % 2,
            block == middle,
            block == middle - 1,
            (block == middle + 1) | (block == middle - 2),
        ]
    ).astype(jnp.int32)
    mixers = (mix_theta, mix_axial, mix_radial)

    shape = jax.ShapeDtypeStruct
    whole = shape(flow_state.shape, f32)
    face = shape((2, fields, columns, radii), f32)
    side = shape((2, fields, layers, radii), f32)
    faces = shape((2, 2, fields, columns, radii), f32)
    work = 4 * 5 * 5 * 3 * 2 * columns * layers * radii

    def exchange(xsend, own, send_a, send_b, weights):
        arrived = lax.ppermute(xsend, "block", pairs_x)
        across = lax.ppermute(xsend, ("azim", "block"), pairs_face)
        if callable(weights):
            weights = weights()
        (payload,) = call(payload_kernel, (place, arrived, own, across, weights), [faces], name="payload")
        both = lax.ppermute(payload, "block", pairs_long)
        got_a = lax.ppermute(send_a, "azim", pairs_a)
        got_b = lax.ppermute(send_b, "azim", pairs_b)
        return (got_a, got_b, both, across, weights)

    weights_of = functools.partial(
        interface_weights, intersection_slot, intersection_code, columns, sector, n_sector, block, middle, radii
    )
    packs = call(pack_kernel, (place, flow_state, cotangent), [face, face, side, side], name="pack")
    halos = exchange(*packs, weights_of)
    weights = halos[-1]
    section_local, reverse_local = call(
        first_local_kernel, (*mixers, flow_state, cotangent), [whole, whole], flops=work, name="first_local"
    )
    section, adjoint, *packs = call(
        first_halo_kernel,
        (place, *mixers, cotangent, section_local, reverse_local, *halos),
        [whole, whole, face, face, side, side],
        scratch=[pltpu.VMEM(whole.shape, f32)],
        name="first_halo",
    )
    halos = exchange(*packs, weights)
    advanced_local, sensitivity_local = call(
        second_local_kernel,
        (*mixers, flow_state, cotangent, section, adjoint),
        [whole, whole],
        flops=work,
        name="second_local",
    )
    return tuple(
        call(
            second_halo_kernel,
            (place, *mixers, flow_state, advanced_local, sensitivity_local, *halos),
            [whole, whole],
            name="second_halo",
        )
    )


def solution(mesh):
    placed = (
        P(None, "azim", "block", None),
        P(None, "azim", "block", None),
        P(),
        P(),
        P(),
        P(),
        P(),
    )
    return jax.shard_map(
        shards,
        mesh=mesh,
        in_specs=placed,
        out_specs=(P(None, "azim", "block", None), P(None, "azim", "block", None)),
        check_vma=False,
    )
```

time: 205 us -> 91.5 us (0.45)
  the two profiles are of different devices: /device:TPU:3 before, /device:TPU:4 now
where the time goes in v1:
time: 91.5 us; the launch traced here: 91 us
  starting transfers between devices  45.9 us (50%)
  waiting for transfers between devices  28.1 us (31%)
  Pallas kernels  12.5 us (14%)
  local copies, waits for them, and re-layouts  3.39 us (4%)
    ppermute x2, waiting for transfers between devices, exchange(): both = lax.ppermute(payload, 'block', pairs_long)  15.9 us
    ppermute x2, starting transfers between devices, exchange(): across = lax.ppermute(xsend, ('azim', 'block'), pairs_face)  15.7 us
    ppermute x2, starting transfers between devices, exchange(): got_b = lax.ppermute(send_b, 'azim', pairs_b)  12.6 us
    pallas_call x7, Pallas kernels, call(): pl.pallas_call(kernel, out_shape=outs, in_specs=[SMEM if small(x) else VM...  12.5 us
    ppermute x2, waiting for transfers between devices, exchange(): across = lax.ppermute(xsend, ('azim', 'block'), pairs_face)  12.1 us
    ppermute x2, starting transfers between devices, exchange(): both = lax.ppermute(payload, 'block', pairs_long)  9.93 us
    ppermute x2, starting transfers between devices, exchange(): arrived = lax.ppermute(xsend, 'block', pairs_x)  3.84 us
    ppermute x2, starting transfers between devices, exchange(): got_a = lax.ppermute(send_a, 'azim', pairs_a)  3.84 us
  transfers between devices with their start and end apart: 10, of which 3 were waited for; matrix products, arithmetic and copies ran while one was open for 1% of the time, Pallas kernels for 9%

profile of v1, /device:TPU:4, one launch (start us, length us, event | category | flops | bytes accessed | tf_op | source)
XLA Modules:
  0.0 91.0 jit_solution(16549162954756357274)
XLA Ops:
  0.7 0.1 stack.44.place
  0.7 0.0 copy-start
  0.7 1.1 %copy-done = f32[5,8,32,128]{3,2,1,0:T(8,128)S(1)} copy-done((f32[5,8,32,128]{3,2,1,0:T(8,128)S(1)}, f32[5,8,32,128]{3,2,1,0:T(8,128)}, u32[]{:S(2)}) %copy-start) | copy-done | bytes 655384
  1.8 0.0 copy-start.2
  1.8 1.1 %copy-done.2 = f32[5,8,32,128]{3,2,1,0:T(8,128)S(1)} copy-done((f32[5,8,32,128]{3,2,1,0:T(8,128)S(1)}, f32[5,8,32,128]{3,2,1,0:T(8,128)}, u32[]{:S(2)}) %copy-start.2) | copy-done | bytes 655384
  2.9 0.0 copy-start.1
  2.9 0.0 copy-start.3
  2.9 0.6 pack.1
  3.6 13.3 %collective-permute-start.3 = (f32[2,5,8,128]{3,2,1,0:T(8,128)S(1)}, f32[2,5,8,128]{3,2,1,0:T(8,128)S(1)}, u32[]{:S(2)}, u32[]{:S(2)}) collective-permute-start(f32[2,5,8,128]{3,2,1,0:T(8,128)S(1)} %get-tuple-element.20), channel_id=1, source_target_pairs={{3,13},{4,507},{11,21},{12,2},{19,29},{20,10},{27,37},{28,18},{35,... | collective-permute-start | bytes 122888 | tf_op jit(solution)/shard_map/ppermute | solution.py:308
  16.8 1.9 %collective-permute-start.2 = (f32[2,5,8,128]{3,2,1,0:T(8,128)S(1)}, f32[2,5,8,128]{3,2,1,0:T(8,128)S(1)}, u32[]{:S(2)}, u32[]{:S(2)}) collective-permute-start(f32[2,5,8,128]{3,2,1,0:T(8,128)S(1)} %get-tuple-element.20), channel_id=1, source_target_pairs={{2,0},{4,2},{6,4},{1,3},{3,5},{5,7},{10,8},{12,10},{14,12},{9,11},... | collective-permute-start | bytes 122888 | tf_op jit(solution)/shard_map/ppermute | solution.py:307
  18.8 1.9 %collective-permute-start = (f32[2,5,32,128]{3,2,1,0:T(8,128)S(1)}, f32[2,5,32,128]{3,2,1,0:T(8,128)S(1)}, u32[]{:S(2)}, u32[]{:S(2)}) collective-permute-start(f32[2,5,32,128]{3,2,1,0:T(8,128)S(1)} %get-tuple-element.18), channel_id=1, source_target_pairs={{0,8},{8,0},{16,24},{24,16},{32,40},{40,32},{48,56},{56,48},{64,72... | collective-permute-start | bytes 491528 | tf_op jit(solution)/shard_map/ppermute | solution.py:313
  20.7 4.5 %collective-permute-start.1 = (f32[2,5,32,128]{3,2,1,0:T(8,128)S(1)}, f32[2,5,32,128]{3,2,1,0:T(8,128)S(1)}, u32[]{:S(2)}, u32[]{:S(2)}) collective-permute-start(f32[2,5,32,128]{3,2,1,0:T(8,128)S(1)} %get-tuple-element.19), channel_id=1, source_target_pairs={{0,504},{8,16},{16,8},{24,32},{32,24},{40,48},{48,40},{56,64},{64,... | collective-permute-start | bytes 491528 | tf_op jit(solution)/shard_map/ppermute | solution.py:314
  25.2 0.0 copy-start.7
  25.2 0.0 copy-start.8
  25.3 0.7 copy-done.7
  25.9 0.1 constant_dynamic-slice_fusion.1
  26.0 0.0 copy-done.8
  26.0 0.1 add_multiply_fusion.1
  26.1 0.1 select_reduce_fusion
  26.2 0.1 copy.18
  26.2 0.1 slice.10
  26.3 0.1 copy.17
  26.4 0.1 copy.15
  26.5 0.1 fusion.1
  26.5 0.0 collective-permute-done.3.across
  26.5 0.0 collective-permute-done.2.arrived
  26.6 0.1 broadcast_in_dim.2.weights
  26.6 0.0 copy-start.4
  26.6 0.0 copy-start.5
  26.6 0.0 copy-start.6
  26.7 0.6 payload.2
  27.3 8.0 %collective-permute-start.4 = (f32[2,2,5,8,128]{4,3,2,1,0:T(8,128)S(1)}, f32[2,2,5,8,128]{4,3,2,1,0:T(8,128)S(1)}, u32[]{:S(2)}, u32[]{:S(2)}) collective-permute-start(f32[2,2,5,8,128]{4,3,2,1,0:T(8,128)S(1)} %payload.2), channel_id=1, source_target_pairs={{0,1},{1,0},{2,3},{3,2},{4,5},{5,4},{6,7},{7,6},{8,9},{9,8},{10,11... | collective-permute-start | bytes 245768 | tf_op jit(solution)/shard_map/ppermute | solution.py:312
  35.3 0.0 copy-done.1
  35.3 0.0 copy-done.3
  35.3 0.0 copy-done.4
  35.3 0.0 copy-done.5
  35.3 0.0 copy-done.6
  35.3 3.5 %first_local.1 = (f32[5,8,32,128]{3,2,1,0:T(8,128)S(1)}, f32[5,8,32,128]{3,2,1,0:T(8,128)S(1)}) custom-call(f32[5,5]{1,0:T(8,128)S(1)} %copy-done.4, f32[5,5]{1,0:T(8,128)S(1)} %copy-done.5, f32[5,5]{1,0:T(8,128)S(1)} %copy-done.6, f32[5,8,32,128]{3,2,1,0:T(8,128)S(1)} %copy-done.3, f32[5,8,32,128]{3,2,1,0:T(8,128)S(1)} %copy-done.1), custom_call_target="tpu_custom_call" | custom-call | flops 19660800 | bytes 2621740 | tf_op jit(solution)/shard_map/first_local/pallas_call | solution.py:32
  38.8 6.5 %collective-permute-done.4.faces = f32[2,2,5,8,128]{4,3,2,1,0:T(8,128)S(1)} collective-permute-done((f32[2,2,5,8,128]{4,3,2,1,0:T(8,128)S(1)}, f32[2,2,5,8,128]{4,3,2,1,0:T(8,128)S(1)}, u32[]{:S(2)}, u32[]{:S(2)}) %collective-permute-start.4) | collective-permute-done | bytes 81952 | tf_op jit(solution)/shard_map/ppermute | solution.py:312
  45.3 0.0 collective-permute-done.got_a
  45.3 0.0 collective-permute-done.1.got_b
  45.3 1.4 %first_halo.1 = (f32[5,8,32,128]{3,2,1,0:T(8,128)S(1)}, f32[5,8,32,128]{3,2,1,0:T(8,128)S(1)}, f32[2,5,8,128]{3,2,1,0:T(8,128)S(1)}, f32[2,5,8,128]{3,2,1,0:T(8,...) custom-call(s32[5]{0:T(128)S(1)} %stack.44.place, f32[5,5]{1,0:T(8,128)S(1)} %copy-done.4, ...), custom_call_target="tpu_custom_call" | custom-call | bytes 4202816 | tf_op jit(solution)/shard_map/first_halo/pallas_call | solution.py:32
  46.7 1.9 %collective-permute-start.5 = (f32[2,5,32,128]{3,2,1,0:T(8,128)S(1)}, f32[2,5,32,128]{3,2,1,0:T(8,128)S(1)}, u32[]{:S(2)}, u32[]{:S(2)}) collective-permute-start(f32[2,5,32,128]{3,2,1,0:T(8,128)S(1)} %get-tuple-element.26), channel_id=1, source_target_pairs={{0,8},{8,0},{16,24},{24,16},{32,40},{40,32},{48,56},{56,48},{64,72... | collective-permute-start | bytes 491528 | tf_op jit(solution)/shard_map/ppermute | solution.py:313
  48.7 8.1 %collective-permute-start.6 = (f32[2,5,32,128]{3,2,1,0:T(8,128)S(1)}, f32[2,5,32,128]{3,2,1,0:T(8,128)S(1)}, u32[]{:S(2)}, u32[]{:S(2)}) collective-permute-start(f32[2,5,32,128]{3,2,1,0:T(8,128)S(1)} %get-tuple-element.27), channel_id=1, source_target_pairs={{0,504},{8,16},{16,8},{24,32},{32,24},{40,48},{48,40},{56,64},{64,... | collective-permute-start | bytes 491528 | tf_op jit(solution)/shard_map/ppermute | solution.py:314
  56.7 2.4 %collective-permute-start.8 = (f32[2,5,8,128]{3,2,1,0:T(8,128)S(1)}, f32[2,5,8,128]{3,2,1,0:T(8,128)S(1)}, u32[]{:S(2)}, u32[]{:S(2)}) collective-permute-start(f32[2,5,8,128]{3,2,1,0:T(8,128)S(1)} %get-tuple-element.28), channel_id=1, source_target_pairs={{3,13},{4,507},{11,21},{12,2},{19,29},{20,10},{27,37},{28,18},{35,... | collective-permute-start | bytes 122888 | tf_op jit(solution)/shard_map/ppermute | solution.py:308
  59.2 1.9 %collective-permute-start.7 = (f32[2,5,8,128]{3,2,1,0:T(8,128)S(1)}, f32[2,5,8,128]{3,2,1,0:T(8,128)S(1)}, u32[]{:S(2)}, u32[]{:S(2)}) collective-permute-start(f32[2,5,8,128]{3,2,1,0:T(8,128)S(1)} %get-tuple-element.28), channel_id=1, source_target_pairs={{2,0},{4,2},{6,4},{1,3},{3,5},{5,7},{10,8},{12,10},{14,12},{9,11},... | collective-permute-start | bytes 122888 | tf_op jit(solution)/shard_map/ppermute | solution.py:307
  61.1 12.1 %collective-permute-done.8.across = f32[2,5,8,128]{3,2,1,0:T(8,128)S(1)} collective-permute-done((f32[2,5,8,128]{3,2,1,0:T(8,128)S(1)}, f32[2,5,8,128]{3,2,1,0:T(8,128)S(1)}, u32[]{:S(2)}, u32[]{:S(2)}) %collective-permute-start.8) | collective-permute-done | bytes 40992 | tf_op jit(solution)/shard_map/ppermute | solution.py:308
  73.2 0.0 collective-permute-done.7.arrived
  73.2 0.6 payload.3
  73.8 1.9 %collective-permute-start.9 = (f32[2,2,5,8,128]{4,3,2,1,0:T(8,128)S(1)}, f32[2,2,5,8,128]{4,3,2,1,0:T(8,128)S(1)}, u32[]{:S(2)}, u32[]{:S(2)}) collective-permute-start(f32[2,2,5,8,128]{4,3,2,1,0:T(8,128)S(1)} %payload.3), channel_id=1, source_target_pairs={{0,1},{1,0},{2,3},{3,2},{4,5},{5,4},{6,7},{7,6},{8,9},{9,8},{10,11... | collective-permute-start | bytes 245768 | tf_op jit(solution)/shard_map/ppermute | solution.py:312
  75.7 3.7 %second_local.1 = (f32[5,8,32,128]{3,2,1,0:T(8,128)S(1)}, f32[5,8,32,128]{3,2,1,0:T(8,128)S(1)}) custom-call(f32[5,5]{1,0:T(8,128)S(1)} %copy-done.4, f32[5,5]{1,0:T(8,128)S(1)} %copy-done.5, f32[5,5]{1,0:T(8,128)S(1)} %copy-done.6, f32[5,8,32,128]{3,2,1,0:T(8,128)S(1)} %copy-done.3, f32[5,8,32,128]{3,2,1,0:T(8,128)S(1)} %copy-done.1, ...), custom_call_target="tpu_custom_call" | custom-call | flops 19660800 | bytes 3932460 | tf_op jit(solution)/shard_map/second_local/pallas_call | solution.py:32
  79.4 9.4 %collective-permute-done.9.faces = f32[2,2,5,8,128]{4,3,2,1,0:T(8,128)S(1)} collective-permute-done((f32[2,2,5,8,128]{4,3,2,1,0:T(8,128)S(1)}, f32[2,2,5,8,128]{4,3,2,1,0:T(8,128)S(1)}, u32[]{:S(2)}, u32[]{:S(2)}) %collective-permute-start.9) | collective-permute-done | bytes 81952 | tf_op jit(solution)/shard_map/ppermute | solution.py:312
  88.9 0.0 collective-permute-done.5.got_a
  88.9 0.0 collective-permute-done.6.got_b
  88.9 2.1 %second_halo.1 = (f32[5,8,32,128]{3,2,1,0:T(8,128)}, f32[5,8,32,128]{3,2,1,0:T(8,128)}) custom-call(s32[5]{0:T(128)S(1)} %stack.44.place, f32[5,5]{1,0:T(8,128)S(1)} %copy-done.4, f32[5,5]{1,0:T(8,128)S(1)} %copy-done.5, f32[5,5]{1,0:T(8,128)S(1)} %copy-done.6, f32[5,8,32,128]{3,2,1,0:T(8,128)S(1)} %copy-done.3, ...), custom_call_target="tpu_custom_call" | custom-call | bytes 3793216 | tf_op jit(solution)/shard_map/second_halo/pallas_call | solution.py:32
  (2 shorter events, 0.0 us)
Async XLA Ops:
  0.7 1.1 %copy-start = (f32[5,8,32,128]{3,2,1,0:T(8,128)S(1)}, f32[5,8,32,128]{3,2,1,0:T(8,128)}, u32[]{:S(2)}) copy-start(f32[5,8,32,128]{3,2,1,0:T(8,128)} %cotangent.7) | copy-start | bytes 1966084
  1.8 1.1 %copy-start.2 = (f32[5,8,32,128]{3,2,1,0:T(8,128)S(1)}, f32[5,8,32,128]{3,2,1,0:T(8,128)}, u32[]{:S(2)}) copy-start(f32[5,8,32,128]{3,2,1,0:T(8,128)} %flow.7) | copy-start | bytes 1966084
  2.9 32.4 %copy-start.1 = (f32[5,8,32,128]{3,2,1,0:T(8,128)S(1)}, f32[5,8,32,128]{3,2,1,0:T(8,128)}, u32[]{:S(2)}) copy-start(f32[5,8,32,128]{3,2,1,0:T(8,128)} %cotangent.7) | copy-start | bytes 1966084
  2.9 32.4 %copy-start.3 = (f32[5,8,32,128]{3,2,1,0:T(8,128)S(1)}, f32[5,8,32,128]{3,2,1,0:T(8,128)}, u32[]{:S(2)}) copy-start(f32[5,8,32,128]{3,2,1,0:T(8,128)} %flow.7) | copy-start | bytes 1966084
  3.6 23.0 %collective-permute-start.3 = (f32[2,5,8,128]{3,2,1,0:T(8,128)S(1)}, f32[2,5,8,128]{3,2,1,0:T(8,128)S(1)}, u32[]{:S(2)}, u32[]{:S(2)}) collective-permute-start(f32[2,5,8,128]{3,2,1,0:T(8,128)S(1)} %get-tuple-element.20), channel_id=1, source_target_pairs={{3,13},{4,507},{11,21},{12,2},{19,29},{20,10},{27,37},{28,18},{35,... | collective-permute-start | bytes 122888 | tf_op jit(solution)/shard_map/ppermute | solution.py:308
  16.8 9.7 %collective-permute-start.2 = (f32[2,5,8,128]{3,2,1,0:T(8,128)S(1)}, f32[2,5,8,128]{3,2,1,0:T(8,128)S(1)}, u32[]{:S(2)}, u32[]{:S(2)}) collective-permute-start(f32[2,5,8,128]{3,2,1,0:T(8,128)S(1)} %get-tuple-element.20), channel_id=1, source_target_pairs={{2,0},{4,2},{6,4},{1,3},{3,5},{5,7},{10,8},{12,10},{14,12},{9,11},... | collective-permute-start | bytes 122888 | tf_op jit(solution)/shard_map/ppermute | solution.py:307
  18.8 26.5 %collective-permute-start = (f32[2,5,32,128]{3,2,1,0:T(8,128)S(1)}, f32[2,5,32,128]{3,2,1,0:T(8,128)S(1)}, u32[]{:S(2)}, u32[]{:S(2)}) collective-permute-start(f32[2,5,32,128]{3,2,1,0:T(8,128)S(1)} %get-tuple-element.18), channel_id=1, source_target_pairs={{0,8},{8,0},{16,24},{24,16},{32,40},{40,32},{48,56},{56,48},{64,72... | collective-permute-start | bytes 491528 | tf_op jit(solution)/shard_map/ppermute | solution.py:313
  20.7 24.6 %collective-permute-start.1 = (f32[2,5,32,128]{3,2,1,0:T(8,128)S(1)}, f32[2,5,32,128]{3,2,1,0:T(8,128)S(1)}, u32[]{:S(2)}, u32[]{:S(2)}) collective-permute-start(f32[2,5,32,128]{3,2,1,0:T(8,128)S(1)} %get-tuple-element.19), channel_id=1, source_target_pairs={{0,504},{8,16},{16,8},{24,32},{32,24},{40,48},{48,40},{56,64},{64,... | collective-permute-start | bytes 491528 | tf_op jit(solution)/shard_map/ppermute | solution.py:314
  25.2 0.7 copy-start.7
  25.2 0.8 copy-start.8
  26.6 8.7 %copy-start.4 = (f32[5,5]{1,0:T(8,128)S(1)}, f32[5,5]{1,0:T(8,128)}, u32[]{:S(2)}) copy-start(f32[5,5]{1,0:T(8,128)} %mix_t.7) | copy-start | bytes 304
  26.6 8.7 %copy-start.5 = (f32[5,5]{1,0:T(8,128)S(1)}, f32[5,5]{1,0:T(8,128)}, u32[]{:S(2)}) copy-start(f32[5,5]{1,0:T(8,128)} %mix_a.7) | copy-start | bytes 304
  26.6 8.7 %copy-start.6 = (f32[5,5]{1,0:T(8,128)S(1)}, f32[5,5]{1,0:T(8,128)}, u32[]{:S(2)}) copy-start(f32[5,5]{1,0:T(8,128)} %mix_r.7) | copy-start | bytes 304
  27.3 18.1 %collective-permute-start.4 = (f32[2,2,5,8,128]{4,3,2,1,0:T(8,128)S(1)}, f32[2,2,5,8,128]{4,3,2,1,0:T(8,128)S(1)}, u32[]{:S(2)}, u32[]{:S(2)}) collective-permute-start(f32[2,2,5,8,128]{4,3,2,1,0:T(8,128)S(1)} %payload.2), channel_id=1, source_target_pairs={{0,1},{1,0},{2,3},{3,2},{4,5},{5,4},{6,7},{7,6},{8,9},{9,8},{10,11... | collective-permute-start | bytes 245768 | tf_op jit(solution)/shard_map/ppermute | solution.py:312
  46.7 42.1 %collective-permute-start.5 = (f32[2,5,32,128]{3,2,1,0:T(8,128)S(1)}, f32[2,5,32,128]{3,2,1,0:T(8,128)S(1)}, u32[]{:S(2)}, u32[]{:S(2)}) collective-permute-start(f32[2,5,32,128]{3,2,1,0:T(8,128)S(1)} %get-tuple-element.26), channel_id=1, source_target_pairs={{0,8},{8,0},{16,24},{24,16},{32,40},{40,32},{48,56},{56,48},{64,72... | collective-permute-start | bytes 491528 | tf_op jit(solution)/shard_map/ppermute | solution.py:313
  48.7 40.2 %collective-permute-start.6 = (f32[2,5,32,128]{3,2,1,0:T(8,128)S(1)}, f32[2,5,32,128]{3,2,1,0:T(8,128)S(1)}, u32[]{:S(2)}, u32[]{:S(2)}) collective-permute-start(f32[2,5,32,128]{3,2,1,0:T(8,128)S(1)} %get-tuple-element.27), channel_id=1, source_target_pairs={{0,504},{8,16},{16,8},{24,32},{32,24},{40,48},{48,40},{56,64},{64,... | collective-permute-start | bytes 491528 | tf_op jit(solution)/shard_map/ppermute | solution.py:314
  56.7 16.5 %collective-permute-start.8 = (f32[2,5,8,128]{3,2,1,0:T(8,128)S(1)}, f32[2,5,8,128]{3,2,1,0:T(8,128)S(1)}, u32[]{:S(2)}, u32[]{:S(2)}) collective-permute-start(f32[2,5,8,128]{3,2,1,0:T(8,128)S(1)} %get-tuple-element.28), channel_id=1, source_target_pairs={{3,13},{4,507},{11,21},{12,2},{19,29},{20,10},{27,37},{28,18},{35,... | collective-permute-start | bytes 122888 | tf_op jit(solution)/shard_map/ppermute | solution.py:308
  59.2 14.1 %collective-permute-start.7 = (f32[2,5,8,128]{3,2,1,0:T(8,128)S(1)}, f32[2,5,8,128]{3,2,1,0:T(8,128)S(1)}, u32[]{:S(2)}, u32[]{:S(2)}) collective-permute-start(f32[2,5,8,128]{3,2,1,0:T(8,128)S(1)} %get-tuple-element.28), channel_id=1, source_target_pairs={{2,0},{4,2},{6,4},{1,3},{3,5},{5,7},{10,8},{12,10},{14,12},{9,11},... | collective-permute-start | bytes 122888 | tf_op jit(solution)/shard_map/ppermute | solution.py:307
  73.8 15.0 %collective-permute-start.9 = (f32[2,2,5,8,128]{4,3,2,1,0:T(8,128)S(1)}, f32[2,2,5,8,128]{4,3,2,1,0:T(8,128)S(1)}, u32[]{:S(2)}, u32[]{:S(2)}) collective-permute-start(f32[2,2,5,8,128]{4,3,2,1,0:T(8,128)S(1)} %payload.3), channel_id=1, source_target_pairs={{0,1},{1,0},{2,3},{3,2},{4,5},{5,4},{6,7},{7,6},{8,9},{9,8},{10,11... | collective-permute-start | bytes 245768 | tf_op jit(solution)/shard_map/ppermute | solution.py:312

commit v2 on v0

v2 whole, which is shorter than its diff:
```python
import jax
import jax.numpy as jnp
from jax import lax
from jax.experimental import pallas as pl
from jax.experimental.pallas import tpu as pltpu
from jax.sharding import PartitionSpec as P

nonlinear_gain = 0.4
time_step = 0.25
forward_rates = (0.55, 0.15, 0.5, 0.2, 0.35, 0.35)
reverse_rates = (0.15, 0.55, 0.2, 0.5, 0.35, 0.35)
HALF, EVEN, PICK, PARTNER_PICK, WRAP, ACROSS = range(6)

VMEM = pl.BlockSpec(memory_space=pltpu.VMEM)
SMEM = pl.BlockSpec(memory_space=pltpu.SMEM)
f32 = jnp.float32
exact = lax.Precision.HIGHEST


def shaping(v):
    return v + 0.5 * nonlinear_gain * v * v


def identity(v):
    return v


def call(kernel, ins, outs, scratch=(), flops=0, name=None):
    small = lambda x: x.dtype == jnp.int32 or x.ndim < 3
    moved = 4 * (sum(x.size for x in ins) + sum(x.size for x in outs))
    return pl.pallas_call(
        kernel,
        out_shape=outs,
        in_specs=[SMEM if small(x) else VMEM for x in ins],
        out_specs=[VMEM] * len(outs),
        scratch_shapes=[pltpu.VMEM(s, f32) for s in scratch],
        compiler_params=pltpu.CompilerParams(vmem_limit_bytes=32 * 2**20),
        cost_estimate=pl.CostEstimate(flops=flops, bytes_accessed=moved, transcendentals=0),
        name=name,
    )(*ins)


def radial_term(v, rates):
    inner_rate, outer_rate = rates[4:]
    radii = v.shape[1]
    lane = lax.broadcasted_iota(jnp.int32, v.shape, 1)
    inner = jnp.where(lane == 0, 0.0, pltpu.roll(v, 1, 1))
    outer = jnp.where(lane == radii - 1, 0.0, pltpu.roll(v, radii - 1, 1))
    return inner_rate * inner + outer_rate * outer - (inner_rate + outer_rate) * v


def mix_into(totals, mixers, transposed, f, terms):
    for g in range(len(totals)):
        at = (f, g) if transposed else (g, f)
        part = None
        for matrix, term in zip(mixers, terms):
            scaled = matrix[at] * term
            part = scaled if part is None else part + scaled
        totals[g] = part if totals[g] is None else totals[g] + part


def operator(source, shaped, rates, mixers, transposed, ends, finish):
    theta_low, theta_high, axial_low, axial_high = rates[:4]
    fields, columns, layers, radii = source.shape

    def column(t, _):
        row = lax.broadcasted_iota(jnp.int32, (layers, radii), 0)
        totals = [None] * fields
        for f in range(fields):
            v = shaped(source[f, t + 1])
            theta = (
                theta_low * shaped(source[f, t])
                + theta_high * shaped(source[f, t + 2])
                - (theta_low + theta_high) * v
            )
            low_end, high_end = ends(f, t)
            lower = jnp.where(row == 0, low_end, pltpu.roll(v, 1, 0))
            upper = jnp.where(row == layers - 1, high_end, pltpu.roll(v, layers - 1, 0))
            axial = axial_low * lower + axial_high * upper - (axial_low + axial_high) * v
            mix_into(totals, mixers, transposed, f, (theta, axial, radial_term(v, rates)))
        for g in range(fields):
            finish(g, t, totals[g])
        return 0

    lax.fori_loop(0, columns - 2, column, 0)


def pack_kernel(place, flow, cotangent, xsend, own, send_a, send_b):
    fields, columns, layers, _ = flow.shape
    half, even, pick = place[HALF], place[EVEN], place[PICK]
    for n, source in enumerate((flow, cotangent)):
        for f in range(fields):
            for t in range(columns):
                rows = slice(t, t + 1)
                for depth in range(2):
                    low = source[f, t, depth : depth + 1, :]
                    high = source[f, t, layers - 1 - depth : layers - depth, :]
                    xsend[depth, n, f, rows, :] = jnp.where(half == 1, high, low)
                    own[depth, n, f, rows, :] = jnp.where(half == 1, low, high)
                    if depth == 0:
                        near = jnp.where(pick == 1, high, low)
                        rows_near = slice(2 * layers + t, 2 * layers + t + 1)
                        send_a[n, f, rows_near, :] = near
                        send_b[n, f, rows_near, :] = near
            for depth in range(2):
                first = jnp.where(even == 1, columns - 1 - depth, depth)
                rows = slice(depth * layers, (depth + 1) * layers)
                send_a[n, f, rows, :] = source[f, first]
                send_b[n, f, rows, :] = source[f, columns - 1 - first]


def payload_kernel(place, arrived, own, send):
    half = place[HALF]
    send[half] = own[...]
    send[1 - half] = arrived[...]


def pass_kernel(place, faces, sent, pass_a, pass_b, pass_far):
    pick, partner_pick = place[PICK], place[PARTNER_PICK]
    wrap, across = place[WRAP], place[ACROSS]

    def choice(flag, depth, other):
        here = 1 - pick if other else pick
        there = 1 - partner_pick if other else partner_pick
        return jnp.where(flag == 1, sent[there, depth], faces[here, depth])

    for n, (depth, other) in enumerate(((0, False), (1, False), (0, True))):
        pass_a[n] = faces[1 - pick if other else pick, depth]
        pass_b[n] = choice(wrap, depth, other)
    pass_far[...] = choice(across, 0, False)


def first_kernel(
    place, mix_t, mix_a, mix_r, flow, cotangent, got_a, got_b,
    section, reverse, reach, flow_wide, reach_wide,
):
    fields, columns, layers, _ = flow.shape
    even = place[EVEN]
    mixers = (mix_t, mix_a, mix_r)
    for n, (source, wide) in enumerate(((flow, flow_wide), (cotangent, reach_wide))):
        wide[:, 2 : 2 + columns] = source[...]
        for f in range(fields):
            for depth in range(2):
                rows = slice(depth * layers, (depth + 1) * layers)
                from_a, from_b = got_a[n, f, rows, :], got_b[n, f, rows, :]
                wide[f, 1 - depth] = jnp.where(even == 1, from_b, from_a)
                wide[f, 2 + columns + depth] = jnp.where(even == 1, from_a, from_b)
    reach[...] = reach_wide[:, 1 : 3 + columns]

    def section_at(g, t, total):
        section[g, t] = flow_wide[g, t + 1] + time_step * total

    def reverse_at(g, t, total):
        reverse[g, t] = total

    ends = lambda f, t: (0.0, 0.0)
    operator(flow_wide, shaping, forward_rates, mixers, False, ends, section_at)
    operator(reach_wide, identity, reverse_rates, mixers, True, ends, reverse_at)


def second_kernel(
    place, mix_t, mix_a, mix_r, flow, cotangent, section_local, reverse_local, reach, got_a, got_b,
    faces, pass_a, pass_b, pass_far, weights,
    advanced, sensitivity,
    section, adjoint, reverse, far_one, far_two, near, virtual, beyond, ends_two,
):
    fields, columns, layers, radii = flow.shape
    even, pick = place[EVEN], place[PICK]
    mixers = (mix_t, mix_a, mix_r)
    all_rates = (forward_rates, reverse_rates)
    all_shapes = (shaping, identity)
    lanes = [
        [slice((n * fields + f) * radii, (n * fields + f + 1) * radii) for f in range(fields)] for n in range(2)
    ]

    def sector_rows(place_in):
        return slice(place_in * columns, (place_in + 1) * columns)

    for side in range(2):
        at_own, at_prior, at_later, at_far = ((2, 1, 3, 0), (1, 0, 2, 3))[side]
        picked = jnp.where(pick == side, 0, 2)
        for n, shaped in enumerate(all_shapes):
            for f in range(fields):
                lane = lanes[n][f]
                from_a, from_b = pass_a[picked, n, f], pass_b[picked, n, f]
                far_one[side, sector_rows(at_own), lane] = shaped(faces[side, 0, n, f])
                far_one[side, sector_rows(at_prior), lane] = shaped(jnp.where(even == 1, from_b, from_a))
                far_one[side, sector_rows(at_later), lane] = shaped(jnp.where(even == 1, from_a, from_b))
                far_one[side, sector_rows(at_far), lane] = shaped(pass_far[n, f])
                from_a, from_b = pass_a[1, n, f], pass_b[1, n, f]
                beside = jnp.where(even == 1, from_b, from_a) if side == 0 else jnp.where(even == 1, from_a, from_b)
                far_two[side, sector_rows(at_own - 1), lane] = shaped(faces[side, 1, n, f])
                far_two[side, sector_rows(2 - at_own), lane] = shaped(beside)
                rows = slice(2 * layers, 2 * layers + columns)
                from_a, from_b = got_a[n, f, rows, :], got_b[n, f, rows, :]
                near[side, sector_rows(0), lane] = shaped(jnp.where(even == 1, from_b, from_a))
                near[side, sector_rows(2), lane] = shaped(jnp.where(even == 1, from_a, from_b))
                source = (flow, cotangent)[n]
                at = layers - 1 if side else 0
                for t in range(columns):
                    rows = slice(columns + t, columns + t + 1)
                    near[side, rows, lane] = shaped(source[f, t, at : at + 1, :])

    two = 2 * columns
    for side in range(2):
        virtual[side] = jnp.dot(weights[side, 0:16, :], far_one[side], precision=exact)
        back = jnp.dot(weights[side, 16:32, 0 : 3 * columns], near[side], precision=exact)
        values = []
        for n, rates in enumerate(all_rates):
            theta_low, theta_high, axial_low, axial_high = rates[:4]
            totals = [None] * fields
            for f in range(fields):
                lane = lanes[n][f]
                v = far_one[side, columns : columns + two, lane]
                theta = (
                    theta_low * far_one[side, columns - 1 : columns - 1 + two, lane]
                    + theta_high * far_one[side, columns + 1 : columns + 1 + two, lane]
                    - (theta_low + theta_high) * v
                )
                lower, upper = far_two[side, :, lane], back[:, lane]
                if side:
                    lower, upper = upper, lower
                axial = axial_low * lower + axial_high * upper - (axial_low + axial_high) * v
                mix_into(totals, mixers, n == 1, f, (theta, axial, radial_term(v, rates)))
            values.append(totals)
        for g in range(fields):
            parts = [faces[side, 0, 0, g], None]
            from_a, from_b = pass_a[jnp.where(pick == side, 0, 2), 0, g], pass_b[jnp.where(pick == side, 0, 2), 0, g]
            if side:
                parts = [parts[0], jnp.where(even == 1, from_a, from_b)]
            else:
                parts = [jnp.where(even == 1, from_b, from_a), parts[0]]
            one = jnp.concatenate(parts, axis=0) + time_step * values[0][g]
            reach_far = far_one[side, columns : columns + two, lanes[1][g]]
            beyond[side, :, lanes[0][g]] = shaping(one)
            beyond[side, :, lanes[1][g]] = 0.5 * reach_far + 0.5 * time_step * (
                1.0 + nonlinear_gain * one
            ) * values[1][g]
        rows_two = jnp.dot(weights[side, 32:40, 0:two], beyond[side], precision=exact)
        for n in range(2):
            for f in range(fields):
                k = (side * 2 + n) * fields + f
                for t in range(columns):
                    ends_two[t, k : k + 1, :] = rows_two[t : t + 1, lanes[n][f]]

    section[...] = section_local[...]
    reverse[...] = reverse_local[...]
    for n, (rates, target, scale) in enumerate(zip(all_rates, (section, reverse), (time_step, 1.0))):
        for side in range(2):
            totals = [None] * fields
            for f in range(fields):
                mix_into(totals, mixers[1:2], n == 1, f, (virtual[side, :, lanes[n][f]],))
            at = slice(layers - 1, layers) if side else slice(0, 1)
            for g in range(fields):
                part = (scale * rates[2 + side]) * totals[g]
                for t in range(columns + 2):
                    target[g, t, at, :] += part[t : t + 1, :]

    def column(t, _):
        for g in range(fields):
            adjoint[g, t] = 0.5 * reach[g, t] + 0.5 * time_step * (
                1.0 + nonlinear_gain * section[g, t]
            ) * reverse[g, t]
        return 0

    lax.fori_loop(0, columns + 2, column, 0)

    def advanced_at(g, t, total):
        advanced[g, t] = 0.5 * flow[g, t] + 0.5 * (section[g, t + 1] + time_step * total)

    def sensitivity_at(g, t, total):
        sensitivity[g, t] = (
            0.5 * cotangent[g, t]
            + adjoint[g, t + 1]
            + time_step * (1.0 + nonlinear_gain * flow[g, t]) * total
        )

    def ends_of(n):
        places = [[(side * 2 + n) * fields + f for side in range(2)] for f in range(fields)]
        return lambda f, t: tuple(ends_two[t, k : k + 1, :] for k in places[f])

    operator(section, shaping, forward_rates, mixers, False, ends_of(0), advanced_at)
    operator(adjoint, identity, reverse_rates, mixers, True, ends_of(1), sensitivity_at)


def interface_weights(slots, codes, cells, sector, block, n_block):
    middle = n_block // 2

    def around(table):
        wide = jnp.concatenate([table[-cells:], table, table[: 2 * cells]], axis=0)
        return lax.dynamic_slice_in_dim(wide, sector * cells, 4 * cells, 0)

    slot = around(slots)
    weight = (around(codes).astype(f32) + 1.0) / 12.0
    index = jnp.arange(4 * cells, dtype=jnp.int32)
    rise = cells * (index // cells)[:, None] + slot
    rotor = jnp.arange(6 * cells, dtype=jnp.int32)
    table = jnp.sum((rise[:, :, None] == rotor) * weight[:, :, None], axis=1)

    def padded(block_of):
        rows, columns = block_of.shape
        return jnp.pad(block_of, ((0, 16 - rows), (0, 4 * cells - columns)))

    def plain(rows, columns, shift):
        return (jnp.arange(columns) == jnp.arange(rows)[:, None] + shift).astype(f32)

    ends = cells + 2
    stator = (table[cells - 1 : 2 * cells + 1, 0 : 4 * cells], table[0 : 3 * cells, cells : 3 * cells].T)
    rotor_side = (table[:, 2 * cells - 1 : 3 * cells + 1].T, table[cells : 3 * cells, cells : 4 * cells])
    sides = []
    for at_interface, inside, pair, shifts in (
        (block == middle, block > 0, stator, (2 * cells - 1, 0)),
        (block == middle - 1, block < n_block - 1, rotor_side, (cells - 1, cells)),
    ):
        forth = jnp.where(at_interface, pair[0], plain(ends, 4 * cells, shifts[0])) * inside
        back = jnp.where(at_interface, pair[1], plain(2 * cells, 3 * cells, shifts[1]))
        sides.append(
            jnp.concatenate(
                [padded(forth), padded(back), padded(forth[1 : cells + 1, cells : 3 * cells])[:cells]], axis=0
            )
        )
    return jnp.stack(sides)


def shards(
    flow_state, cotangent, mix_theta, mix_axial, mix_radial, intersection_slot, intersection_code
):
    fields, columns, layers, radii = flow_state.shape
    sector, block = lax.axis_index("azim"), lax.axis_index("block")
    n_sector, n_block = lax.axis_size("azim"), lax.axis_size("block")
    middle = n_block // 2

    at = lambda s, b: s * n_block + b
    sectors, blocks = range(n_sector), range(n_block)
    pairs_a = [(i, i ^ 1) for i in sectors]
    pairs_b = [(i, (i + 1 if i % 2 else i - 1) % n_sector) for i in sectors]
    pairs_x = [(b, b - 2) for b in range(2, n_block, 2)] + [(b, b + 2) for b in range(1, n_block - 2, 2)]
    pairs_long = [(b, b ^ 1) for b in blocks]
    pairs_pass = [
        (at(i, b), at(j, b ^ 1 if abs(i - j) > 1 else b)) for i, j in pairs_b for b in blocks
    ]
    pairs_far = []
    for s in sectors:
        inside = s + 2 < n_sector
        pairs_far.append((at(s, middle if inside else middle + 1), at((s + 2) % n_sector, middle)))
        inside = s >= 2
        pairs_far.append((at(s, middle - 1 if inside else middle - 2), at((s - 2) % n_sector, middle - 1)))

    place = jnp.stack(
        [
            block % 2,
            1 - sector % 2,
            block != middle,
            block != middle + 1,
            (sector == 0) | (sector == n_sector - 1),
            (block == middle + 1) | (block == middle - 2),
        ]
    ).astype(jnp.int32)
    mixers = (mix_theta, mix_axial, mix_radial)

    shape = lambda *dims: jax.ShapeDtypeStruct(dims, f32)
    whole = shape(*flow_state.shape)
    wide = shape(fields, columns + 2, layers, radii)
    face = shape(2, 2, fields, columns, radii)
    side = shape(2, fields, 2 * layers + columns, radii)
    both = shape(2, 2, 2, fields, columns, radii)
    passed = shape(3, 2, fields, columns, radii)
    far = shape(2, fields, columns, radii)
    work = 4 * 5 * 5 * 3 * 2 * columns * layers * radii

    xsend, own, send_a, send_b = call(
        pack_kernel, (place, flow_state, cotangent), [face, face, side, side], name="pack"
    )
    arrived = lax.ppermute(xsend, "block", pairs_x)
    got_b = lax.ppermute(send_b, "azim", pairs_b)
    (payload,) = call(payload_kernel, (place, arrived, own), [both], name="payload")
    faces = lax.ppermute(payload, "block", pairs_long)
    got_a = lax.ppermute(send_a, "azim", pairs_a)
    got_a, slots, codes = lax.optimization_barrier((got_a, intersection_slot, intersection_code))
    weights = interface_weights(slots, codes, columns, sector, block, n_block)
    section, reverse, reach = call(
        first_kernel,
        (place, *mixers, flow_state, cotangent, got_a, got_b),
        [wide, wide, wide],
        scratch=[(fields, columns + 4, layers, radii)] * 2,
        flops=work,
        name="first",
    )
    faces, section, weights = lax.optimization_barrier((faces, section, weights))
    passes = call(pass_kernel, (place, faces, payload), [passed, passed, far], name="pass_on")
    pass_a = lax.ppermute(passes[0], "azim", pairs_a)
    pass_b = lax.ppermute(passes[1], ("azim", "block"), pairs_pass)
    pass_far = lax.ppermute(passes[2], ("azim", "block"), pairs_far)
    span = 2 * fields * radii
    return tuple(
        call(
            second_kernel,
            (place, *mixers, flow_state, cotangent, section, reverse, reach, got_a, got_b)
            + (faces, pass_a, pass_b, pass_far, weights),
            [whole, whole],
            scratch=[wide.shape] * 3
            + [(2, 4 * columns, span), (2, 2 * columns, span), (2, 3 * columns, span)]
            + [(2, 16, span), (2, 2 * columns, span), (columns, 4 * fields, radii)],
            flops=work,
            name="second",
        )
    )


def solution(mesh):
    placed = (
        P(None, "azim", "block", None),
        P(None, "azim", "block", None),
        P(),
        P(),
        P(),
        P(),
        P(),
    )
    return jax.shard_map(
        shards,
        mesh=mesh,
        in_specs=placed,
        out_specs=(P(None, "azim", "block", None), P(None, "azim", "block", None)),
        check_vma=False,
    )
```

time: 205 us -> 65.9 us (0.32)
  the two profiles are of different devices: /device:TPU:3 before, /device:TPU:36 now
where the time goes in v2:
time: 65.9 us; the launch traced here: 65.5 us
  starting transfers between devices  33.3 us (51%)
  waiting for transfers between devices  14.8 us (22%)
  Pallas kernels  12.4 us (19%)
  local copies, waits for them, and re-layouts  3.56 us (5%)
  between operations  0.91 us (1%)
    ppermute x1, starting transfers between devices, shards(): faces = lax.ppermute(payload, 'block', pairs_long)  16.4 us
    pallas_call x5, Pallas kernels, call(): pl.pallas_call(kernel, out_shape=outs, in_specs=[SMEM if small(x) else VM...  12.4 us
    ppermute x1, waiting for transfers between devices, shards(): faces = lax.ppermute(payload, 'block', pairs_long)  10.8 us
    ppermute x1, starting transfers between devices, shards(): got_b = lax.ppermute(send_b, 'azim', pairs_b)  4.57 us
    ppermute x1, starting transfers between devices, shards(): pass_far = lax.ppermute(passes[2], ('azim', 'block'), pairs_far)  4.02 us
    ppermute x1, waiting for transfers between devices, shards(): pass_far = lax.ppermute(passes[2], ('azim', 'block'), pairs_far)  3.97 us
    unnamed x20, local copies, waits for them, and re-layouts  3.01 us
    ppermute x1, starting transfers between devices, shards(): arrived = lax.ppermute(xsend, 'block', pairs_x)  2.57 us
  transfers between devices with their start and end apart: 7, of which 2 were waited for; matrix products, arithmetic and copies ran while one was open for 2% of the time, Pallas kernels for 7%

profile of v2, /device:TPU:36, one launch (start us, length us, event | category | flops | bytes accessed | tf_op | source)
XLA Modules:
  0.0 65.5 jit_solution(9212255026543739285)
XLA Ops:
  0.7 0.1 stack.52.place
  0.7 0.0 copy-start
  0.8 1.1 %copy-done = f32[5,8,32,128]{3,2,1,0:T(8,128)S(1)} copy-done((f32[5,8,32,128]{3,2,1,0:T(8,128)S(1)}, f32[5,8,32,128]{3,2,1,0:T(8,128)}, u32[]{:S(2)}) %copy-start) | copy-done | bytes 655384
  1.8 0.0 copy-start.2
  1.8 1.1 %copy-done.2 = f32[5,8,32,128]{3,2,1,0:T(8,128)S(1)} copy-done((f32[5,8,32,128]{3,2,1,0:T(8,128)S(1)}, f32[5,8,32,128]{3,2,1,0:T(8,128)}, u32[]{:S(2)}) %copy-start.2) | copy-done | bytes 655384
  2.9 0.0 copy-start.8
  2.9 0.0 copy-start.7
  2.9 0.0 slice-start
  2.9 0.0 slice-start.1
  2.9 0.0 copy-start.3
  2.9 0.7 %pack.1 = (f32[2,2,5,8,128]{4,3,2,1,0:T(8,128)S(1)}, f32[2,2,5,8,128]{4,3,2,1,0:T(8,128)S(1)}, f32[2,5,72,128]{3,2,1,0:T(8,128)S(1)}, f32[2,5,72,128]{3,2,1,0:T(8,128)S(1)}) custom-call(s32[6]{0:T(128)S(1)} %stack.52.place, f32[5,8,32,128]{3,2,1,0:T(8,128)S(1)} %copy-done, f32[5,8,32,128]{3,2,1,0:T(8,128)S(1)} %copy-done.2), custom_call_target="tpu_custom_call" | custom-call | bytes 2211864 | tf_op jit(solution)/shard_map/pack/pallas_call | solution.py:31
  3.7 0.0 copy-start.1
  3.7 2.6 %collective-permute-start = (f32[2,2,5,8,128]{4,3,2,1,0:T(8,128)S(1)}, f32[2,2,5,8,128]{4,3,2,1,0:T(8,128)S(1)}, u32[]{:S(2)}, u32[]{:S(2)}) collective-permute-start(f32[2,2,5,8,128]{4,3,2,1,0:T(8,128)S(1)} %get-tuple-element.18), channel_id=1, source_target_pairs={{2,0},{4,2},{6,4},{1,3},{3,5},{5,7},{10,8},{12,10},{14,12},{9,11},... | collective-permute-start | bytes 245768 | tf_op jit(solution)/shard_map/ppermute | solution.py:374
  6.3 1.9 %collective-permute-start.2 = (f32[2,5,72,128]{3,2,1,0:T(8,128)S(1)}, f32[2,5,72,128]{3,2,1,0:T(8,128)S(1)}, u32[]{:S(2)}, u32[]{:S(2)}) collective-permute-start(f32[2,5,72,128]{3,2,1,0:T(8,128)S(1)} %get-tuple-element.20), channel_id=1, source_target_pairs={{0,8},{8,0},{16,24},{24,16},{32,40},{40,32},{48,56},{56,48},{64,72... | collective-permute-start | bytes 1105928 | tf_op jit(solution)/shard_map/ppermute | solution.py:378
  8.2 4.6 %collective-permute-start.3 = (f32[2,5,72,128]{3,2,1,0:T(8,128)S(1)}, f32[2,5,72,128]{3,2,1,0:T(8,128)S(1)}, u32[]{:S(2)}, u32[]{:S(2)}) collective-permute-start(f32[2,5,72,128]{3,2,1,0:T(8,128)S(1)} %get-tuple-element.22), channel_id=1, source_target_pairs={{0,504},{8,16},{16,8},{24,32},{32,24},{40,48},{48,40},{56,64},{64,... | collective-permute-start | bytes 1105928 | tf_op jit(solution)/shard_map/ppermute | solution.py:375
  12.8 0.0 collective-permute-done.arrived
  12.8 0.6 payload.1.sent
  13.4 16.4 %collective-permute-start.1 = (f32[2,2,2,5,8,128]{5,4,3,2,1,0:T(8,128)S(1)}, f32[2,2,2,5,8,128]{5,4,3,2,1,0:T(8,128)S(1)}, u32[]{:S(2)}, u32[]{:S(2)}) collective-permute-start(f32[2,2,2,5,8,128]{5,4,3,2,1,0:T(8,128)S(1)} %payload.1.sent), channel_id=1, source_target_pairs={{0,1},{1,0},{2,3},{3,2},{4,5},{5,4},{6,7},{7,6},{8,9},{9,8},{10,11... | collective-permute-start | bytes 491528 | tf_op jit(solution)/shard_map/ppermute | solution.py:377
  29.8 0.0 collective-permute-done.2.got_a
  29.8 0.0 copy-done.8
  29.8 0.1 slice.36
  29.9 0.0 copy-done.7
  29.9 0.1 slice.38
  30.0 0.0 slice-done
  30.0 0.1 fusion.14
  30.1 0.0 slice-done.1
  30.1 0.1 fusion.13
  30.1 0.1 select_reduce_fusion
  30.3 0.1 slice.49
  30.3 0.1 slice.51
  30.4 0.1 fusion.5
  30.5 0.1 slice.50
  30.6 0.1 copy.15
  30.6 0.1 copy.16
  30.7 0.1 fusion.6
  30.8 0.1 slice.53
  30.9 0.1 slice_select_fusion
  31.0 0.0 copy-start.4
  31.0 0.0 copy-start.5
  31.0 0.0 copy-start.6
  31.0 0.0 collective-permute-done.3.got_b
  31.0 0.0 copy-done.3
  31.0 0.0 copy-done.1
  31.0 0.6 copy-done.4
  31.7 0.0 copy-done.5
  31.7 0.0 copy-done.6
  31.7 4.3 %first.1 = (f32[5,10,32,128]{3,2,1,0:T(8,128)S(1)}, f32[5,10,32,128]{3,2,1,0:T(8,128)S(1)}, f32[5,10,32,128]{3,2,1,0:T(8,128)S(1)}) custom-call(s32[6]{0:T(128)S(1)} %stack.52.place, f32[5,5]{1,0:T(8,128)S(1)} %copy-done.4, f32[5,5]{1,0:T(8,128)S(1)} %copy-done.5, f32[5,5]{1,0:T(8,128)S(1)} %copy-done.6, f32[5,8,32,128]{3,2,1,0:T(8,128)S(1)} %copy-done.1, ...), custom_call_target="tpu_custom_call" | custom-call | flops 19660800 | bytes 4505924 | tf_op jit(solution)/shard_map/first/pallas_call | solution.py:31
  36.0 10.8 %collective-permute-done.1.faces = f32[2,2,2,5,8,128]{5,4,3,2,1,0:T(8,128)S(1)} collective-permute-done((f32[2,2,2,5,8,128]{5,4,3,2,1,0:T(8,128)S(1)}, f32[2,2,2,5,8,128]{5,4,3,2,1,0:T(8,128)S(1)}, u32[]{:S(2)}, u32[]{:S(2)}) %collective-permute-start.1) | collective-permute-done | bytes 163872 | tf_op jit(solution)/shard_map/ppermute | solution.py:377
  46.8 0.6 pass_on.1
  47.3 1.9 %collective-permute-start.4 = (f32[3,2,5,8,128]{4,3,2,1,0:T(8,128)S(1)}, f32[3,2,5,8,128]{4,3,2,1,0:T(8,128)S(1)}, u32[]{:S(2)}, u32[]{:S(2)}) collective-permute-start(f32[3,2,5,8,128]{4,3,2,1,0:T(8,128)S(1)} %get-tuple-element.30), channel_id=1, source_target_pairs={{0,8},{8,0},{16,24},{24,16},{32,40},{40,32},{48,56},{56,48},{64,72... | collective-permute-start | bytes 368648 | tf_op jit(solution)/shard_map/ppermute | solution.py:391
  49.3 1.9 %collective-permute-start.5 = (f32[3,2,5,8,128]{4,3,2,1,0:T(8,128)S(1)}, f32[3,2,5,8,128]{4,3,2,1,0:T(8,128)S(1)}, u32[]{:S(2)}, u32[]{:S(2)}) collective-permute-start(f32[3,2,5,8,128]{4,3,2,1,0:T(8,128)S(1)} %get-tuple-element.31), channel_id=1, source_target_pairs={{0,505},{1,504},{2,507},{3,506},{4,509},{5,508},{6,511},{7,510},{8... | collective-permute-start | bytes 368648 | tf_op jit(solution)/shard_map/ppermute | solution.py:392
  51.2 4.0 %collective-permute-start.6 = (f32[2,5,8,128]{3,2,1,0:T(8,128)S(1)}, f32[2,5,8,128]{3,2,1,0:T(8,128)S(1)}, u32[]{:S(2)}, u32[]{:S(2)}) collective-permute-start(f32[2,5,8,128]{3,2,1,0:T(8,128)S(1)} %get-tuple-element.32), channel_id=1, source_target_pairs={{4,20},{2,499},{12,28},{10,507},{20,36},{19,3},{28,44},{27,11},{36... | collective-permute-start | bytes 122888 | tf_op jit(solution)/shard_map/ppermute | solution.py:393
  55.2 4.0 %collective-permute-done.6.pass_far = f32[2,5,8,128]{3,2,1,0:T(8,128)S(1)} collective-permute-done((f32[2,5,8,128]{3,2,1,0:T(8,128)S(1)}, f32[2,5,8,128]{3,2,1,0:T(8,128)S(1)}, u32[]{:S(2)}, u32[]{:S(2)}) %collective-permute-start.6) | collective-permute-done | bytes 40992 | tf_op jit(solution)/shard_map/ppermute | solution.py:393
  59.2 0.0 collective-permute-done.4.pass_a
  59.2 0.0 collective-permute-done.5.pass_b
  59.2 6.3 %second.1 = (f32[5,8,32,128]{3,2,1,0:T(8,128)}, f32[5,8,32,128]{3,2,1,0:T(8,128)}) custom-call(s32[6]{0:T(128)S(1)} %stack.52.place, f32[5,5]{1,0:T(8,128)S(1)} %copy-done.4, f32[5,5]{1,0:T(8,128)S(1)} %copy-done.5, f32[5,5]{1,0:T(8,128)S(1)} %copy-done.6, f32[5,8,32,128]{3,2,1,0:T(8,128)S(1)} %copy-done.1, f32[5,8,32,128]{3,2,1,0:T(8,128)S(1)} %copy-done.3, ...), custom_call_target="tpu_custom_call" | custom-call | flops 19660800 | bytes 6277444 | tf_op jit(solution)/shard_map/second/pallas_call | solution.py:31
  (9 shorter events, 0.1 us)
Async XLA Ops:
  0.7 1.1 %copy-start = (f32[5,8,32,128]{3,2,1,0:T(8,128)S(1)}, f32[5,8,32,128]{3,2,1,0:T(8,128)}, u32[]{:S(2)}) copy-start(f32[5,8,32,128]{3,2,1,0:T(8,128)} %flow.5) | copy-start | bytes 1966084
  1.8 1.1 %copy-start.2 = (f32[5,8,32,128]{3,2,1,0:T(8,128)S(1)}, f32[5,8,32,128]{3,2,1,0:T(8,128)}, u32[]{:S(2)}) copy-start(f32[5,8,32,128]{3,2,1,0:T(8,128)} %cotangent.5) | copy-start | bytes 1966084
  2.9 26.9 %copy-start.8 = (s32[512,3]{0,1:T(4,128)S(1)}, s32[512,3]{0,1:T(4,128)}, u32[]{:S(2)}) copy-start(s32[512,3]{0,1:T(4,128)} %param.12) | copy-start | bytes 18436
  2.9 27.0 %copy-start.7 = (s32[512,3]{0,1:T(4,128)S(1)}, s32[512,3]{0,1:T(4,128)}, u32[]{:S(2)}) copy-start(s32[512,3]{0,1:T(4,128)} %param.13) | copy-start | bytes 18436
  2.9 27.0 %slice-start = ((s32[512,3]{0,1:T(4,128)}), s32[16,3]{0,1:T(4,128)S(1)}, s32[]{:S(2)}) async-start(s32[512,3]{0,1:T(4,128)} %param.13), calls=%async_computation | async-start | bytes 4096 | tf_op jit(solution)/shard_map/slice | solution.py:290
  2.9 27.1 %slice-start.1 = ((s32[512,3]{0,1:T(4,128)}), s32[16,3]{0,1:T(4,128)S(1)}, s32[]{:S(2)}) async-start(s32[512,3]{0,1:T(4,128)} %param.12), calls=%async_computation.1 | async-start | bytes 4096 | tf_op jit(solution)/shard_map/slice | solution.py:290
  2.9 28.1 %copy-start.3 = (f32[5,8,32,128]{3,2,1,0:T(8,128)S(1)}, f32[5,8,32,128]{3,2,1,0:T(8,128)}, u32[]{:S(2)}) copy-start(f32[5,8,32,128]{3,2,1,0:T(8,128)} %cotangent.5) | copy-start | bytes 1966084
  3.7 27.3 %copy-start.1 = (f32[5,8,32,128]{3,2,1,0:T(8,128)S(1)}, f32[5,8,32,128]{3,2,1,0:T(8,128)}, u32[]{:S(2)}) copy-start(f32[5,8,32,128]{3,2,1,0:T(8,128)} %flow.5) | copy-start | bytes 1966084
  3.7 9.1 %collective-permute-start = (f32[2,2,5,8,128]{4,3,2,1,0:T(8,128)S(1)}, f32[2,2,5,8,128]{4,3,2,1,0:T(8,128)S(1)}, u32[]{:S(2)}, u32[]{:S(2)}) collective-permute-start(f32[2,2,5,8,128]{4,3,2,1,0:T(8,128)S(1)} %get-tuple-element.18), channel_id=1, source_target_pairs={{2,0},{4,2},{6,4},{1,3},{3,5},{5,7},{10,8},{12,10},{14,12},{9,11},... | collective-permute-start | bytes 245768 | tf_op jit(solution)/shard_map/ppermute | solution.py:374
  6.3 23.5 %collective-permute-start.2 = (f32[2,5,72,128]{3,2,1,0:T(8,128)S(1)}, f32[2,5,72,128]{3,2,1,0:T(8,128)S(1)}, u32[]{:S(2)}, u32[]{:S(2)}) collective-permute-start(f32[2,5,72,128]{3,2,1,0:T(8,128)S(1)} %get-tuple-element.20), channel_id=1, source_target_pairs={{0,8},{8,0},{16,24},{24,16},{32,40},{40,32},{48,56},{56,48},{64,72... | collective-permute-start | bytes 1105928 | tf_op jit(solution)/shard_map/ppermute | solution.py:378
  8.2 22.8 %collective-permute-start.3 = (f32[2,5,72,128]{3,2,1,0:T(8,128)S(1)}, f32[2,5,72,128]{3,2,1,0:T(8,128)S(1)}, u32[]{:S(2)}, u32[]{:S(2)}) collective-permute-start(f32[2,5,72,128]{3,2,1,0:T(8,128)S(1)} %get-tuple-element.22), channel_id=1, source_target_pairs={{0,504},{8,16},{16,8},{24,32},{32,24},{40,48},{48,40},{56,64},{64,... | collective-permute-start | bytes 1105928 | tf_op jit(solution)/shard_map/ppermute | solution.py:375
  13.4 33.4 %collective-permute-start.1 = (f32[2,2,2,5,8,128]{5,4,3,2,1,0:T(8,128)S(1)}, f32[2,2,2,5,8,128]{5,4,3,2,1,0:T(8,128)S(1)}, u32[]{:S(2)}, u32[]{:S(2)}) collective-permute-start(f32[2,2,2,5,8,128]{5,4,3,2,1,0:T(8,128)S(1)} %payload.1.sent), channel_id=1, source_target_pairs={{0,1},{1,0},{2,3},{3,2},{4,5},{5,4},{6,7},{7,6},{8,9},{9,8},{10,11... | collective-permute-start | bytes 491528 | tf_op jit(solution)/shard_map/ppermute | solution.py:377
  31.0 0.7 %copy-start.4 = (f32[5,5]{1,0:T(8,128)S(1)}, f32[5,5]{1,0:T(8,128)}, u32[]{:S(2)}) copy-start(f32[5,5]{1,0:T(8,128)} %mix_t.3) | copy-start | bytes 304
  31.0 0.7 %copy-start.5 = (f32[5,5]{1,0:T(8,128)S(1)}, f32[5,5]{1,0:T(8,128)}, u32[]{:S(2)}) copy-start(f32[5,5]{1,0:T(8,128)} %mix_a.3) | copy-start | bytes 304
  31.0 0.7 %copy-start.6 = (f32[5,5]{1,0:T(8,128)S(1)}, f32[5,5]{1,0:T(8,128)}, u32[]{:S(2)}) copy-start(f32[5,5]{1,0:T(8,128)} %mix_r.3) | copy-start | bytes 304
  47.3 11.9 %collective-permute-start.4 = (f32[3,2,5,8,128]{4,3,2,1,0:T(8,128)S(1)}, f32[3,2,5,8,128]{4,3,2,1,0:T(8,128)S(1)}, u32[]{:S(2)}, u32[]{:S(2)}) collective-permute-start(f32[3,2,5,8,128]{4,3,2,1,0:T(8,128)S(1)} %get-tuple-element.30), channel_id=1, source_target_pairs={{0,8},{8,0},{16,24},{24,16},{32,40},{40,32},{48,56},{56,48},{64,72... | collective-permute-start | bytes 368648 | tf_op jit(solution)/shard_map/ppermute | solution.py:391
  49.3 9.9 %collective-permute-start.5 = (f32[3,2,5,8,128]{4,3,2,1,0:T(8,128)S(1)}, f32[3,2,5,8,128]{4,3,2,1,0:T(8,128)S(1)}, u32[]{:S(2)}, u32[]{:S(2)}) collective-permute-start(f32[3,2,5,8,128]{4,3,2,1,0:T(8,128)S(1)} %get-tuple-element.31), channel_id=1, source_target_pairs={{0,505},{1,504},{2,507},{3,506},{4,509},{5,508},{6,511},{7,510},{8... | collective-permute-start | bytes 368648 | tf_op jit(solution)/shard_map/ppermute | solution.py:392
  51.2 8.0 %collective-permute-start.6 = (f32[2,5,8,128]{3,2,1,0:T(8,128)S(1)}, f32[2,5,8,128]{3,2,1,0:T(8,128)S(1)}, u32[]{:S(2)}, u32[]{:S(2)}) collective-permute-start(f32[2,5,8,128]{3,2,1,0:T(8,128)S(1)} %get-tuple-element.32), channel_id=1, source_target_pairs={{4,20},{2,499},{12,28},{10,507},{20,36},{19,3},{28,44},{27,11},{36... | collective-permute-start | bytes 122888 | tf_op jit(solution)/shard_map/ppermute | solution.py:393

commit v3 on v2

v3 whole, which is shorter than its diff:
```python
import jax
import jax.numpy as jnp
from jax import lax
from jax.experimental import pallas as pl
from jax.experimental.pallas import tpu as pltpu
from jax.sharding import PartitionSpec as P

nonlinear_gain = 0.4
time_step = 0.25
forward_rates = (0.55, 0.15, 0.5, 0.2, 0.35, 0.35)
reverse_rates = (0.15, 0.55, 0.2, 0.5, 0.35, 0.35)
HALF, EVEN, PICK, ACROSS, RISING, SECTOR = range(6)

VMEM = pl.BlockSpec(memory_space=pltpu.VMEM)
SMEM = pl.BlockSpec(memory_space=pltpu.SMEM)
f32 = jnp.float32
exact = lax.Precision.HIGHEST


def shaping(v):
    return v + 0.5 * nonlinear_gain * v * v


def identity(v):
    return v


def call(kernel, ins, outs, scratch=(), flops=0, name=None, fetched=False):
    small = lambda x: x.dtype == jnp.int32 or x.ndim < 3
    place = pl.BlockSpec(memory_space=pl.ANY) if fetched else VMEM
    moved = 4 * (sum(x.size for x in ins) + sum(x.size for x in outs))
    return pl.pallas_call(
        kernel,
        out_shape=outs,
        in_specs=[SMEM if small(x) else place for x in ins],
        out_specs=[VMEM] * len(outs),
        scratch_shapes=[pltpu.VMEM(s, f32) if isinstance(s, tuple) else s for s in scratch],
        compiler_params=pltpu.CompilerParams(vmem_limit_bytes=(60 if fetched else 32) * 2**20),
        cost_estimate=pl.CostEstimate(flops=flops, bytes_accessed=moved, transcendentals=0),
        name=name,
    )(*ins)


def radial_term(v, rates):
    inner_rate, outer_rate = rates[4:]
    radii = v.shape[1]
    lane = lax.broadcasted_iota(jnp.int32, v.shape, 1)
    inner = jnp.where(lane == 0, 0.0, pltpu.roll(v, 1, 1))
    outer = jnp.where(lane == radii - 1, 0.0, pltpu.roll(v, radii - 1, 1))
    return inner_rate * inner + outer_rate * outer - (inner_rate + outer_rate) * v


def mix_into(totals, mixers, transposed, f, terms):
    for g in range(len(totals)):
        at = (f, g) if transposed else (g, f)
        part = None
        for matrix, term in zip(mixers, terms):
            scaled = matrix[at] * term
            part = scaled if part is None else part + scaled
        totals[g] = part if totals[g] is None else totals[g] + part


def axial_term(v, low_end, high_end, rates):
    axial_low, axial_high = rates[2:4]
    count = v.shape[0]
    row = lax.broadcasted_iota(jnp.int32, v.shape, 0)
    lower = jnp.where(row == 0, low_end, pltpu.roll(v, 1, 0))
    upper = jnp.where(row == count - 1, high_end, pltpu.roll(v, count - 1, 0))
    return axial_low * lower + axial_high * upper - (axial_low + axial_high) * v


def theta_term(prior, v, later, rates):
    theta_low, theta_high = rates[:2]
    return theta_low * prior + theta_high * later - (theta_low + theta_high) * v


def axial_term(v, low_end, high_end, rates):
    axial_low, axial_high = rates[2:4]
    count = v.shape[0]
    row = lax.broadcasted_iota(jnp.int32, v.shape, 0)
    lower = jnp.where(row == 0, low_end, pltpu.roll(v, 1, 0))
    upper = jnp.where(row == count - 1, high_end, pltpu.roll(v, count - 1, 0))
    return axial_low * lower + axial_high * upper - (axial_low + axial_high) * v


def theta_term(prior, v, later, rates):
    theta_low, theta_high = rates[:2]
    return theta_low * prior + theta_high * later - (theta_low + theta_high) * v


def axial_term(v, low_end, high_end, rates):
    axial_low, axial_high = rates[2:4]
    count = v.shape[0]
    row = lax.broadcasted_iota(jnp.int32, v.shape, 0)
    lower = jnp.where(row == 0, low_end, pltpu.roll(v, 1, 0))
    upper = jnp.where(row == count - 1, high_end, pltpu.roll(v, count - 1, 0))
    return axial_low * lower + axial_high * upper - (axial_low + axial_high) * v


def theta_term(prior, v, later, rates):
    theta_low, theta_high = rates[:2]
    return theta_low * prior + theta_high * later - (theta_low + theta_high) * v


def axial_term(v, low_end, high_end, rates):
    axial_low, axial_high = rates[2:4]
    count = v.shape[0]
    row = lax.broadcasted_iota(jnp.int32, v.shape, 0)
    lower = jnp.where(row == 0, low_end, pltpu.roll(v, 1, 0))
    upper = jnp.where(row == count - 1, high_end, pltpu.roll(v, count - 1, 0))
    return axial_low * lower + axial_high * upper - (axial_low + axial_high) * v


def theta_term(prior, v, later, rates):
    theta_low, theta_high = rates[:2]
    return theta_low * prior + theta_high * later - (theta_low + theta_high) * v


def axial_term(v, low_end, high_end, rates):
    axial_low, axial_high = rates[2:4]
    count = v.shape[0]
    row = lax.broadcasted_iota(jnp.int32, v.shape, 0)
    lower = jnp.where(row == 0, low_end, pltpu.roll(v, 1, 0))
    upper = jnp.where(row == count - 1, high_end, pltpu.roll(v, count - 1, 0))
    return axial_low * lower + axial_high * upper - (axial_low + axial_high) * v


def theta_term(prior, v, later, rates):
    theta_low, theta_high = rates[:2]
    return theta_low * prior + theta_high * later - (theta_low + theta_high) * v


def axial_term(v, low_end, high_end, rates):
    axial_low, axial_high = rates[2:4]
    count = v.shape[0]
    row = lax.broadcasted_iota(jnp.int32, v.shape, 0)
    lower = jnp.where(row == 0, low_end, pltpu.roll(v, 1, 0))
    upper = jnp.where(row == count - 1, high_end, pltpu.roll(v, count - 1, 0))
    return axial_low * lower + axial_high * upper - (axial_low + axial_high) * v


def theta_term(prior, v, later, rates):
    theta_low, theta_high = rates[:2]
    return theta_low * prior + theta_high * later - (theta_low + theta_high) * v


def axial_term(v, low_end, high_end, rates):
    axial_low, axial_high = rates[2:4]
    count = v.shape[0]
    row = lax.broadcasted_iota(jnp.int32, v.shape, 0)
    lower = jnp.where(row == 0, low_end, pltpu.roll(v, 1, 0))
    upper = jnp.where(row == count - 1, high_end, pltpu.roll(v, count - 1, 0))
    return axial_low * lower + axial_high * upper - (axial_low + axial_high) * v


def theta_term(prior, v, later, rates):
    theta_low, theta_high = rates[:2]
    return theta_low * prior + theta_high * later - (theta_low + theta_high) * v


def operator(source, shaped, rates, mixers, transposed, rows, finish):
    fields, columns, layers, _ = source.shape
    first, last = rows

    def column(t, _):
        totals = [None] * fields
        for f in range(fields):
            v = shaped(source[f, t + 1, first:last, :])
            low_end = shaped(source[f, t + 1, first - 1 : first, :]) if first > 0 else 0.0
            high_end = shaped(source[f, t + 1, last : last + 1, :]) if last < layers else 0.0
            theta = theta_term(
                shaped(source[f, t, first:last, :]), v, shaped(source[f, t + 2, first:last, :]), rates
            )
            axial = axial_term(v, low_end, high_end, rates)
            mix_into(totals, mixers, transposed, f, (theta, axial, radial_term(v, rates)))
        for g in range(fields):
            finish(g, t, totals[g])
        return 0

    lax.fori_loop(0, columns - 2, column, 0)


def first_step(flow, cotangent, mixers, flow_at, cotangent_at, section, adjoint, reverse):
    columns, layers = flow.shape[1:3]

    def section_at(g, t, total):
        section[g, t] = flow_at(g, t) + time_step * total

    def reverse_at(g, t, total):
        reverse[g, t] = total
        adjoint[g, t] = adjoint_of(cotangent_at(g, t), section[g, t], total)

    operator(flow, shaping, forward_rates, mixers, False, (0, layers), section_at)
    operator(cotangent, identity, reverse_rates, mixers, True, (0, layers), reverse_at)


def adjoint_of(reach, section, reverse):
    return 0.5 * reach + 0.5 * time_step * (1.0 + nonlinear_gain * section) * reverse


def advanced_of(flow, section, total):
    return 0.5 * flow + 0.5 * (section + time_step * total)


def sensitivity_of(reach, adjoint, flow, total):
    return 0.5 * reach + adjoint + time_step * (1.0 + nonlinear_gain * flow) * total


def second_step(section, adjoint, mixers, flow_at, cotangent_at, rows, advanced_to, sensitivity_to):
    inner = slice(*rows)

    def advanced_at(g, t, total):
        advanced_to(g, t, advanced_of(flow_at(g, t), section[g, t + 1, inner, :], total))

    def sensitivity_at(g, t, total):
        value = sensitivity_of(cotangent_at(g, t), adjoint[g, t + 1, inner, :], flow_at(g, t), total)
        sensitivity_to(g, t, value)

    operator(section, shaping, forward_rates, mixers, False, rows, advanced_at)
    operator(adjoint, identity, reverse_rates, mixers, True, rows, sensitivity_at)


def pack_axial_kernel(place, flow, cotangent, xsend, farsend, tiles, landed):
    fields, columns, layers, _ = flow.shape
    half = place[HALF]
    at = pl.ds(pl.multiple_of(half * (layers - 8), 8), 8)
    copies = [
        pltpu.make_async_copy(source.at[:, :, at, :], tiles.at[n], landed.at[n])
        for n, source in enumerate((flow, cotangent))
    ]
    for copy in copies:
        copy.start()
    for n in range(2):
        copies[n].wait()
        for f in range(fields):
            for t in range(columns):
                rows = slice(t, t + 1)
                for depth in range(2):
                    low = tiles[n, f, t, depth : depth + 1, :]
                    high = tiles[n, f, t, 7 - depth : 8 - depth, :]
                    value = jnp.where(half == 1, high, low)
                    xsend[depth, n, f, rows, :] = value
                    if depth == 0:
                        farsend[n, f, rows, :] = value


def pack_column(place, n, f, source, first, send):
    columns, layers = source.shape[1:3]
    pick = place[PICK]
    for depth in range(2):
        rows = slice(depth * layers, (depth + 1) * layers)
        send[n, f, rows, :] = source[f, first + depth - 2 * depth * (first > 0)]
    for t in range(columns):
        low = source[f, t, 0:1, :]
        high = source[f, t, layers - 1 : layers, :]
        rows = slice(2 * layers + t, 2 * layers + t + 1)
        send[n, f, rows, :] = jnp.where(pick == 1, high, low)


def pack_own_kernel(place, flow, cotangent, own, send_wrap):
    fields, columns, layers, _ = flow.shape
    half, even = place[HALF], place[EVEN]
    first = jnp.where(even == 1, 0, columns - 1)
    for n, source in enumerate((flow, cotangent)):
        for f in range(fields):
            pack_column(place, n, f, source, first, send_wrap)
            for t in range(columns):
                for depth in range(2):
                    low = source[f, t, depth : depth + 1, :]
                    high = source[f, t, layers - 1 - depth : layers - depth, :]
                    own[depth, n, f, t : t + 1, :] = jnp.where(half == 1, low, high)


def pack_columns(place, flow, cotangent, send_a, send_b):
    fields, columns = flow.shape[:2]
    first = jnp.where(place[EVEN] == 1, 0, columns - 1)
    for n, source in enumerate((flow, cotangent)):
        for f in range(fields):
            pack_column(place, n, f, source, first, send_b)
            pack_column(place, n, f, source, columns - 1 - first, send_a)


def payload_kernel(place, slots, codes, arrived, own, far, send):
    fields, columns = own.shape[2:4]
    count = slots.shape[1]
    half, rising, sector = place[HALF], place[RISING], place[SECTOR]
    for depth in range(2):
        for n in range(2):
            for f in range(fields):
                k = (depth * 2 + n) * fields + f
                send[4 * fields * half + k] = own[depth, n, f]
                send[4 * fields * (1 - half) + k] = arrived[depth, n, f]
    rest = send.shape[0] - 8 * fields
    for k in range(rest):
        send[8 * fields + k] = jnp.zeros(send.shape[1:], f32)

    @pl.when(place[ACROSS] == 1)
    def _():
        weights = []
        for j in range(columns):
            spot = jnp.where(rising == 1, sector * columns - 1, (sector + 2) * columns + j)
            spot = jnp.where(spot < 0, spot + count, jnp.where(spot >= count, spot - count, spot))
            wanted = jnp.where(rising == 1, j, 0)
            weight = jnp.float32(0.0)
            for k in range(slots.shape[0]):
                share = (codes[k, spot].astype(f32) + 1.0) * (1.0 / 12.0)
                weight = weight + jnp.where(slots[k, spot] == wanted, share, 0.0)
            weights.append(weight)
        for n, shaped in enumerate((shaping, identity)):
            for f in range(fields):
                face = shaped(far[n, f])
                total = weights[0] * face[0:1, :]
                for j in range(1, columns):
                    total = total + weights[j] * face[j : j + 1, :]
                side_row = jnp.where(rising == 1, face[columns - 1 : columns, :], face[0:1, :])
                for k, value in ((n * fields + f, total), ((2 + n) * fields + f, side_row)):
                    send[8 * fields + k // 8, k % 8 : k % 8 + 1, :] = value


def inner_kernel(
    place, mix_t, mix_a, mix_r, flow, cotangent,
    section, adjoint, reverse_ends, advanced, sensitivity, send_a, send_b, reverse,
):
    fields, columns, layers, _ = flow.shape
    mixers = (mix_t, mix_a, mix_r)
    pack_columns(place, flow, cotangent, send_a, send_b)
    first_step(
        flow, cotangent, mixers, lambda g, t: flow[g, t + 1], lambda g, t: cotangent[g, t + 1],
        section, adjoint, reverse,
    )
    for side, a in enumerate((0, layers - 1)):
        for g in range(fields):
            for t in range(columns - 2):
                reverse_ends[side, g, t : t + 1, :] = reverse[g, t, a : a + 1, :]
    rows = (8, layers - 8)
    inner = slice(*rows)

    def advanced_to(g, t, value):
        advanced[g, t] = value

    def sensitivity_to(g, t, value):
        sensitivity[g, t] = value

    second_step(
        section, adjoint, mixers, lambda g, t: flow[g, t + 2, inner, :], lambda g, t: cotangent[g, t + 2, inner, :],
        rows, advanced_to, sensitivity_to,
    )


def outer_kernel(
    place, mix_t, mix_a, mix_r, flow, cotangent, got_a, got_b, got_wrap,
    section_inner, adjoint_inner, reverse_ends,
    section, adjoint, ends, advanced, sensitivity, flow_ends, reach_ends, reverse,
):
    fields, columns, layers, _ = flow.shape
    even = place[EVEN]
    mixers = (mix_t, mix_a, mix_r)
    wide = columns + 2
    for n, (source, both) in enumerate(((flow, flow_ends), (cotangent, reach_ends))):
        for f in range(fields):
            for depth in range(2):
                rows = slice(depth * layers, (depth + 1) * layers)
                from_a = got_a[n, f, rows, :]
                from_b = got_b[n, f, rows, :] + got_wrap[n, f, rows, :]
                both[0, f, 1 - depth] = jnp.where(even == 1, from_b, from_a)
                both[0, f, 2 + depth] = source[f, depth]
                both[1, f, 1 - depth] = source[f, columns - 1 - depth]
                both[1, f, 2 + depth] = jnp.where(even == 1, from_a, from_b)
    section[:, 2 : wide - 2] = section_inner[...]
    adjoint[:, 2 : wide - 2] = adjoint_inner[...]
    rows = (8, layers - 8)
    inner = slice(*rows)
    for side in range(2):
        flow_side, reach_side = flow_ends.at[side], reach_ends.at[side]
        at = slice(wide - 2, wide) if side else slice(0, 2)
        first_step(
            flow_side, reach_side, mixers, lambda g, t: flow_side[g, t + 1], lambda g, t: reach_side[g, t + 1],
            section.at[:, at], adjoint.at[:, at], reverse.at[side],
        )
    for side in range(2):
        at = slice(wide - 4, wide) if side else slice(0, 4)
        own = columns - 2 if side else 0

        def advanced_to(g, t, value):
            advanced[g, 2 * side + t] = value

        def sensitivity_to(g, t, value):
            sensitivity[g, 2 * side + t] = value

        second_step(
            section.at[:, at], adjoint.at[:, at], mixers,
            lambda g, t: flow[g, own + t, inner, :], lambda g, t: cotangent[g, own + t, inner, :],
            rows, advanced_to, sensitivity_to,
        )
    for side, a in enumerate((0, layers - 1)):
        row = slice(a, a + 1)
        for g in range(fields):
            for t in range(wide):
                to = slice(t, t + 1)
                ends[side, 0, g, to, :] = section[g, t, row, :]
                if t < 2 or t >= wide - 2:
                    end, place_in = (0, t) if t < 2 else (1, t - wide + 2)
                    ends[side, 1, g, to, :] = reverse[end, g, place_in, row, :]
                    ends[side, 2, g, to, :] = reach_ends[end, g, place_in + 1, row, :]
                else:
                    ends[side, 1, g, to, :] = reverse_ends[side, g, t - 2 : t - 1, :]
                    ends[side, 2, g, to, :] = cotangent[g, t - 1, row, :]


def last_kernel(
    place, mix_t, mix_a, mix_r, flow, cotangent, section, adjoint, ends, faces, pass_a, pass_b, far,
    got_a, got_b, got_wrap, weights, advanced_inner, sensitivity_inner, advanced_outer, sensitivity_outer,
    advanced, sensitivity,
    far_one, far_two, near, virtual, beyond, ends_two, tiles, section_ends,
):
    fields, columns, layers, radii = flow.shape
    even, pick = place[EVEN], place[PICK]
    mixers = (mix_t, mix_a, mix_r)
    all_rates = (forward_rates, reverse_rates)
    all_shapes = (shaping, identity)
    lanes = [
        [slice((n * fields + f) * radii, (n * fields + f + 1) * radii) for f in range(fields)] for n in range(2)
    ]
    inner = slice(8, layers - 8)
    advanced[:, 2 : columns - 2, inner, :] = advanced_inner[...]
    sensitivity[:, 2 : columns - 2, inner, :] = sensitivity_inner[...]
    for side in range(2):
        at = slice(columns - 2, columns) if side else slice(0, 2)
        from_outer = slice(2 * side, 2 * side + 2)
        advanced[:, at, inner, :] = advanced_outer[:, from_outer]
        sensitivity[:, at, inner, :] = sensitivity_outer[:, from_outer]

    def prior_later(from_a, from_b):
        return jnp.where(even == 1, from_b, from_a), jnp.where(even == 1, from_a, from_b)

    def spot(side, depth, n, f):
        return ((side * 2 + depth) * 2 + n) * fields + f

    def sector_rows(place_in):
        return slice(place_in * columns, (place_in + 1) * columns)

    for side in range(2):
        at_own, at_prior, at_later, at_far = ((2, 1, 3, 0), (1, 0, 2, 3))[side]
        for n, shaped in enumerate(all_shapes):
            for f in range(fields):
                lane = lanes[n][f]
                k = spot(side, 0, n, f)
                prior, later = prior_later(pass_a[k], pass_b[k])
                far_one[side, sector_rows(at_own), lane] = shaped(faces[k])
                far_one[side, sector_rows(at_prior), lane] = shaped(prior)
                far_one[side, sector_rows(at_later), lane] = shaped(later)
                far_one[side, sector_rows(at_far), lane] = shaped(far[n, f])
                k = spot(side, 1, n, f)
                beside = prior_later(pass_a[k], pass_b[k])[side]
                far_two[side, sector_rows(at_own - 1), lane] = shaped(faces[k])
                far_two[side, sector_rows(2 - at_own), lane] = shaped(beside)
                rows = slice(2 * layers, 2 * layers + columns)
                prior, later = prior_later(got_a[n, f, rows, :], got_b[n, f, rows, :] + got_wrap[n, f, rows, :])
                near[side, sector_rows(0), lane] = shaped(prior)
                near[side, sector_rows(2), lane] = shaped(later)
                source = (flow, cotangent)[n]
                at = layers - 1 if side else 0
                for t in range(columns):
                    rows = slice(columns + t, columns + t + 1)
                    near[side, rows, lane] = shaped(source[f, t, at : at + 1, :])

    two = 2 * columns
    for side in range(2):
        virtual[side] = jnp.dot(weights[side, 0:16, :], far_one[side], precision=exact)
        back = jnp.dot(weights[side, 16:32, 0 : 3 * columns], near[side], precision=exact)
        here = jnp.where(pick == side, 1.0, 0.0).astype(f32)
        row = slice(columns + 1, columns + 2) if side else slice(0, 1)
        spot_near = 3 * columns if side else columns - 1
        nearest = slice(spot_near, spot_near + 1)
        values = []
        for n, rates in enumerate(all_rates):
            totals = [None] * fields
            for f in range(fields):
                lane = lanes[n][f]
                k = n * fields + f
                for target, at, k in ((virtual, row, k), (far_one, nearest, k + 2 * fields)):
                    target[side, at, lane] += here * faces[8 * fields + k // 8, k % 8 : k % 8 + 1, :]
                v = far_one[side, columns : columns + two, lane]
                theta = theta_term(
                    far_one[side, columns - 1 : columns - 1 + two, lane], v,
                    far_one[side, columns + 1 : columns + 1 + two, lane], rates,
                )
                lower, upper = far_two[side, :, lane], back[:, lane]
                if side:
                    lower, upper = upper, lower
                axial_low, axial_high = rates[2:4]
                axial = axial_low * lower + axial_high * upper - (axial_low + axial_high) * v
                mix_into(totals, mixers, n == 1, f, (theta, axial, radial_term(v, rates)))
            values.append(totals)
        for g in range(fields):
            k = spot(side, 0, 0, g)
            parts = [faces[k], prior_later(pass_a[k], pass_b[k])[side]]
            one = jnp.concatenate(parts if side else parts[::-1], axis=0) + time_step * values[0][g]
            reach_far = far_one[side, columns : columns + two, lanes[1][g]]
            beyond[side, :, lanes[0][g]] = shaping(one)
            beyond[side, :, lanes[1][g]] = adjoint_of(reach_far, one, values[1][g])
        ends_two[side] = jnp.dot(weights[side, 32:40, 0:two], beyond[side], precision=exact)

        totals = [[None] * fields for _ in range(2)]
        for n in range(2):
            for f in range(fields):
                mix_into(totals[n], mixers[1:2], n == 1, f, (virtual[side, :, lanes[n][f]],))
        a = layers - 8 if side else 0
        edge = lax.broadcasted_iota(jnp.int32, (8, radii), 0) == (7 if side else 0)
        for g in range(fields):
            section_end = ends[side, 0, g] + (time_step * forward_rates[2 + side]) * totals[0][g]
            reverse_end = ends[side, 1, g] + reverse_rates[2 + side] * totals[1][g]
            adjoint_end = adjoint_of(ends[side, 2, g], section_end, reverse_end)
            section_ends[side, g] = section_end
            for t in range(columns + 2):
                to = slice(t, t + 1)
                tile = jnp.where(edge, section_end[to, :], section[g, t, a : a + 8, :])
                tiles[side, 0, g, t] = shaping(tile)
                tiles[side, 1, g, t] = jnp.where(edge, adjoint_end[to, :], adjoint[g, t, a : a + 8, :])

        for t in range(columns):
            for n, (rates, shaped, source) in enumerate(zip(all_rates, all_shapes, (section, adjoint))):
                totals = [None] * fields
                for f in range(fields):
                    v = tiles[side, n, f, t + 1]
                    theta = theta_term(tiles[side, n, f, t], v, tiles[side, n, f, t + 2], rates)
                    far_end = ends_two[side, t : t + 1, lanes[n][f]]
                    b = a - 1 if side else a + 8
                    inner_end = shaped(source[f, t + 1, b : b + 1, :])
                    low_end, high_end = (inner_end, far_end) if side else (far_end, inner_end)
                    axial = axial_term(v, low_end, high_end, rates)
                    mix_into(totals, mixers, n == 1, f, (theta, axial, radial_term(v, rates)))
                rows = slice(a, a + 8)
                for g in range(fields):
                    flow_tile = flow[g, t, rows, :]
                    if n == 0:
                        tile = jnp.where(
                            edge, section_ends[side, g, t + 1 : t + 2, :], section[g, t + 1, rows, :]
                        )
                        advanced[g, t, rows, :] = advanced_of(flow_tile, tile, totals[g])
                    else:
                        sensitivity[g, t, rows, :] = sensitivity_of(
                            cotangent[g, t, rows, :], tiles[side, 1, g, t + 1], flow_tile, totals[g]
                        )


def interface_weights(slots, codes, cells, sector, block, n_block):
    middle = n_block // 2

    def around(table):
        wide = jnp.concatenate([table[-cells:], table, table[: 2 * cells]], axis=0)
        return lax.dynamic_slice_in_dim(wide, sector * cells, 4 * cells, 0)

    slot = around(slots)
    weight = (around(codes).astype(f32) + 1.0) / 12.0
    index = jnp.arange(4 * cells, dtype=jnp.int32)
    rise = cells * (index // cells)[:, None] + slot
    rotor = jnp.arange(6 * cells, dtype=jnp.int32)
    table = jnp.sum((rise[:, :, None] == rotor) * weight[:, :, None], axis=1)

    def padded(block_of):
        rows, columns = block_of.shape
        return jnp.pad(block_of, ((0, 16 - rows), (0, 4 * cells - columns)))

    def plain(rows, columns, shift):
        return (jnp.arange(columns) == jnp.arange(rows)[:, None] + shift).astype(f32)

    ends = cells + 2
    stator = (table[cells - 1 : 2 * cells + 1, 0 : 4 * cells], table[0 : 3 * cells, cells : 3 * cells].T)
    rotor_side = (table[:, 2 * cells - 1 : 3 * cells + 1].T, table[cells : 3 * cells, cells : 4 * cells])
    sides = []
    for at_interface, inside, pair, shifts in (
        (block == middle, block > 0, stator, (2 * cells - 1, 0)),
        (block == middle - 1, block < n_block - 1, rotor_side, (cells - 1, cells)),
    ):
        forth = jnp.where(at_interface, pair[0], plain(ends, 4 * cells, shifts[0])) * inside
        back = jnp.where(at_interface, pair[1], plain(2 * cells, 3 * cells, shifts[1]))
        sides.append(
            jnp.concatenate(
                [padded(forth), padded(back), padded(forth[1 : cells + 1, cells : 3 * cells])[:cells]], axis=0
            )
        )
    return jnp.stack(sides)


def shards(
    flow_state, cotangent, mix_theta, mix_axial, mix_radial, intersection_slot, intersection_code
):
    fields, columns, layers, radii = flow_state.shape
    sector, block = lax.axis_index("azim"), lax.axis_index("block")
    n_sector, n_block = lax.axis_size("azim"), lax.axis_size("block")
    middle = n_block // 2

    at = lambda s, b: s * n_block + b
    sectors, blocks = range(n_sector), range(n_block)
    pairs_a = [(i, i ^ 1) for i in sectors]
    pairs_b = [(i, (i + 1 if i % 2 else i - 1) % n_sector) for i in sectors]
    pairs_wrap = [(i, j) for i, j in pairs_b if abs(i - j) > 1]
    pairs_near = [(i, j) for i, j in pairs_b if abs(i - j) == 1]
    pairs_x = [(b, b - 2) for b in range(2, n_block, 2)] + [(b, b + 2) for b in range(1, n_block - 2, 2)]
    pairs_long = [(b, b ^ 1) for b in blocks]
    pairs_pass = [
        (at(i, b), at(j, b ^ 1 if abs(i - j) > 1 else b)) for i, j in pairs_b for b in blocks
    ]
    pairs_far = []
    for s in sectors:
        inside = s + 2 < n_sector
        pairs_far.append((at(s, middle - 1), at((s + 2) % n_sector, middle + 1 if inside else middle)))
        inside = s >= 2
        pairs_far.append((at(s, middle), at((s - 2) % n_sector, middle - 2 if inside else middle - 1)))

    wrap = (sector == 0) | (sector == n_sector - 1)
    place = jnp.stack(
        [
            block % 2,
            1 - sector % 2,
            block != middle,
            (block == middle + 1) | (block == middle - 2),
            block == middle + 1,
            sector,
        ]
    ).astype(jnp.int32)
    mixers = (mix_theta, mix_axial, mix_radial)

    shape = lambda *dims: jax.ShapeDtypeStruct(dims, f32)
    whole = shape(*flow_state.shape)
    inner = shape(fields, columns - 2, layers, radii)
    wide = shape(fields, columns + 2, layers, radii)
    half_out = shape(fields, columns - 4, layers - 16, radii)
    outer_out = shape(fields, 4, layers - 16, radii)
    face = shape(2, 2, fields, columns, radii)
    side = shape(2, fields, 2 * layers + columns, radii)
    sent = shape(8 * fields + (4 * fields + 7) // 8, columns, radii)
    far_face = shape(2, fields, columns, radii)
    work = 4 * 5 * 5 * 3 * columns * layers * radii

    xsend, farsend = call(
        pack_axial_kernel,
        (place, flow_state, cotangent),
        [face, far_face],
        scratch=[(2, fields, columns, 8, radii), pltpu.SemaphoreType.DMA((2,))],
        name="pack_axial",
        fetched=True,
    )
    arrived = lax.ppermute(xsend, "block", pairs_x)
    far = lax.ppermute(farsend, ("azim", "block"), pairs_far)
    own, send_wrap = call(pack_own_kernel, (place, flow_state, cotangent), [face, side], name="pack_own")
    got_wrap = lax.ppermute(send_wrap, "azim", pairs_wrap)
    (payload,) = call(
        payload_kernel,
        (place, intersection_slot.T, intersection_code.T, arrived, own, far),
        [sent],
        name="payload",
    )
    faces = lax.ppermute(payload, "block", pairs_long)

    place_later, payload = lax.optimization_barrier((place, payload))
    section, adjoint, reverse_ends, advanced_inner, sensitivity_inner, send_a, send_b = call(
        inner_kernel,
        (place_later, *mixers, flow_state, cotangent),
        [inner, inner, shape(2, fields, columns, radii), half_out, half_out, side, side],
        scratch=[inner.shape],
        flops=20 * work,
        name="inner",
    )
    got_a = lax.ppermute(send_a, "azim", pairs_a)
    got_b = lax.ppermute(send_b, "azim", pairs_near)
    faces, section, slots, codes = lax.optimization_barrier(
        (faces, section, intersection_slot, intersection_code)
    )
    pass_a = lax.ppermute(faces, "azim", pairs_a)
    pass_b = lax.ppermute(jnp.where(wrap, payload, faces), ("azim", "block"), pairs_pass)
    section, adjoint, ends, advanced_outer, sensitivity_outer = call(
        outer_kernel,
        (place, *mixers, flow_state, cotangent, got_a, got_b, got_wrap, section, adjoint, reverse_ends),
        [wide, wide, shape(2, 3, fields, 16, radii), outer_out, outer_out],
        scratch=[(2, fields, 4, layers, radii), (2, fields, 4, layers, radii), (2, fields, 2, layers, radii)],
        flops=0,
        name="outer",
    )
    weights = interface_weights(slots, codes, columns, sector, block, n_block)
    span = 2 * fields * radii
    return tuple(
        call(
            last_kernel,
            (place, *mixers, flow_state, cotangent, section, adjoint, ends, faces, pass_a, pass_b, far)
            + (got_a, got_b, got_wrap, weights)
            + (advanced_inner, sensitivity_inner, advanced_outer, sensitivity_outer),
            [whole, whole],
            scratch=[
                (2, 4 * columns, span),
                (2, 2 * columns, span),
                (2, 3 * columns, span),
                (2, 16, span),
                (2, 2 * columns, span),
                (2, columns, span),
                (2, 2, fields, columns + 2, 8, radii),
                (2, fields, 16, radii),
            ],
            flops=0,
            name="last",
        )
    )


def solution(mesh):
    placed = (
        P(None, "azim", "block", None),
        P(None, "azim", "block", None),
        P(),
        P(),
        P(),
        P(),
        P(),
    )
    return jax.shard_map(
        shards,
        mesh=mesh,
        in_specs=placed,
        out_specs=(P(None, "azim", "block", None), P(None, "azim", "block", None)),
        check_vma=False,
    )
```

time: 65.9 us -> 73.6 us (1.12)
  the two profiles are of different devices: /device:TPU:36 before, /device:TPU:6 now
where the time goes in v3:
time: 73.6 us; the launch traced here: 72.9 us
  starting transfers between devices  36.1 us (49%)
  Pallas kernels  17.5 us (24%)
  local copies, waits for them, and re-layouts  8.88 us (12%)
  waiting for transfers between devices  6 us (8%)
  other arithmetic  3.51 us (5%)
  between operations  0.94 us (1%)
    pallas_call x6, Pallas kernels, call(): pl.pallas_call(kernel, out_shape=outs, in_specs=[SMEM if small(x) else pl...  17.5 us
    ppermute x1, starting transfers between devices, shards(): arrived = lax.ppermute(xsend, 'block', pairs_x)  15.9 us
    unnamed x42, local copies, waits for them, and re-layouts  6.58 us
    ppermute x1, starting transfers between devices, shards(): lax.ppermute(jnp.where(wrap, payload, faces), ('azim', 'block'), pairs_pass)  6.12 us
    ppermute x1, waiting for transfers between devices, shards(): faces = lax.ppermute(payload, 'block', pairs_long)  5.52 us
    ppermute x1, starting transfers between devices, shards(): faces = lax.ppermute(payload, 'block', pairs_long)  5.38 us
    ppermute x1, starting transfers between devices, shards(): got_wrap = lax.ppermute(send_wrap, 'azim', pairs_wrap)  3.4 us
    ppermute x1, starting transfers between devices, shards(): pass_a = lax.ppermute(faces, 'azim', pairs_a)  2.04 us
  transfers between devices with their start and end apart: 8, of which 2 were waited for; matrix products, arithmetic and copies ran while one was open for 10% of the time, Pallas kernels for 14%

profile of v3, /device:TPU:6, one launch (start us, length us, event | category | flops | bytes accessed | tf_op | source)
XLA Modules:
  0.0 72.9 jit_solution(3855752740322182254)
XLA Ops:
  0.7 0.7 stack.48.place
  1.3 2.5 %pack_axial.1 = (f32[2,2,5,8,128]{4,3,2,1,0:T(8,128)}, f32[2,5,8,128]{3,2,1,0:T(8,128)}) custom-call(s32[6]{0:T(128)} %stack.48.place, f32[5,8,32,128]{3,2,1,0:T(8,128)} %flow.9, f32[5,8,32,128]{3,2,1,0:T(8,128)} %cotangent.9), custom_call_target="tpu_custom_call" | custom-call | bytes 1433624 | tf_op jit(solution)/shard_map/pack_axial/pallas_call | solution.py:32
  3.8 0.0 copy-start.11
  3.9 0.7 collective-permute-start.1
  4.5 15.9 %collective-permute-start = (f32[2,2,5,8,128]{4,3,2,1,0:T(8,128)}, f32[2,2,5,8,128]{4,3,2,1,0:T(8,128)S(1)}, u32[]{:S(2)}, u32[]{:S(2)}) collective-permute-start(f32[2,2,5,8,128]{4,3,2,1,0:T(8,128)} %get-tuple-element.24), channel_id=1, source_target_pairs={{2,0},{4,2},{6,4},{1,3},{3,5},{5,7},{10,8},{12,10},{14,12},{9,11},... | collective-permute-start | bytes 245768 | tf_op jit(solution)/shard_map/ppermute | solution.py:645
  20.4 0.0 copy-done
  20.4 0.0 copy-done.1
  20.5 0.0 copy-done.11
  20.5 0.0 copy-start.7
  20.5 1.4 %pack_own.1 = (f32[2,2,5,8,128]{4,3,2,1,0:T(8,128)S(1)}, f32[2,5,72,128]{3,2,1,0:T(8,128)}) custom-call(s32[6]{0:T(128)S(1)} %copy-done.11, f32[5,8,32,128]{3,2,1,0:T(8,128)S(1)} %copy-done, f32[5,8,32,128]{3,2,1,0:T(8,128)S(1)} %copy-done.1), custom_call_target="tpu_custom_call" | custom-call | bytes 1761304 | tf_op jit(solution)/shard_map/pack_own/pallas_call | solution.py:32
  21.9 3.4 %collective-permute-start.4 = (f32[2,5,72,128]{3,2,1,0:T(8,128)}, f32[2,5,72,128]{3,2,1,0:T(8,128)S(1)}, u32[]{:S(2)}, u32[]{:S(2)}) collective-permute-start(f32[2,5,72,128]{3,2,1,0:T(8,128)} %get-tuple-element.30), channel_id=1, source_target_pairs={{0,504},{504,0},{1,505},{505,1},{2,506},{506,2},{3,507},{507,3},{4... | collective-permute-start | bytes 1105928 | tf_op jit(solution)/shard_map/ppermute | solution.py:648
  25.3 0.5 iota_add_fusion.2
  25.9 0.6 iota_add_fusion.1
  26.4 0.0 collective-permute-done.1.far
  26.4 0.0 collective-permute-done.arrived
  26.4 0.0 copy-done.7
  26.4 0.0 copy-done.6
  26.4 0.8 %payload.1 = f32[43,8,128]{2,1,0:T(8,128)S(1)} custom-call(s32[6]{0:T(128)S(1)} %copy-done.11, s32[3,512]{1,0:T(4,128)S(1)} %bitcast.19, s32[3,512]{1,0:T(4,128)S(1)} %bitcast.18, f32[2,2,5,8,128]{4,3,2,1,0:T(8,128)S(1)} %collective-permute-done.arrived, f32[2,2,5,8,128]{4,3,2,1,0:T(8,128)S(1)} %get-tuple-element.25.own, ...), custom_call_target="tpu_custom_call" | custom-call | bytes 393240 | tf_op jit(solution)/shard_map/payload/pallas_call | solution.py:32
  27.3 5.4 %collective-permute-start.5 = (f32[43,8,128]{2,1,0:T(8,128)S(1)}, f32[43,8,128]{2,1,0:T(8,128)S(1)}, u32[]{:S(2)}, u32[]{:S(2)}) collective-permute-start(f32[43,8,128]{2,1,0:T(8,128)S(1)} %payload.1), channel_id=1, source_target_pairs={{0,1},{1,0},{2,3},{3,2},{4,5},{5,4},{6,7},{7,6},{8,9},{9,8},{10,11... | collective-permute-start | bytes 528392 | tf_op jit(solution)/shard_map/ppermute | solution.py:655
  32.7 0.6 iota_add_fusion
  33.3 0.7 copy-done.10
  33.9 0.0 copy-done.9
  34.0 0.0 copy-done.8
  34.0 4.8 %inner.1 = (f32[5,6,32,128]{3,2,1,0:T(8,128)S(1)}, f32[5,6,32,128]{3,2,1,0:T(8,128)S(1)}, f32[2,5,8,128]{3,2,1,0:T(8,128)S(1)}, f32[5,4,16,128]{3,2,1,0:T(8,128)...) custom-call(s32[6]{0:T(128)S(1)} %copy-done.11, f32[5,5]{1,0:T(8,128)S(1)} %copy-done.8, ...), custom_call_target="tpu_custom_call" | custom-call | flops 196608000 | bytes 3400004 | tf_op jit(solution)/shard_map/inner/pallas_call | solution.py:32
  38.8 0.8 %copy-done.2 = f32[5,6,32,128]{3,2,1,0:T(8,128)} copy-done((f32[5,6,32,128]{3,2,1,0:T(8,128)}, f32[5,6,32,128]{3,2,1,0:T(8,128)S(1)}, u32[]{:S(2)}) %copy-start.2) | copy-done | bytes 491544
  39.5 0.7 copy-done.4
  40.2 1.9 %collective-permute-start.2 = (f32[2,5,72,128]{3,2,1,0:T(8,128)}, f32[2,5,72,128]{3,2,1,0:T(8,128)S(1)}, u32[]{:S(2)}, u32[]{:S(2)}) collective-permute-start(f32[2,5,72,128]{3,2,1,0:T(8,128)} %get-tuple-element.28), channel_id=1, source_target_pairs={{0,8},{8,0},{16,24},{24,16},{32,40},{40,32},{48,56},{56,48},{64,72... | collective-permute-start | bytes 1105928 | tf_op jit(solution)/shard_map/ppermute | solution.py:666
  42.1 0.7 collective-permute-start.3
  42.8 5.5 %collective-permute-done.5.faces = f32[43,8,128]{2,1,0:T(8,128)S(1)} collective-permute-done((f32[43,8,128]{2,1,0:T(8,128)S(1)}, f32[43,8,128]{2,1,0:T(8,128)S(1)}, u32[]{:S(2)}, u32[]{:S(2)}) %collective-permute-start.5) | collective-permute-done | bytes 176160 | tf_op jit(solution)/shard_map/ppermute | solution.py:655
  48.3 0.1 slice.36
  48.4 0.1 slice.38
  48.5 0.1 fusion.14
  48.6 0.1 fusion.13
  48.7 0.1 select_reduce_fusion
  48.8 0.7 slice.49
  49.4 0.1 slice.51
  49.5 0.5 copy-done.18
  50.1 0.1 fusion.5
  50.1 0.6 copy-done.12
  50.7 0.7 slice.50
  51.4 1.4 %copy.15 = f32[24,16]{0,1:T(8,128)} copy(f32[24,16]{1,0:T(8,128)} %slice.49) | data formatting | bytes 3072
  52.8 1.3 %bitcast_select_fusion.1 = f32[16,24]{1,0:T(8,128)} fusion(f32[24,16]{0,1:T(8,128)} %copy.15, pred[]{:T(512)S(6)} %eq.91), kind=kLoop, calls=%fused_computation.25 | loop fusion | flops 1152 | bytes 3073 | tf_op jit(solution)/shard_map/jit(_where)/select_n | solution.py:577
  54.1 0.7 copy.16
  54.7 2.0 %collective-permute-start.6 = (f32[43,8,128]{2,1,0:T(8,128)S(1)}, f32[43,8,128]{2,1,0:T(8,128)S(1)}, u32[]{:S(2)}, u32[]{:S(2)}) collective-permute-start(f32[43,8,128]{2,1,0:T(8,128)S(1)} %collective-permute-done.5.faces), channel_id=1, source_target_pairs={{0,8},{8,0},{16,24},{24,16},{32,40},{40,32},{48,56},{56,48},{64,72... | collective-permute-start | bytes 528392 | tf_op jit(solution)/shard_map/ppermute | solution.py:671
  56.8 0.0 copy-done.19
  56.8 0.0 copy-start.15
  56.8 0.0 copy-start.17
  56.8 0.1 slice_select_fusion
  56.9 0.6 copy-done.15
  57.5 0.0 copy-done.17
  57.5 0.1 fusion.6
  57.6 0.6 copy-done.16
  58.2 0.1 slice.53
  58.3 6.1 %collective-permute-start.7 = (f32[43,8,128]{2,1,0:T(8,128)S(1)}, f32[43,8,128]{2,1,0:T(8,128)S(1)}, u32[]{:S(2)}, u32[]{:S(2)}) collective-permute-start(f32[43,8,128]{2,1,0:T(8,128)S(1)} %broadcast_select_fusion), channel_id=1, source_target_pairs={{0,505},{1,504},{2,507},{3,506},{4,509},{5,508},{6,511},{7,510},{8... | collective-permute-start | bytes 528392 | tf_op jit(solution)/shard_map/ppermute | solution.py:672
  64.4 0.0 copy-done.13
  64.4 0.0 copy-done.14
  64.5 0.0 collective-permute-done.4.got_wrap
  64.5 0.0 collective-permute-done.2.got_a
  64.5 0.0 collective-permute-done.3.got_b
  64.5 3.4 %outer.1 = (f32[5,10,32,128]{3,2,1,0:T(8,128)S(1)}, f32[5,10,32,128]{3,2,1,0:T(8,128)S(1)}, f32[2,3,5,16,128]{4,3,2,1,0:T(8,128)S(1)}, f32[5,4,16,128]{3,2,1,0:T(8,128)S(1)}, f32[5,4,16,128]{3,2,1,0:T(8,128)S(1)}) custom-call(s32[6]{0:T(128)S(1)} %copy-done.11, f32[5,5]{1,0:T(8,128)S(1)} %copy-done.8, f32[5,5]{1,0:T(8,128)S(1)} %copy-done.9, ...), custom_call_target="tpu_custom_call" | custom-call | bytes 5652804 | tf_op jit(solution)/shard_map/outer/pallas_call | solution.py:32
  67.9 0.5 collective-permute-done.7.pass_b
  68.4 0.0 collective-permute-done.6.pass_a
  68.4 0.0 copy-done.5
  68.4 4.6 %last.1 = (f32[5,8,32,128]{3,2,1,0:T(8,128)}, f32[5,8,32,128]{3,2,1,0:T(8,128)}) custom-call(s32[6]{0:T(128)S(1)} %copy-done.11, f32[5,5]{1,0:T(8,128)S(1)} %copy-done.8, f32[5,5]{1,0:T(8,128)S(1)} %copy-done.9, f32[5,5]{1,0:T(8,128)S(1)} %copy-done.10, f32[5,8,32,128]{3,2,1,0:T(8,128)S(1)} %copy-done, f32[5,8,32,128]{3,2,1,0:T(8,128)S(1)} %copy-done.1, ...), custom_call_target="tpu_custom_call" | custom-call | bytes 6846788 | tf_op jit(solution)/shard_map/last/pallas_call | solution.py:32
  (25 shorter events, 0.1 us)
Async XLA Ops:
  1.3 19.1 %copy-start = (f32[5,8,32,128]{3,2,1,0:T(8,128)S(1)}, f32[5,8,32,128]{3,2,1,0:T(8,128)}, u32[]{:S(2)}) copy-start(f32[5,8,32,128]{3,2,1,0:T(8,128)} %flow.9) | copy-start | bytes 1966084
  1.3 19.1 %copy-start.1 = (f32[5,8,32,128]{3,2,1,0:T(8,128)S(1)}, f32[5,8,32,128]{3,2,1,0:T(8,128)}, u32[]{:S(2)}) copy-start(f32[5,8,32,128]{3,2,1,0:T(8,128)} %cotangent.9) | copy-start | bytes 1966084
  3.8 16.6 %copy-start.11 = (s32[6]{0:T(128)S(1)}, s32[6]{0:T(128)}, u32[]{:S(2)}) copy-start(s32[6]{0:T(128)} %stack.48.place) | copy-start | bytes 76
  3.9 22.6 %collective-permute-start.1 = (f32[2,5,8,128]{3,2,1,0:T(8,128)}, f32[2,5,8,128]{3,2,1,0:T(8,128)S(1)}, u32[]{:S(2)}, u32[]{:S(2)}) collective-permute-start(f32[2,5,8,128]{3,2,1,0:T(8,128)} %get-tuple-element.26), channel_id=1, source_target_pairs={{3,21},{4,499},{11,29},{12,507},{19,37},{20,2},{27,45},{28,10},{35... | collective-permute-start | bytes 122888 | tf_op jit(solution)/shard_map/ppermute | solution.py:646
  4.5 21.9 %collective-permute-start = (f32[2,2,5,8,128]{4,3,2,1,0:T(8,128)}, f32[2,2,5,8,128]{4,3,2,1,0:T(8,128)S(1)}, u32[]{:S(2)}, u32[]{:S(2)}) collective-permute-start(f32[2,2,5,8,128]{4,3,2,1,0:T(8,128)} %get-tuple-element.24), channel_id=1, source_target_pairs={{2,0},{4,2},{6,4},{1,3},{3,5},{5,7},{10,8},{12,10},{14,12},{9,11},... | collective-permute-start | bytes 245768 | tf_op jit(solution)/shard_map/ppermute | solution.py:645
  20.5 6.0 %copy-start.7 = (s32[512,3]{0,1:T(4,128)S(1)}, s32[512,3]{0,1:T(4,128)}, u32[]{:S(2)}) copy-start(s32[512,3]{0,1:T(4,128)} %param.12) | copy-start | bytes 18436
  21.9 4.5 %copy-start.6 = (s32[512,3]{0,1:T(4,128)S(1)}, s32[512,3]{0,1:T(4,128)}, u32[]{:S(2)}) copy-start(s32[512,3]{0,1:T(4,128)} %param.13) | copy-start | bytes 18436
  21.9 42.6 %collective-permute-start.4 = (f32[2,5,72,128]{3,2,1,0:T(8,128)}, f32[2,5,72,128]{3,2,1,0:T(8,128)S(1)}, u32[]{:S(2)}, u32[]{:S(2)}) collective-permute-start(f32[2,5,72,128]{3,2,1,0:T(8,128)} %get-tuple-element.30), channel_id=1, source_target_pairs={{0,504},{504,0},{1,505},{505,1},{2,506},{506,2},{3,507},{507,3},{4... | collective-permute-start | bytes 1105928 | tf_op jit(solution)/shard_map/ppermute | solution.py:648
  27.3 21.0 %collective-permute-start.5 = (f32[43,8,128]{2,1,0:T(8,128)S(1)}, f32[43,8,128]{2,1,0:T(8,128)S(1)}, u32[]{:S(2)}, u32[]{:S(2)}) collective-permute-start(f32[43,8,128]{2,1,0:T(8,128)S(1)} %payload.1), channel_id=1, source_target_pairs={{0,1},{1,0},{2,3},{3,2},{4,5},{5,4},{6,7},{7,6},{8,9},{9,8},{10,11... | collective-permute-start | bytes 528392 | tf_op jit(solution)/shard_map/ppermute | solution.py:655
  33.3 0.7 copy-start.10
  33.3 0.7 copy-start.9
  33.3 0.7 copy-start.8
  38.8 0.8 %copy-start.2 = (f32[5,6,32,128]{3,2,1,0:T(8,128)}, f32[5,6,32,128]{3,2,1,0:T(8,128)S(1)}, u32[]{:S(2)}) copy-start(f32[5,6,32,128]{3,2,1,0:T(8,128)S(1)} %get-tuple-element.33.adjoint_inner) | copy-start | bytes 1474564
  39.5 0.7 copy-start.4
  40.2 24.3 %collective-permute-start.2 = (f32[2,5,72,128]{3,2,1,0:T(8,128)}, f32[2,5,72,128]{3,2,1,0:T(8,128)S(1)}, u32[]{:S(2)}, u32[]{:S(2)}) collective-permute-start(f32[2,5,72,128]{3,2,1,0:T(8,128)} %get-tuple-element.28), channel_id=1, source_target_pairs={{0,8},{8,0},{16,24},{24,16},{32,40},{40,32},{48,56},{56,48},{64,72... | collective-permute-start | bytes 1105928 | tf_op jit(solution)/shard_map/ppermute | solution.py:666
  42.1 22.4 %collective-permute-start.3 = (f32[2,5,72,128]{3,2,1,0:T(8,128)}, f32[2,5,72,128]{3,2,1,0:T(8,128)S(1)}, u32[]{:S(2)}, u32[]{:S(2)}) collective-permute-start(f32[2,5,72,128]{3,2,1,0:T(8,128)} %get-tuple-element.29), channel_id=1, source_target_pairs={{8,16},{16,8},{24,32},{32,24},{40,48},{48,40},{56,64},{64,56},{72,... | collective-permute-start | bytes 1105928 | tf_op jit(solution)/shard_map/ppermute | solution.py:667
  49.4 0.6 copy-start.18
  50.1 0.6 copy-start.12
  54.7 2.1 %copy-start.19 = (s32[16]{0:T(128)S(1)}, s32[16]{0:T(128)}, u32[]{:S(2)}) copy-start(s32[16]{0:T(128)} %iota_add_fusion) | copy-start | bytes 196
  54.7 9.8 %copy-start.3 = (f32[5,6,32,128]{3,2,1,0:T(8,128)S(1)}, f32[5,6,32,128]{3,2,1,0:T(8,128)}, u32[]{:S(2)}) copy-start(f32[5,6,32,128]{3,2,1,0:T(8,128)} %copy-done.2) | copy-start | bytes 1474564
  54.7 13.6 %collective-permute-start.6 = (f32[43,8,128]{2,1,0:T(8,128)S(1)}, f32[43,8,128]{2,1,0:T(8,128)S(1)}, u32[]{:S(2)}, u32[]{:S(2)}) collective-permute-start(f32[43,8,128]{2,1,0:T(8,128)S(1)} %collective-permute-done.5.faces), channel_id=1, source_target_pairs={{0,8},{8,0},{16,24},{24,16},{32,40},{40,32},{48,56},{56,48},{64,72... | collective-permute-start | bytes 528392 | tf_op jit(solution)/shard_map/ppermute | solution.py:671
  56.8 0.7 copy-start.15
  56.8 0.7 copy-start.17
  57.5 0.7 copy-start.16
  58.2 6.2 %copy-start.13 = (f32[10,32]{1,0:T(8,128)S(1)}, f32[10,32]{1,0:T(8,128)}, u32[]{:S(2)}) copy-start(f32[10,32]{1,0:T(8,128)} %copy-done.12) | copy-start | bytes 3844
  58.2 6.2 %copy-start.14 = (f32[16,24]{1,0:T(8,128)S(1)}, f32[16,24]{1,0:T(8,128)}, u32[]{:S(2)}) copy-start(f32[16,24]{1,0:T(8,128)} %bitcast_select_fusion.1) | copy-start | bytes 4612
  58.3 10.1 %collective-permute-start.7 = (f32[43,8,128]{2,1,0:T(8,128)S(1)}, f32[43,8,128]{2,1,0:T(8,128)S(1)}, u32[]{:S(2)}, u32[]{:S(2)}) collective-permute-start(f32[43,8,128]{2,1,0:T(8,128)S(1)} %broadcast_select_fusion), channel_id=1, source_target_pairs={{0,505},{1,504},{2,507},{3,506},{4,509},{5,508},{6,511},{7,510},{8... | collective-permute-start | bytes 528392 | tf_op jit(solution)/shard_map/ppermute | solution.py:672
  64.5 3.8 %copy-start.5 = (f32[5,4,16,128]{3,2,1,0:T(8,128)S(1)}, f32[5,4,16,128]{3,2,1,0:T(8,128)}, u32[]{:S(2)}) copy-start(f32[5,4,16,128]{3,2,1,0:T(8,128)} %copy-done.4) | copy-start | bytes 491524

commit v4 on v3

--- a/solution.py
+++ b/solution.py
@@ -25,17 +25,16 @@
     return v
 
 
-def call(kernel, ins, outs, scratch=(), flops=0, name=None, fetched=False):
+def call(kernel, ins, outs, scratch=(), flops=0, name=None):
     small = lambda x: x.dtype == jnp.int32 or x.ndim < 3
-    place = pl.BlockSpec(memory_space=pl.ANY) if fetched else VMEM
     moved = 4 * (sum(x.size for x in ins) + sum(x.size for x in outs))
     return pl.pallas_call(
         kernel,
         out_shape=outs,
-        in_specs=[SMEM if small(x) else place for x in ins],
+        in_specs=[SMEM if small(x) else VMEM for x in ins],
         out_specs=[VMEM] * len(outs),
-        scratch_shapes=[pltpu.VMEM(s, f32) if isinstance(s, tuple) else s for s in scratch],
-        compiler_params=pltpu.CompilerParams(vmem_limit_bytes=(60 if fetched else 32) * 2**20),
+        scratch_shapes=[pltpu.VMEM(s, f32) for s in scratch],
+        compiler_params=pltpu.CompilerParams(vmem_limit_bytes=24 * 2**20),
         cost_estimate=pl.CostEstimate(flops=flops, bytes_accessed=moved, transcendentals=0),
         name=name,
     )(*ins)
@@ -58,6 +57,20 @@
             scaled = matrix[at] * term
             part = scaled if part is None else part + scaled
         totals[g] = part if totals[g] is None else totals[g] + part
+
+
+def axial_term(v, low_end, high_end, rates):
+    axial_low, axial_high = rates[2:4]
+    count = v.shape[0]
+    row = lax.broadcasted_iota(jnp.int32, v.shape, 0)
+    lower = jnp.where(row == 0, low_end, pltpu.roll(v, 1, 0))
+    upper = jnp.where(row == count - 1, high_end, pltpu.roll(v, count - 1, 0))
+    return axial_low * lower + axial_high * upper - (axial_low + axial_high) * v
+
+
+def theta_term(prior, v, later, rates):
+    theta_low, theta_high = rates[:2]
+    return theta_low * prior + theta_high * later - (theta_low + theta_high) * v
 
 
 def axial_term(v, low_end, high_end, rates):
@@ -220,24 +233,16 @@
     operator(adjoint, identity, reverse_rates, mixers, True, rows, sensitivity_at)
 
 
-def pack_axial_kernel(place, flow, cotangent, xsend, farsend, tiles, landed):
+def pack_axial_kernel(place, flow, cotangent, xsend, farsend):
     fields, columns, layers, _ = flow.shape
     half = place[HALF]
-    at = pl.ds(pl.multiple_of(half * (layers - 8), 8), 8)
-    copies = [
-        pltpu.make_async_copy(source.at[:, :, at, :], tiles.at[n], landed.at[n])
-        for n, source in enumerate((flow, cotangent))
-    ]
-    for copy in copies:
-        copy.start()
-    for n in range(2):
-        copies[n].wait()
+    for n, source in enumerate((flow, cotangent)):
         for f in range(fields):
             for t in range(columns):
                 rows = slice(t, t + 1)
                 for depth in range(2):
-                    low = tiles[n, f, t, depth : depth + 1, :]
-                    high = tiles[n, f, t, 7 - depth : 8 - depth, :]
+                    low = source[f, t, depth : depth + 1, :]
+                    high = source[f, t, layers - 1 - depth : layers - depth, :]
                     value = jnp.where(half == 1, high, low)
                     xsend[depth, n, f, rows, :] = value
                     if depth == 0:
@@ -638,9 +643,7 @@
         pack_axial_kernel,
         (place, flow_state, cotangent),
         [face, far_face],
-        scratch=[(2, fields, columns, 8, radii), pltpu.SemaphoreType.DMA((2,))],
         name="pack_axial",
-        fetched=True,
     )
     arrived = lax.ppermute(xsend, "block", pairs_x)
     far = lax.ppermute(farsend, ("azim", "block"), pairs_far)
@@ -663,11 +666,11 @@
         flops=20 * work,
         name="inner",
     )
+    send_a, slots, codes = lax.optimization_barrier((send_a, intersection_slot, intersection_code))
+    weights = interface_weights(slots, codes, columns, sector, block, n_block)
     got_a = lax.ppermute(send_a, "azim", pairs_a)
     got_b = lax.ppermute(send_b, "azim", pairs_near)
-    faces, section, slots, codes = lax.optimization_barrier(
-        (faces, section, intersection_slot, intersection_code)
-    )
+    faces, section, weights = lax.optimization_barrier((faces, section, weights))
     pass_a = lax.ppermute(faces, "azim", pairs_a)
     pass_b = lax.ppermute(jnp.where(wrap, payload, faces), ("azim", "block"), pairs_pass)
     section, adjoint, ends, advanced_outer, sensitivity_outer = call(
@@ -678,7 +681,6 @@
         flops=0,
         name="outer",
     )
-    weights = interface_weights(slots, codes, columns, sector, block, n_block)
     span = 2 * fields * radii
     return tuple(
         call(

time: 73.6 us -> 66.5 us (0.904)
  the two profiles are of different devices: /device:TPU:6 before, /device:TPU:1 now
where the time goes in v4:
time: 66.5 us; the launch traced here: 66.1 us
  starting transfers between devices  42.3 us (64%)
  Pallas kernels  14.9 us (22%)
  local copies, waits for them, and re-layouts  4.38 us (7%)
  waiting for transfers between devices  2.92 us (4%)
  between operations  0.98 us (1%)
    ppermute x1, starting transfers between devices, shards(): faces = lax.ppermute(payload, 'block', pairs_long)  19.3 us
    pallas_call x6, Pallas kernels, call(): pl.pallas_call(kernel, out_shape=outs, in_specs=[SMEM if small(x) else VM...  14.9 us
    ppermute x1, starting transfers between devices, shards(): got_a = lax.ppermute(send_a, 'azim', pairs_a)  7.51 us
    ppermute x1, starting transfers between devices, shards(): pass_a = lax.ppermute(faces, 'azim', pairs_a)  7.2 us
    unnamed x24, local copies, waits for them, and re-layouts  3.83 us
    ppermute x1, starting transfers between devices, shards(): lax.ppermute(jnp.where(wrap, payload, faces), ('azim', 'block'), pairs_pass)  3.64 us
    ppermute x1, waiting for transfers between devices, shards(): arrived = lax.ppermute(xsend, 'block', pairs_x)  2.9 us
    ppermute x1, starting transfers between devices, shards(): got_b = lax.ppermute(send_b, 'azim', pairs_near)  1.92 us
  transfers between devices with their start and end apart: 8, of which 1 were waited for; matrix products, arithmetic and copies ran while one was open for 2% of the time, Pallas kernels for 15%

profile of v4, /device:TPU:1, one launch (start us, length us, event | category | flops | bytes accessed | tf_op | source)
XLA Modules:
  0.0 66.1 jit_solution(18276406748212143187)
XLA Ops:
  0.7 0.1 stack.48.place
  0.7 0.0 copy-start
  0.7 1.1 %copy-done = f32[5,8,32,128]{3,2,1,0:T(8,128)S(1)} copy-done((f32[5,8,32,128]{3,2,1,0:T(8,128)S(1)}, f32[5,8,32,128]{3,2,1,0:T(8,128)}, u32[]{:S(2)}) %copy-start) | copy-done | bytes 655384
  1.8 0.0 copy-start.2
  1.8 1.1 %copy-done.2 = f32[5,8,32,128]{3,2,1,0:T(8,128)S(1)} copy-done((f32[5,8,32,128]{3,2,1,0:T(8,128)S(1)}, f32[5,8,32,128]{3,2,1,0:T(8,128)}, u32[]{:S(2)}) %copy-start.2) | copy-done | bytes 655384
  2.9 0.6 pack_axial.1
  3.6 0.7 %collective-permute-start.1 = (f32[2,5,8,128]{3,2,1,0:T(8,128)S(1)}, f32[2,5,8,128]{3,2,1,0:T(8,128)S(1)}, u32[]{:S(2)}, u32[]{:S(2)}) collective-permute-start(f32[2,5,8,128]{3,2,1,0:T(8,128)S(1)} %get-tuple-element.28), channel_id=1, source_target_pairs={{3,21},{4,499},{11,29},{12,507},{19,37},{20,2},{27,45},{28,10},{35... | collective-permute-start | bytes 122888 | tf_op jit(solution)/shard_map/ppermute | solution.py:649
  4.2 0.0 copy-start.1
  4.3 0.0 copy-start.3
  4.3 1.4 %collective-permute-start = (f32[2,2,5,8,128]{4,3,2,1,0:T(8,128)S(1)}, f32[2,2,5,8,128]{4,3,2,1,0:T(8,128)S(1)}, u32[]{:S(2)}, u32[]{:S(2)}) collective-permute-start(f32[2,2,5,8,128]{4,3,2,1,0:T(8,128)S(1)} %get-tuple-element.26), channel_id=1, source_target_pairs={{2,0},{4,2},{6,4},{1,3},{3,5},{5,7},{10,8},{12,10},{14,12},{9,11},... | collective-permute-start | bytes 245768 | tf_op jit(solution)/shard_map/ppermute | solution.py:648
  5.7 1.4 %pack_own.1 = (f32[2,2,5,8,128]{4,3,2,1,0:T(8,128)S(1)}, f32[2,5,72,128]{3,2,1,0:T(8,128)}) custom-call(s32[6]{0:T(128)S(1)} %stack.48.place, f32[5,8,32,128]{3,2,1,0:T(8,128)S(1)} %copy-done, f32[5,8,32,128]{3,2,1,0:T(8,128)S(1)} %copy-done.2), custom_call_target="tpu_custom_call" | custom-call | bytes 1761304 | tf_op jit(solution)/shard_map/pack_own/pallas_call | solution.py:31
  7.1 0.7 %collective-permute-start.4 = (f32[2,5,72,128]{3,2,1,0:T(8,128)}, f32[2,5,72,128]{3,2,1,0:T(8,128)S(1)}, u32[]{:S(2)}, u32[]{:S(2)}) collective-permute-start(f32[2,5,72,128]{3,2,1,0:T(8,128)} %get-tuple-element.33), channel_id=1, source_target_pairs={{0,504},{504,0},{1,505},{505,1},{2,506},{506,2},{3,507},{507,3},{4... | collective-permute-start | bytes 1105928 | tf_op jit(solution)/shard_map/ppermute | solution.py:651
  7.9 0.0 copy-start.5
  7.9 0.0 copy-start.4
  7.9 0.0 collective-permute-done.1.far
  7.9 2.9 %collective-permute-done.arrived = f32[2,2,5,8,128]{4,3,2,1,0:T(8,128)S(1)} collective-permute-done((f32[2,2,5,8,128]{4,3,2,1,0:T(8,128)S(1)}, f32[2,2,5,8,128]{4,3,2,1,0:T(8,128)S(1)}, u32[]{:S(2)}, u32[]{:S(2)}) %collective-permute-start) | collective-permute-done | bytes 81952 | tf_op jit(solution)/shard_map/ppermute | solution.py:648
  10.8 0.0 copy-done.5
  10.8 0.0 copy-done.4
  10.8 0.0 copy-start.6
  10.8 0.0 copy-start.7
  10.8 0.0 copy-start.8
  10.8 0.8 %payload.1 = f32[43,8,128]{2,1,0:T(8,128)S(1)} custom-call(s32[6]{0:T(128)S(1)} %stack.48.place, s32[3,512]{1,0:T(4,128)S(1)} %bitcast.19, s32[3,512]{1,0:T(4,128)S(1)} %bitcast.18, f32[2,2,5,8,128]{4,3,2,1,0:T(8,128)S(1)} %collective-permute-done.arrived, f32[2,2,5,8,128]{4,3,2,1,0:T(8,128)S(1)} %get-tuple-element.27.own, ...), custom_call_target="tpu_custom_call" | custom-call | bytes 393240 | tf_op jit(solution)/shard_map/payload/pallas_call | solution.py:31
  11.7 19.3 %collective-permute-start.5 = (f32[43,8,128]{2,1,0:T(8,128)S(1)}, f32[43,8,128]{2,1,0:T(8,128)S(1)}, u32[]{:S(2)}, u32[]{:S(2)}) collective-permute-start(f32[43,8,128]{2,1,0:T(8,128)S(1)} %payload.1), channel_id=1, source_target_pairs={{0,1},{1,0},{2,3},{3,2},{4,5},{5,4},{6,7},{7,6},{8,9},{9,8},{10,11... | collective-permute-start | bytes 528392 | tf_op jit(solution)/shard_map/ppermute | solution.py:658
  31.0 0.0 copy-done.1
  31.0 0.0 copy-done.3
  31.0 0.0 copy-done.6
  31.0 0.0 copy-done.7
  31.0 0.0 copy-done.8
  31.0 4.0 %inner.1 = (f32[5,6,32,128]{3,2,1,0:T(8,128)S(1)}, f32[5,6,32,128]{3,2,1,0:T(8,128)S(1)}, f32[2,5,8,128]{3,2,1,0:T(8,128)S(1)}, f32[5,4,16,128]{3,2,1,0:T(8,128)...) custom-call(s32[6]{0:T(128)S(1)} %stack.48.place, ...), custom_call_target="tpu_custom_call" | custom-call | flops 196608000 | bytes 3400004 | tf_op jit(solution)/shard_map/inner/pallas_call | solution.py:31
  35.0 0.0 copy-start.9
  35.0 0.7 %copy-done.9 = f32[2,5,72,128]{3,2,1,0:T(8,128)} copy-done((f32[2,5,72,128]{3,2,1,0:T(8,128)}, f32[2,5,72,128]{3,2,1,0:T(8,128)S(1)}, u32[]{:S(2)}) %copy-start.9) | copy-done | bytes 368664
  35.7 0.0 copy-start.10
  35.7 0.7 %copy-done.10 = f32[2,5,72,128]{3,2,1,0:T(8,128)} copy-done((f32[2,5,72,128]{3,2,1,0:T(8,128)}, f32[2,5,72,128]{3,2,1,0:T(8,128)S(1)}, u32[]{:S(2)}) %copy-start.10) | copy-done | bytes 368664
  36.5 0.1 slice.36
  36.5 0.1 slice.38
  36.6 0.1 fusion.14
  36.7 0.1 fusion.13
  36.8 0.1 select_reduce_fusion
  36.9 0.1 slice.49
  37.0 0.1 slice.51
  37.0 0.1 fusion.5
  37.1 0.1 slice.50
  37.2 0.1 copy.15
  37.3 0.1 copy.16
  37.4 0.1 slice_select_fusion
  37.4 0.1 fusion.6
  37.5 0.1 slice.53
  37.6 7.5 %collective-permute-start.2 = (f32[2,5,72,128]{3,2,1,0:T(8,128)}, f32[2,5,72,128]{3,2,1,0:T(8,128)S(1)}, u32[]{:S(2)}, u32[]{:S(2)}) collective-permute-start(f32[2,5,72,128]{3,2,1,0:T(8,128)} %copy-done.10), channel_id=1, source_target_pairs={{0,8},{8,0},{16,24},{24,16},{32,40},{40,32},{48,56},{56,48},{64,72... | collective-permute-start | bytes 1105928 | tf_op jit(solution)/shard_map/ppermute | solution.py:671
  45.1 1.9 %collective-permute-start.3 = (f32[2,5,72,128]{3,2,1,0:T(8,128)}, f32[2,5,72,128]{3,2,1,0:T(8,128)S(1)}, u32[]{:S(2)}, u32[]{:S(2)}) collective-permute-start(f32[2,5,72,128]{3,2,1,0:T(8,128)} %copy-done.9), channel_id=1, source_target_pairs={{8,16},{16,8},{24,32},{32,24},{40,48},{48,40},{56,64},{64,56},{72,... | collective-permute-start | bytes 1105928 | tf_op jit(solution)/shard_map/ppermute | solution.py:672
  47.1 0.0 collective-permute-done.5.faces
  47.1 3.6 %collective-permute-start.7 = (f32[43,8,128]{2,1,0:T(8,128)S(1)}, f32[43,8,128]{2,1,0:T(8,128)S(1)}, u32[]{:S(2)}, u32[]{:S(2)}) collective-permute-start(f32[43,8,128]{2,1,0:T(8,128)S(1)} %broadcast_select_fusion), channel_id=1, source_target_pairs={{0,505},{1,504},{2,507},{3,506},{4,509},{5,508},{6,511},{7,510},{8... | collective-permute-start | bytes 528392 | tf_op jit(solution)/shard_map/ppermute | solution.py:675
  50.8 7.2 %collective-permute-start.6 = (f32[43,8,128]{2,1,0:T(8,128)S(1)}, f32[43,8,128]{2,1,0:T(8,128)S(1)}, u32[]{:S(2)}, u32[]{:S(2)}) collective-permute-start(f32[43,8,128]{2,1,0:T(8,128)S(1)} %collective-permute-done.5.faces), channel_id=1, source_target_pairs={{0,8},{8,0},{16,24},{24,16},{32,40},{40,32},{48,56},{56,48},{64,72... | collective-permute-start | bytes 528392 | tf_op jit(solution)/shard_map/ppermute | solution.py:674
  58.0 0.0 collective-permute-done.4.got_wrap
  58.0 0.0 collective-permute-done.2.got_a
  58.0 0.0 collective-permute-done.3.got_b
  58.0 3.4 %outer.1 = (f32[5,10,32,128]{3,2,1,0:T(8,128)S(1)}, f32[5,10,32,128]{3,2,1,0:T(8,128)S(1)}, f32[2,3,5,16,128]{4,3,2,1,0:T(8,128)S(1)}, f32[5,4,16,128]{3,2,1,0:T(8,128)S(1)}, f32[5,4,16,128]{3,2,1,0:T(8,128)S(1)}) custom-call(s32[6]{0:T(128)S(1)} %stack.48.place, f32[5,5]{1,0:T(8,128)S(1)} %copy-done.6, f32[5,5]{1,0:T(8,128)S(1)} %copy-done.7, ...), custom_call_target="tpu_custom_call" | custom-call | bytes 5652804 | tf_op jit(solution)/shard_map/outer/pallas_call | solution.py:31
  61.4 0.0 collective-permute-done.7.pass_b
  61.4 0.0 collective-permute-done.6.pass_a
  61.4 4.6 %last.1 = (f32[5,8,32,128]{3,2,1,0:T(8,128)}, f32[5,8,32,128]{3,2,1,0:T(8,128)}) custom-call(s32[6]{0:T(128)S(1)} %stack.48.place, f32[5,5]{1,0:T(8,128)S(1)} %copy-done.6, f32[5,5]{1,0:T(8,128)S(1)} %copy-done.7, f32[5,5]{1,0:T(8,128)S(1)} %copy-done.8, f32[5,8,32,128]{3,2,1,0:T(8,128)S(1)} %copy-done.1, f32[5,8,32,128]{3,2,1,0:T(8,128)S(1)} %copy-done.3, ...), custom_call_target="tpu_custom_call" | custom-call | bytes 6846788 | tf_op jit(solution)/shard_map/last/pallas_call | solution.py:31
  (12 shorter events, 0.1 us)
Async XLA Ops:
  0.7 1.1 %copy-start = (f32[5,8,32,128]{3,2,1,0:T(8,128)S(1)}, f32[5,8,32,128]{3,2,1,0:T(8,128)}, u32[]{:S(2)}) copy-start(f32[5,8,32,128]{3,2,1,0:T(8,128)} %flow.9) | copy-start | bytes 1966084
  1.8 1.1 %copy-start.2 = (f32[5,8,32,128]{3,2,1,0:T(8,128)S(1)}, f32[5,8,32,128]{3,2,1,0:T(8,128)}, u32[]{:S(2)}) copy-start(f32[5,8,32,128]{3,2,1,0:T(8,128)} %cotangent.9) | copy-start | bytes 1966084
  3.6 4.3 %collective-permute-start.1 = (f32[2,5,8,128]{3,2,1,0:T(8,128)S(1)}, f32[2,5,8,128]{3,2,1,0:T(8,128)S(1)}, u32[]{:S(2)}, u32[]{:S(2)}) collective-permute-start(f32[2,5,8,128]{3,2,1,0:T(8,128)S(1)} %get-tuple-element.28), channel_id=1, source_target_pairs={{3,21},{4,499},{11,29},{12,507},{19,37},{20,2},{27,45},{28,10},{35... | collective-permute-start | bytes 122888 | tf_op jit(solution)/shard_map/ppermute | solution.py:649
  4.2 26.7 %copy-start.1 = (f32[5,8,32,128]{3,2,1,0:T(8,128)S(1)}, f32[5,8,32,128]{3,2,1,0:T(8,128)}, u32[]{:S(2)}) copy-start(f32[5,8,32,128]{3,2,1,0:T(8,128)} %flow.9) | copy-start | bytes 1966084
  4.3 26.7 %copy-start.3 = (f32[5,8,32,128]{3,2,1,0:T(8,128)S(1)}, f32[5,8,32,128]{3,2,1,0:T(8,128)}, u32[]{:S(2)}) copy-start(f32[5,8,32,128]{3,2,1,0:T(8,128)} %cotangent.9) | copy-start | bytes 1966084
  4.3 6.5 %collective-permute-start = (f32[2,2,5,8,128]{4,3,2,1,0:T(8,128)S(1)}, f32[2,2,5,8,128]{4,3,2,1,0:T(8,128)S(1)}, u32[]{:S(2)}, u32[]{:S(2)}) collective-permute-start(f32[2,2,5,8,128]{4,3,2,1,0:T(8,128)S(1)} %get-tuple-element.26), channel_id=1, source_target_pairs={{2,0},{4,2},{6,4},{1,3},{3,5},{5,7},{10,8},{12,10},{14,12},{9,11},... | collective-permute-start | bytes 245768 | tf_op jit(solution)/shard_map/ppermute | solution.py:648
  7.1 50.9 %collective-permute-start.4 = (f32[2,5,72,128]{3,2,1,0:T(8,128)}, f32[2,5,72,128]{3,2,1,0:T(8,128)S(1)}, u32[]{:S(2)}, u32[]{:S(2)}) collective-permute-start(f32[2,5,72,128]{3,2,1,0:T(8,128)} %get-tuple-element.33), channel_id=1, source_target_pairs={{0,504},{504,0},{1,505},{505,1},{2,506},{506,2},{3,507},{507,3},{4... | collective-permute-start | bytes 1105928 | tf_op jit(solution)/shard_map/ppermute | solution.py:651
  7.9 2.9 %copy-start.5 = (s32[512,3]{0,1:T(4,128)S(1)}, s32[512,3]{0,1:T(4,128)}, u32[]{:S(2)}) copy-start(s32[512,3]{0,1:T(4,128)} %param.12) | copy-start | bytes 18436
  7.9 2.9 %copy-start.4 = (s32[512,3]{0,1:T(4,128)S(1)}, s32[512,3]{0,1:T(4,128)}, u32[]{:S(2)}) copy-start(s32[512,3]{0,1:T(4,128)} %param.13) | copy-start | bytes 18436
  10.8 20.2 %copy-start.6 = (f32[5,5]{1,0:T(8,128)S(1)}, f32[5,5]{1,0:T(8,128)}, u32[]{:S(2)}) copy-start(f32[5,5]{1,0:T(8,128)} %mix_t.5) | copy-start | bytes 304
  10.8 20.2 %copy-start.7 = (f32[5,5]{1,0:T(8,128)S(1)}, f32[5,5]{1,0:T(8,128)}, u32[]{:S(2)}) copy-start(f32[5,5]{1,0:T(8,128)} %mix_a.5) | copy-start | bytes 304
  10.8 20.2 %copy-start.8 = (f32[5,5]{1,0:T(8,128)S(1)}, f32[5,5]{1,0:T(8,128)}, u32[]{:S(2)}) copy-start(f32[5,5]{1,0:T(8,128)} %mix_r.5) | copy-start | bytes 304
  11.7 35.4 %collective-permute-start.5 = (f32[43,8,128]{2,1,0:T(8,128)S(1)}, f32[43,8,128]{2,1,0:T(8,128)S(1)}, u32[]{:S(2)}, u32[]{:S(2)}) collective-permute-start(f32[43,8,128]{2,1,0:T(8,128)S(1)} %payload.1), channel_id=1, source_target_pairs={{0,1},{1,0},{2,3},{3,2},{4,5},{5,4},{6,7},{7,6},{8,9},{9,8},{10,11... | collective-permute-start | bytes 528392 | tf_op jit(solution)/shard_map/ppermute | solution.py:658
  35.0 0.7 %copy-start.9 = (f32[2,5,72,128]{3,2,1,0:T(8,128)}, f32[2,5,72,128]{3,2,1,0:T(8,128)S(1)}, u32[]{:S(2)}) copy-start(f32[2,5,72,128]{3,2,1,0:T(8,128)S(1)} %get-tuple-element.32) | copy-start | bytes 1105924
  35.7 0.7 %copy-start.10 = (f32[2,5,72,128]{3,2,1,0:T(8,128)}, f32[2,5,72,128]{3,2,1,0:T(8,128)S(1)}, u32[]{:S(2)}) copy-start(f32[2,5,72,128]{3,2,1,0:T(8,128)S(1)} %get-tuple-element.31) | copy-start | bytes 1105924
  37.6 20.4 %collective-permute-start.2 = (f32[2,5,72,128]{3,2,1,0:T(8,128)}, f32[2,5,72,128]{3,2,1,0:T(8,128)S(1)}, u32[]{:S(2)}, u32[]{:S(2)}) collective-permute-start(f32[2,5,72,128]{3,2,1,0:T(8,128)} %copy-done.10), channel_id=1, source_target_pairs={{0,8},{8,0},{16,24},{24,16},{32,40},{40,32},{48,56},{56,48},{64,72... | collective-permute-start | bytes 1105928 | tf_op jit(solution)/shard_map/ppermute | solution.py:671
  45.1 12.9 %collective-permute-start.3 = (f32[2,5,72,128]{3,2,1,0:T(8,128)}, f32[2,5,72,128]{3,2,1,0:T(8,128)S(1)}, u32[]{:S(2)}, u32[]{:S(2)}) collective-permute-start(f32[2,5,72,128]{3,2,1,0:T(8,128)} %copy-done.9), channel_id=1, source_target_pairs={{8,16},{16,8},{24,32},{32,24},{40,48},{48,40},{56,64},{64,56},{72,... | collective-permute-start | bytes 1105928 | tf_op jit(solution)/shard_map/ppermute | solution.py:672
  47.1 14.3 %collective-permute-start.7 = (f32[43,8,128]{2,1,0:T(8,128)S(1)}, f32[43,8,128]{2,1,0:T(8,128)S(1)}, u32[]{:S(2)}, u32[]{:S(2)}) collective-permute-start(f32[43,8,128]{2,1,0:T(8,128)S(1)} %broadcast_select_fusion), channel_id=1, source_target_pairs={{0,505},{1,504},{2,507},{3,506},{4,509},{5,508},{6,511},{7,510},{8... | collective-permute-start | bytes 528392 | tf_op jit(solution)/shard_map/ppermute | solution.py:675
  50.8 10.7 %collective-permute-start.6 = (f32[43,8,128]{2,1,0:T(8,128)S(1)}, f32[43,8,128]{2,1,0:T(8,128)S(1)}, u32[]{:S(2)}, u32[]{:S(2)}) collective-permute-start(f32[43,8,128]{2,1,0:T(8,128)S(1)} %collective-permute-done.5.faces), channel_id=1, source_target_pairs={{0,8},{8,0},{16,24},{24,16},{32,40},{40,32},{48,56},{56,48},{64,72... | collective-permute-start | bytes 528392 | tf_op jit(solution)/shard_map/ppermute | solution.py:674

commit v5 on v4

--- a/solution.py
+++ b/solution.py
@@ -57,6 +57,34 @@
             scaled = matrix[at] * term
             part = scaled if part is None else part + scaled
         totals[g] = part if totals[g] is None else totals[g] + part
+
+
+def axial_term(v, low_end, high_end, rates):
+    axial_low, axial_high = rates[2:4]
+    count = v.shape[0]
+    row = lax.broadcasted_iota(jnp.int32, v.shape, 0)
+    lower = jnp.where(row == 0, low_end, pltpu.roll(v, 1, 0))
+    upper = jnp.where(row == count - 1, high_end, pltpu.roll(v, count - 1, 0))
+    return axial_low * lower + axial_high * upper - (axial_low + axial_high) * v
+
+
+def theta_term(prior, v, later, rates):
+    theta_low, theta_high = rates[:2]
+    return theta_low * prior + theta_high * later - (theta_low + theta_high) * v
+
+
+def axial_term(v, low_end, high_end, rates):
+    axial_low, axial_high = rates[2:4]
+    count = v.shape[0]
+    row = lax.broadcasted_iota(jnp.int32, v.shape, 0)
+    lower = jnp.where(row == 0, low_end, pltpu.roll(v, 1, 0))
+    upper = jnp.where(row == count - 1, high_end, pltpu.roll(v, count - 1, 0))
+    return axial_low * lower + axial_high * upper - (axial_low + axial_high) * v
+
+
+def theta_term(prior, v, later, rates):
+    theta_low, theta_high = rates[:2]
+    return theta_low * prior + theta_high * later - (theta_low + theta_high) * v
 
 
 def axial_term(v, low_end, high_end, rates):
@@ -233,7 +261,7 @@
     operator(adjoint, identity, reverse_rates, mixers, True, rows, sensitivity_at)
 
 
-def pack_axial_kernel(place, flow, cotangent, xsend, farsend):
+def pack_faces_kernel(place, flow, cotangent, face_a, face_b, farsend):
     fields, columns, layers, _ = flow.shape
     half = place[HALF]
     for n, source in enumerate((flow, cotangent)):
@@ -241,12 +269,14 @@
             for t in range(columns):
                 rows = slice(t, t + 1)
                 for depth in range(2):
+                    k = (depth * 2 + n) * fields + f
                     low = source[f, t, depth : depth + 1, :]
                     high = source[f, t, layers - 1 - depth : layers - depth, :]
+                    face_a[k, rows, :] = jnp.where(half == 1, low, high)
                     value = jnp.where(half == 1, high, low)
-                    xsend[depth, n, f, rows, :] = value
+                    face_b[k, rows, :] = value
                     if depth == 0:
-                        farsend[n, f, rows, :] = value
+                        farsend[k, rows, :] = value
 
 
 def pack_column(place, n, f, source, first, send):
@@ -262,20 +292,6 @@
         send[n, f, rows, :] = jnp.where(pick == 1, high, low)
 
 
-def pack_own_kernel(place, flow, cotangent, own, send_wrap):
-    fields, columns, layers, _ = flow.shape
-    half, even = place[HALF], place[EVEN]
-    first = jnp.where(even == 1, 0, columns - 1)
-    for n, source in enumerate((flow, cotangent)):
-        for f in range(fields):
-            pack_column(place, n, f, source, first, send_wrap)
-            for t in range(columns):
-                for depth in range(2):
-                    low = source[f, t, depth : depth + 1, :]
-                    high = source[f, t, layers - 1 - depth : layers - depth, :]
-                    own[depth, n, f, t : t + 1, :] = jnp.where(half == 1, low, high)
-
-
 def pack_columns(place, flow, cotangent, send_a, send_b):
     fields, columns = flow.shape[:2]
     first = jnp.where(place[EVEN] == 1, 0, columns - 1)
@@ -285,19 +301,14 @@
             pack_column(place, n, f, source, columns - 1 - first, send_a)
 
 
-def payload_kernel(place, slots, codes, arrived, own, far, send):
-    fields, columns = own.shape[2:4]
+def payload_kernel(place, slots, codes, face, far, send):
+    whole, columns = face.shape[:2]
+    fields = whole // 4
     count = slots.shape[1]
-    half, rising, sector = place[HALF], place[RISING], place[SECTOR]
-    for depth in range(2):
-        for n in range(2):
-            for f in range(fields):
-                k = (depth * 2 + n) * fields + f
-                send[4 * fields * half + k] = own[depth, n, f]
-                send[4 * fields * (1 - half) + k] = arrived[depth, n, f]
-    rest = send.shape[0] - 8 * fields
-    for k in range(rest):
-        send[8 * fields + k] = jnp.zeros(send.shape[1:], f32)
+    rising, sector = place[RISING], place[SECTOR]
+    send[0:whole] = face[...]
+    for k in range(whole, send.shape[0]):
+        send[k] = jnp.zeros(send.shape[1:], f32)
 
     @pl.when(place[ACROSS] == 1)
     def _():
@@ -313,13 +324,13 @@
             weights.append(weight)
         for n, shaped in enumerate((shaping, identity)):
             for f in range(fields):
-                face = shaped(far[n, f])
-                total = weights[0] * face[0:1, :]
+                layer = shaped(far[n * fields + f])
+                total = weights[0] * layer[0:1, :]
                 for j in range(1, columns):
-                    total = total + weights[j] * face[j : j + 1, :]
-                side_row = jnp.where(rising == 1, face[columns - 1 : columns, :], face[0:1, :])
+                    total = total + weights[j] * layer[j : j + 1, :]
+                side_row = jnp.where(rising == 1, layer[columns - 1 : columns, :], layer[0:1, :])
                 for k, value in ((n * fields + f, total), ((2 + n) * fields + f, side_row)):
-                    send[8 * fields + k // 8, k % 8 : k % 8 + 1, :] = value
+                    send[whole + k // 8, k % 8 : k % 8 + 1, :] = value
 
 
 def inner_kernel(
@@ -353,7 +364,7 @@
 
 
 def outer_kernel(
-    place, mix_t, mix_a, mix_r, flow, cotangent, got_a, got_b, got_wrap,
+    place, mix_t, mix_a, mix_r, flow, cotangent, got_a, got_b,
     section_inner, adjoint_inner, reverse_ends,
     section, adjoint, ends, advanced, sensitivity, flow_ends, reach_ends, reverse,
 ):
@@ -365,8 +376,7 @@
         for f in range(fields):
             for depth in range(2):
                 rows = slice(depth * layers, (depth + 1) * layers)
-                from_a = got_a[n, f, rows, :]
-                from_b = got_b[n, f, rows, :] + got_wrap[n, f, rows, :]
+                from_a, from_b = got_a[n, f, rows, :], got_b[n, f, rows, :]
                 both[0, f, 1 - depth] = jnp.where(even == 1, from_b, from_a)
                 both[0, f, 2 + depth] = source[f, depth]
                 both[1, f, 1 - depth] = source[f, columns - 1 - depth]
@@ -413,8 +423,8 @@
 
 
 def last_kernel(
-    place, mix_t, mix_a, mix_r, flow, cotangent, section, adjoint, ends, faces, pass_a, pass_b, far,
-    got_a, got_b, got_wrap, weights, advanced_inner, sensitivity_inner, advanced_outer, sensitivity_outer,
+    place, mix_t, mix_a, mix_r, flow, cotangent, section, adjoint, ends, long_a, long_b, pass_a, pass_b,
+    wrap_a, wrap_b, far, got_a, got_b, weights, advanced_inner, sensitivity_inner, advanced_outer, sensitivity_outer,
     advanced, sensitivity,
     far_one, far_two, near, virtual, beyond, ends_two, tiles, section_ends,
 ):
@@ -435,11 +445,26 @@
         advanced[:, at, inner, :] = advanced_outer[:, from_outer]
         sensitivity[:, at, inner, :] = sensitivity_outer[:, from_outer]
 
+    half = place[HALF]
+    whole = 4 * fields
+
     def prior_later(from_a, from_b):
         return jnp.where(even == 1, from_b, from_a), jnp.where(even == 1, from_a, from_b)
 
-    def spot(side, depth, n, f):
-        return ((side * 2 + depth) * 2 + n) * fields + f
+    def of_side(side, from_long_a, from_long_b):
+        return jnp.where(half == 1 - side, from_long_a, from_long_b)
+
+    def faces_at(side, k):
+        return of_side(side, long_a[k], long_b[k])
+
+    def beside_at(side, k):
+        return prior_later(
+            of_side(side, pass_a[k], pass_a[whole + k]),
+            of_side(side, pass_b[k] + wrap_a[k], pass_b[whole + k] + wrap_b[k]),
+        )
+
+    def spot(depth, n, f):
+        return (depth * 2 + n) * fields + f
 
     def sector_rows(place_in):
         return slice(place_in * columns, (place_in + 1) * columns)
@@ -449,18 +474,18 @@
         for n, shaped in enumerate(all_shapes):
             for f in range(fields):
                 lane = lanes[n][f]
-                k = spot(side, 0, n, f)
-                prior, later = prior_later(pass_a[k], pass_b[k])
-                far_one[side, sector_rows(at_own), lane] = shaped(faces[k])
+                k = spot(0, n, f)
+                prior, later = beside_at(side, k)
+                far_one[side, sector_rows(at_own), lane] = shaped(faces_at(side, k))
                 far_one[side, sector_rows(at_prior), lane] = shaped(prior)
                 far_one[side, sector_rows(at_later), lane] = shaped(later)
-                far_one[side, sector_rows(at_far), lane] = shaped(far[n, f])
-                k = spot(side, 1, n, f)
-                beside = prior_later(pass_a[k], pass_b[k])[side]
-                far_two[side, sector_rows(at_own - 1), lane] = shaped(faces[k])
+                far_one[side, sector_rows(at_far), lane] = shaped(far[n * fields + f])
+                k = spot(1, n, f)
+                beside = beside_at(side, k)[side]
+                far_two[side, sector_rows(at_own - 1), lane] = shaped(faces_at(side, k))
                 far_two[side, sector_rows(2 - at_own), lane] = shaped(beside)
                 rows = slice(2 * layers, 2 * layers + columns)
-                prior, later = prior_later(got_a[n, f, rows, :], got_b[n, f, rows, :] + got_wrap[n, f, rows, :])
+                prior, later = prior_later(got_a[n, f, rows, :], got_b[n, f, rows, :])
                 near[side, sector_rows(0), lane] = shaped(prior)
                 near[side, sector_rows(2), lane] = shaped(later)
                 source = (flow, cotangent)[n]
@@ -484,7 +509,7 @@
                 lane = lanes[n][f]
                 k = n * fields + f
                 for target, at, k in ((virtual, row, k), (far_one, nearest, k + 2 * fields)):
-                    target[side, at, lane] += here * faces[8 * fields + k // 8, k % 8 : k % 8 + 1, :]
+                    target[side, at, lane] += here * long_b[whole + k // 8, k % 8 : k % 8 + 1, :]
                 v = far_one[side, columns : columns + two, lane]
                 theta = theta_term(
                     far_one[side, columns - 1 : columns - 1 + two, lane], v,
@@ -498,8 +523,8 @@
                 mix_into(totals, mixers, n == 1, f, (theta, axial, radial_term(v, rates)))
             values.append(totals)
         for g in range(fields):
-            k = spot(side, 0, 0, g)
-            parts = [faces[k], prior_later(pass_a[k], pass_b[k])[side]]
+            k = spot(0, 0, g)
+            parts = [faces_at(side, k), beside_at(side, k)[side]]
             one = jnp.concatenate(parts if side else parts[::-1], axis=0) + time_step * values[0][g]
             reach_far = far_one[side, columns : columns + two, lanes[1][g]]
             beyond[side, :, lanes[0][g]] = shaping(one)
@@ -600,28 +625,28 @@
     sectors, blocks = range(n_sector), range(n_block)
     pairs_a = [(i, i ^ 1) for i in sectors]
     pairs_b = [(i, (i + 1 if i % 2 else i - 1) % n_sector) for i in sectors]
+    pairs_near = [(i, j) for i, j in pairs_b if abs(i - j) == 1]
     pairs_wrap = [(i, j) for i, j in pairs_b if abs(i - j) > 1]
-    pairs_near = [(i, j) for i, j in pairs_b if abs(i - j) == 1]
-    pairs_x = [(b, b - 2) for b in range(2, n_block, 2)] + [(b, b + 2) for b in range(1, n_block - 2, 2)]
-    pairs_long = [(b, b ^ 1) for b in blocks]
-    pairs_pass = [
-        (at(i, b), at(j, b ^ 1 if abs(i - j) > 1 else b)) for i, j in pairs_b for b in blocks
-    ]
-    pairs_far = []
+    axial_a = [(b, b ^ 1) for b in blocks]
+    axial_b = [(b, b + 1 if b % 2 else b - 1) for b in blocks if 0 < b < n_block - 1]
+    pairs_wrap_a, pairs_wrap_b = (
+        [(at(i, b), at(j, c)) for i, j in pairs_wrap for b, c in axial] for axial in (axial_a, axial_b)
+    )
+    pairs_far, pairs_far_wrap = [], []
     for s in sectors:
-        inside = s + 2 < n_sector
-        pairs_far.append((at(s, middle - 1), at((s + 2) % n_sector, middle + 1 if inside else middle)))
-        inside = s >= 2
-        pairs_far.append((at(s, middle), at((s - 2) % n_sector, middle - 2 if inside else middle - 1)))
-
-    wrap = (sector == 0) | (sector == n_sector - 1)
+        for b, shift in ((middle - 1, 2), (middle, -2)):
+            if 0 <= s + shift < n_sector:
+                pairs_far.append((at(s, b), at(s + shift, b)))
+            else:
+                pairs_far_wrap.append((at(s, b), at((s + shift) % n_sector, n_block - 1 - b)))
+
     place = jnp.stack(
         [
             block % 2,
             1 - sector % 2,
             block != middle,
-            (block == middle + 1) | (block == middle - 2),
-            block == middle + 1,
+            (block == middle) | (block == middle - 1),
+            block == middle - 1,
             sector,
         ]
     ).astype(jnp.int32)
@@ -633,29 +658,21 @@
     wide = shape(fields, columns + 2, layers, radii)
     half_out = shape(fields, columns - 4, layers - 16, radii)
     outer_out = shape(fields, 4, layers - 16, radii)
-    face = shape(2, 2, fields, columns, radii)
     side = shape(2, fields, 2 * layers + columns, radii)
-    sent = shape(8 * fields + (4 * fields + 7) // 8, columns, radii)
-    far_face = shape(2, fields, columns, radii)
+    face = shape(4 * fields, columns, radii)
+    sent = shape(4 * fields + (4 * fields + 7) // 8, columns, radii)
+    layer = shape(2 * fields, columns, radii)
     work = 4 * 5 * 5 * 3 * columns * layers * radii
 
-    xsend, farsend = call(
-        pack_axial_kernel,
-        (place, flow_state, cotangent),
-        [face, far_face],
-        name="pack_axial",
-    )
-    arrived = lax.ppermute(xsend, "block", pairs_x)
+    face_a, face_b, farsend = call(
+        pack_faces_kernel, (place, flow_state, cotangent), [face, face, layer], name="pack_faces"
+    )
     far = lax.ppermute(farsend, ("azim", "block"), pairs_far)
-    own, send_wrap = call(pack_own_kernel, (place, flow_state, cotangent), [face, side], name="pack_own")
-    got_wrap = lax.ppermute(send_wrap, "azim", pairs_wrap)
+    long_a = lax.ppermute(face_a, "block", axial_a)
     (payload,) = call(
-        payload_kernel,
-        (place, intersection_slot.T, intersection_code.T, arrived, own, far),
-        [sent],
-        name="payload",
-    )
-    faces = lax.ppermute(payload, "block", pairs_long)
+        payload_kernel, (place, intersection_slot.T, intersection_code.T, face_b, far), [sent], name="payload"
+    )
+    long_b = lax.ppermute(payload, "block", axial_b)
 
     place_later, payload = lax.optimization_barrier((place, payload))
     section, adjoint, reverse_ends, advanced_inner, sensitivity_inner, send_a, send_b = call(
@@ -666,16 +683,25 @@
         flops=20 * work,
         name="inner",
     )
-    send_a, slots, codes = lax.optimization_barrier((send_a, intersection_slot, intersection_code))
+    section, face_a, face_b, farsend, slots, codes = lax.optimization_barrier(
+        (section, face_a, face_b, farsend, intersection_slot, intersection_code)
+    )
+    got_b = lax.ppermute(send_b, "azim", pairs_b)
+    got_a = lax.ppermute(send_a, "azim", pairs_a)
+    wrap_a = lax.ppermute(face_a, ("azim", "block"), pairs_wrap_a)
+    wrap_b = lax.ppermute(face_b, ("azim", "block"), pairs_wrap_b)
+    far_wrap = lax.ppermute(farsend, ("azim", "block"), pairs_far_wrap)
     weights = interface_weights(slots, codes, columns, sector, block, n_block)
-    got_a = lax.ppermute(send_a, "azim", pairs_a)
-    got_b = lax.ppermute(send_b, "azim", pairs_near)
-    faces, section, weights = lax.optimization_barrier((faces, section, weights))
-    pass_a = lax.ppermute(faces, "azim", pairs_a)
-    pass_b = lax.ppermute(jnp.where(wrap, payload, faces), ("azim", "block"), pairs_pass)
+
+    long_b, section, weights, wrap_a, wrap_b, far_wrap = lax.optimization_barrier(
+        (long_b, section, weights, wrap_a, wrap_b, far_wrap)
+    )
+    both = jnp.concatenate([long_a, long_b[: 4 * fields]])
+    pass_a = lax.ppermute(both, "azim", pairs_a)
+    pass_b = lax.ppermute(both, "azim", pairs_near)
     section, adjoint, ends, advanced_outer, sensitivity_outer = call(
         outer_kernel,
-        (place, *mixers, flow_state, cotangent, got_a, got_b, got_wrap, section, adjoint, reverse_ends),
+        (place, *mixers, flow_state, cotangent, got_a, got_b, section, adjoint, reverse_ends),
         [wide, wide, shape(2, 3, fields, 16, radii), outer_out, outer_out],
         scratch=[(2, fields, 4, layers, radii), (2, fields, 4, layers, radii), (2, fields, 2, layers, radii)],
         flops=0,
@@ -685,8 +711,8 @@
     return tuple(
         call(
             last_kernel,
-            (place, *mixers, flow_state, cotangent, section, adjoint, ends, faces, pass_a, pass_b, far)
-            + (got_a, got_b, got_wrap, weights)
+            (place, *mixers, flow_state, cotangent, section, adjoint, ends, long_a, long_b, pass_a, pass_b)
+            + (wrap_a, wrap_b, far_wrap, got_a, got_b, weights)
             + (advanced_inner, sensitivity_inner, advanced_outer, sensitivity_outer),
             [whole, whole],
             scratch=[

time: 66.5 us -> 83.2 us (1.25)
  the two profiles are of different devices: /device:TPU:1 before, /device:TPU:6 now
where the time goes in v5:
time: 83.2 us; the launch traced here: 82.6 us
  starting transfers between devices  49.1 us (59%)
  Pallas kernels  13.5 us (16%)
  waiting for transfers between devices  9.48 us (11%)
  local copies, waits for them, and re-layouts  6.04 us (7%)
  other arithmetic  3.51 us (4%)
  between operations  0.97 us (1%)
    ppermute x1, starting transfers between devices, shards(): wrap_b = lax.ppermute(face_b, ('azim', 'block'), pairs_wrap_b)  17.9 us
    ppermute x1, starting transfers between devices, shards(): long_a = lax.ppermute(face_a, 'block', axial_a)  15.7 us
    pallas_call x5, Pallas kernels, call(): pl.pallas_call(kernel, out_shape=outs, in_specs=[SMEM if small(x) else VM...  13.5 us
    ppermute x1, waiting for transfers between devices, shards(): got_b = lax.ppermute(send_b, 'azim', pairs_b)  9.46 us
    ppermute x1, starting transfers between devices, shards(): pass_a = lax.ppermute(both, 'azim', pairs_a)  5.38 us
    unnamed x32, local copies, waits for them, and re-layouts  4.91 us
    ppermute x1, starting transfers between devices, shards(): long_b = lax.ppermute(payload, 'block', axial_b)  2.19 us
    ppermute x1, starting transfers between devices, shards(): wrap_a = lax.ppermute(face_a, ('azim', 'block'), pairs_wrap_a)  2.11 us
  transfers between devices with their start and end apart: 10, of which 1 were waited for; matrix products, arithmetic and copies ran while one was open for 6% of the time, Pallas kernels for 10%

profile of v5, /device:TPU:6, one launch (start us, length us, event | category | flops | bytes accessed | tf_op | source)
XLA Modules:
  0.0 82.6 jit_solution(1558196878375018958)
XLA Ops:
  0.7 0.1 stack.48.place
  0.7 0.0 copy-start
  0.7 1.1 %copy-done = f32[5,8,32,128]{3,2,1,0:T(8,128)S(1)} copy-done((f32[5,8,32,128]{3,2,1,0:T(8,128)S(1)}, f32[5,8,32,128]{3,2,1,0:T(8,128)}, u32[]{:S(2)}) %copy-start) | copy-done | bytes 655384
  1.8 0.0 copy-start.2
  1.8 1.1 %copy-done.2 = f32[5,8,32,128]{3,2,1,0:T(8,128)S(1)} copy-done((f32[5,8,32,128]{3,2,1,0:T(8,128)S(1)}, f32[5,8,32,128]{3,2,1,0:T(8,128)}, u32[]{:S(2)}) %copy-start.2) | copy-done | bytes 655384
  2.9 0.0 copy-start.1
  2.9 0.0 copy-start.3
  2.9 0.7 pack_faces.1
  3.6 0.7 collective-permute-start
  4.3 15.7 %collective-permute-start.7 = (f32[20,8,128]{2,1,0:T(8,128)S(1)}, f32[20,8,128]{2,1,0:T(8,128)S(1)}, u32[]{:S(2)}, u32[]{:S(2)}) collective-permute-start(f32[20,8,128]{2,1,0:T(8,128)S(1)} %get-tuple-element.40), channel_id=1, source_target_pairs={{0,1},{1,0},{2,3},{3,2},{4,5},{5,4},{6,7},{7,6},{8,9},{9,8},{10,11... | collective-permute-start | bytes 245768 | tf_op jit(solution)/shard_map/ppermute | solution.py:671
  20.0 0.5 iota_add_fusion.2
  20.5 0.5 iota_add_fusion.1
  21.1 0.0 collective-permute-done.far
  21.1 0.7 copy-done.5
  21.8 0.0 copy-done.4
  21.8 0.8 payload.1
  22.6 2.2 %collective-permute-start.3 = (f32[23,8,128]{2,1,0:T(8,128)S(1)}, f32[23,8,128]{2,1,0:T(8,128)S(1)}, u32[]{:S(2)}, u32[]{:S(2)}) collective-permute-start(f32[23,8,128]{2,1,0:T(8,128)S(1)} %payload.1), channel_id=1, source_target_pairs={{1,2},{2,1},{3,4},{4,3},{5,6},{6,5},{9,10},{10,9},{11,12},{12,11},... | collective-permute-start | bytes 282632 | tf_op jit(solution)/shard_map/ppermute | solution.py:675
  24.8 0.0 copy-done.1
  24.8 0.0 copy-done.3
  24.8 0.0 copy-done.6
  24.8 0.0 copy-done.7
  24.8 0.0 copy-done.8
  24.8 4.0 %inner.1 = (f32[5,6,32,128]{3,2,1,0:T(8,128)S(1)}, f32[5,6,32,128]{3,2,1,0:T(8,128)S(1)}, f32[2,5,8,128]{3,2,1,0:T(8,128)S(1)}, f32[5,4,16,128]{3,2,1,0:T(8,128)...) custom-call(s32[6]{0:T(128)S(1)} %stack.48.place, ...), custom_call_target="tpu_custom_call" | custom-call | flops 196608000 | bytes 3400004 | tf_op jit(solution)/shard_map/inner/pallas_call | solution.py:31
  28.8 0.0 copy-start.9
  28.9 0.7 copy-done.9
  29.6 0.1 slice.39
  29.7 0.1 slice.41
  29.7 0.1 fusion.14
  29.8 0.1 fusion.13
  29.9 0.1 select_reduce_fusion
  30.0 0.1 slice.53
  30.1 0.1 slice.55
  30.2 0.5 copy-done.14
  30.7 0.1 fusion.5
  30.8 0.1 slice.54
  30.8 0.6 pad_slice_fusion.1
  31.4 0.0 copy-done.10
  31.4 0.7 slice_select_fusion
  32.1 0.7 copy.15
  32.8 0.7 bitcast_select_fusion.1
  33.5 0.1 copy.16
  33.6 0.7 fusion.6
  34.3 0.1 slice.57
  34.3 0.7 collective-permute-start.6
  35.0 2.1 %collective-permute-start.4 = (f32[20,8,128]{2,1,0:T(8,128)S(1)}, f32[20,8,128]{2,1,0:T(8,128)S(1)}, u32[]{:S(2)}, u32[]{:S(2)}) collective-permute-start(f32[20,8,128]{2,1,0:T(8,128)S(1)} %get-tuple-element.40), channel_id=1, source_target_pairs={{0,505},{1,504},{2,507},{3,506},{4,509},{5,508},{6,511},{7,510},{5... | collective-permute-start | bytes 245768 | tf_op jit(solution)/shard_map/ppermute | solution.py:691
  37.1 17.9 %collective-permute-start.5 = (f32[20,8,128]{2,1,0:T(8,128)S(1)}, f32[20,8,128]{2,1,0:T(8,128)S(1)}, u32[]{:S(2)}, u32[]{:S(2)}) collective-permute-start(f32[20,8,128]{2,1,0:T(8,128)S(1)} %get-tuple-element.41.face), channel_id=1, source_target_pairs={{1,506},{2,505},{3,508},{4,507},{5,510},{6,509},{505,2},{506,1},{5... | collective-permute-start | bytes 245768 | tf_op jit(solution)/shard_map/ppermute | solution.py:692
  55.0 0.0 copy-done.13
  55.0 0.0 copy-done.11
  55.0 0.0 copy-done.12
  55.1 0.0 collective-permute-done.6.far
  55.1 1.9 %collective-permute-start.1 = (f32[2,5,72,128]{3,2,1,0:T(8,128)}, f32[2,5,72,128]{3,2,1,0:T(8,128)S(1)}, u32[]{:S(2)}, u32[]{:S(2)}) collective-permute-start(f32[2,5,72,128]{3,2,1,0:T(8,128)} %copy-done.9), channel_id=1, source_target_pairs={{0,8},{8,0},{16,24},{24,16},{32,40},{40,32},{48,56},{56,48},{64,72... | collective-permute-start | bytes 1105928 | tf_op jit(solution)/shard_map/ppermute | solution.py:690
  57.0 0.0 collective-permute-done.4.wrap_a
  57.0 1.9 %collective-permute-start.2 = (f32[2,5,72,128]{3,2,1,0:T(8,128)S(1)}, f32[2,5,72,128]{3,2,1,0:T(8,128)S(1)}, u32[]{:S(2)}, u32[]{:S(2)}) collective-permute-start(f32[2,5,72,128]{3,2,1,0:T(8,128)S(1)} %get-tuple-element.34), channel_id=1, source_target_pairs={{0,504},{8,16},{16,8},{24,32},{32,24},{40,48},{48,40},{56,64},{64,... | collective-permute-start | bytes 1105928 | tf_op jit(solution)/shard_map/ppermute | solution.py:689
  59.0 0.0 collective-permute-done.5.wrap_b
  59.0 0.0 collective-permute-done.3.long_b
  59.0 0.0 collective-permute-done.7.long_a
  59.0 0.7 collective-permute-start.9
  59.7 5.4 %collective-permute-start.8 = (f32[40,8,128]{2,1,0:T(8,128)S(1)}, f32[40,8,128]{2,1,0:T(8,128)S(1)}, u32[]{:S(2)}, u32[]{:S(2)}) collective-permute-start(f32[40,8,128]{2,1,0:T(8,128)S(1)} %pad_maximum_fusion), channel_id=1, source_target_pairs={{0,8},{8,0},{16,24},{24,16},{32,40},{40,32},{48,56},{56,48},{64,72... | collective-permute-start | bytes 491528 | tf_op jit(solution)/shard_map/ppermute | solution.py:700
  65.1 0.0 collective-permute-done.1.got_a
  65.1 9.5 %collective-permute-done.2.got_b = f32[2,5,72,128]{3,2,1,0:T(8,128)S(1)} collective-permute-done((f32[2,5,72,128]{3,2,1,0:T(8,128)S(1)}, f32[2,5,72,128]{3,2,1,0:T(8,128)S(1)}, u32[]{:S(2)}, u32[]{:S(2)}) %collective-permute-start.2) | collective-permute-done | bytes 368672 | tf_op jit(solution)/shard_map/ppermute | solution.py:689
  74.6 3.4 %outer.1 = (f32[5,10,32,128]{3,2,1,0:T(8,128)S(1)}, f32[5,10,32,128]{3,2,1,0:T(8,128)S(1)}, f32[2,3,5,16,128]{4,3,2,1,0:T(8,128)S(1)}, f32[5,4,16,128]{3,2,1,0:T(8,128)S(1)}, f32[5,4,16,128]{3,2,1,0:T(8,128)S(1)}) custom-call(s32[6]{0:T(128)S(1)} %stack.48.place, f32[5,5]{1,0:T(8,128)S(1)} %copy-done.6, f32[5,5]{1,0:T(8,128)S(1)} %copy-done.7, ...), custom_call_target="tpu_custom_call" | custom-call | bytes 5284164 | tf_op jit(solution)/shard_map/outer/pallas_call | solution.py:31
  77.9 0.0 collective-permute-done.9.pass_b
  77.9 0.0 collective-permute-done.8.pass_a
  77.9 4.7 %last.1 = (f32[5,8,32,128]{3,2,1,0:T(8,128)}, f32[5,8,32,128]{3,2,1,0:T(8,128)}) custom-call(s32[6]{0:T(128)S(1)} %stack.48.place, f32[5,5]{1,0:T(8,128)S(1)} %copy-done.6, f32[5,5]{1,0:T(8,128)S(1)} %copy-done.7, f32[5,5]{1,0:T(8,128)S(1)} %copy-done.8, f32[5,8,32,128]{3,2,1,0:T(8,128)S(1)} %copy-done.1, f32[5,8,32,128]{3,2,1,0:T(8,128)S(1)} %copy-done.3, ...), custom_call_target="tpu_custom_call" | custom-call | bytes 6617412 | tf_op jit(solution)/shard_map/last/pallas_call | solution.py:31
  (19 shorter events, 0.1 us)
Async XLA Ops:
  0.7 1.1 %copy-start = (f32[5,8,32,128]{3,2,1,0:T(8,128)S(1)}, f32[5,8,32,128]{3,2,1,0:T(8,128)}, u32[]{:S(2)}) copy-start(f32[5,8,32,128]{3,2,1,0:T(8,128)} %flow.7) | copy-start | bytes 1966084
  1.8 1.1 %copy-start.2 = (f32[5,8,32,128]{3,2,1,0:T(8,128)S(1)}, f32[5,8,32,128]{3,2,1,0:T(8,128)}, u32[]{:S(2)}) copy-start(f32[5,8,32,128]{3,2,1,0:T(8,128)} %cotangent.7) | copy-start | bytes 1966084
  2.9 21.9 %copy-start.1 = (f32[5,8,32,128]{3,2,1,0:T(8,128)S(1)}, f32[5,8,32,128]{3,2,1,0:T(8,128)}, u32[]{:S(2)}) copy-start(f32[5,8,32,128]{3,2,1,0:T(8,128)} %flow.7) | copy-start | bytes 1966084
  2.9 21.9 %copy-start.3 = (f32[5,8,32,128]{3,2,1,0:T(8,128)S(1)}, f32[5,8,32,128]{3,2,1,0:T(8,128)}, u32[]{:S(2)}) copy-start(f32[5,8,32,128]{3,2,1,0:T(8,128)} %cotangent.7) | copy-start | bytes 1966084
  3.6 17.5 %collective-permute-start = (f32[10,8,128]{2,1,0:T(8,128)S(1)}, f32[10,8,128]{2,1,0:T(8,128)S(1)}, u32[]{:S(2)}, u32[]{:S(2)}) collective-permute-start(f32[10,8,128]{2,1,0:T(8,128)S(1)} %get-tuple-element.42), channel_id=1, source_target_pairs={{3,19},{11,27},{19,35},{20,4},{27,43},{28,12},{35,51},{36,20},{43,... | collective-permute-start | bytes 122888 | tf_op jit(solution)/shard_map/ppermute | solution.py:670
  4.3 54.7 %collective-permute-start.7 = (f32[20,8,128]{2,1,0:T(8,128)S(1)}, f32[20,8,128]{2,1,0:T(8,128)S(1)}, u32[]{:S(2)}, u32[]{:S(2)}) collective-permute-start(f32[20,8,128]{2,1,0:T(8,128)S(1)} %get-tuple-element.40), channel_id=1, source_target_pairs={{0,1},{1,0},{2,3},{3,2},{4,5},{5,4},{6,7},{7,6},{8,9},{9,8},{10,11... | collective-permute-start | bytes 245768 | tf_op jit(solution)/shard_map/ppermute | solution.py:671
  21.1 0.7 copy-start.5
  21.1 0.7 copy-start.4
  21.8 3.0 %copy-start.6 = (f32[5,5]{1,0:T(8,128)S(1)}, f32[5,5]{1,0:T(8,128)}, u32[]{:S(2)}) copy-start(f32[5,5]{1,0:T(8,128)} %mix_t.5) | copy-start | bytes 304
  21.8 3.0 %copy-start.7 = (f32[5,5]{1,0:T(8,128)S(1)}, f32[5,5]{1,0:T(8,128)}, u32[]{:S(2)}) copy-start(f32[5,5]{1,0:T(8,128)} %mix_a.5) | copy-start | bytes 304
  21.8 3.1 %copy-start.8 = (f32[5,5]{1,0:T(8,128)S(1)}, f32[5,5]{1,0:T(8,128)}, u32[]{:S(2)}) copy-start(f32[5,5]{1,0:T(8,128)} %mix_r.5) | copy-start | bytes 304
  22.6 36.4 %collective-permute-start.3 = (f32[23,8,128]{2,1,0:T(8,128)S(1)}, f32[23,8,128]{2,1,0:T(8,128)S(1)}, u32[]{:S(2)}, u32[]{:S(2)}) collective-permute-start(f32[23,8,128]{2,1,0:T(8,128)S(1)} %payload.1), channel_id=1, source_target_pairs={{1,2},{2,1},{3,4},{4,3},{5,6},{6,5},{9,10},{10,9},{11,12},{12,11},... | collective-permute-start | bytes 282632 | tf_op jit(solution)/shard_map/ppermute | solution.py:675
  28.8 0.7 copy-start.9
  30.1 0.6 copy-start.14
  30.8 0.7 copy-start.10
  33.6 21.5 %copy-start.13 = (f32[8,32]{1,0:T(8,128)S(1)}, f32[8,32]{1,0:T(8,128)}, u32[]{:S(2)}) copy-start(f32[8,32]{1,0:T(8,128)} %pad_slice_fusion.1) | copy-start | bytes 3076
  34.3 20.8 %copy-start.11 = (f32[10,32]{1,0:T(8,128)S(1)}, f32[10,32]{1,0:T(8,128)}, u32[]{:S(2)}) copy-start(f32[10,32]{1,0:T(8,128)} %copy-done.10) | copy-start | bytes 3844
  34.3 20.8 %copy-start.12 = (f32[16,24]{1,0:T(8,128)S(1)}, f32[16,24]{1,0:T(8,128)}, u32[]{:S(2)}) copy-start(f32[16,24]{1,0:T(8,128)} %slice_select_fusion) | copy-start | bytes 4612
  34.3 20.7 %collective-permute-start.6 = (f32[10,8,128]{2,1,0:T(8,128)S(1)}, f32[10,8,128]{2,1,0:T(8,128)S(1)}, u32[]{:S(2)}, u32[]{:S(2)}) collective-permute-start(f32[10,8,128]{2,1,0:T(8,128)S(1)} %get-tuple-element.42), channel_id=1, source_target_pairs={{4,499},{12,507},{499,4},{507,12}} | collective-permute-start | bytes 122888 | tf_op jit(solution)/shard_map/ppermute | solution.py:693
  35.0 22.0 %collective-permute-start.4 = (f32[20,8,128]{2,1,0:T(8,128)S(1)}, f32[20,8,128]{2,1,0:T(8,128)S(1)}, u32[]{:S(2)}, u32[]{:S(2)}) collective-permute-start(f32[20,8,128]{2,1,0:T(8,128)S(1)} %get-tuple-element.40), channel_id=1, source_target_pairs={{0,505},{1,504},{2,507},{3,506},{4,509},{5,508},{6,511},{7,510},{5... | collective-permute-start | bytes 245768 | tf_op jit(solution)/shard_map/ppermute | solution.py:691
  37.1 21.8 %collective-permute-start.5 = (f32[20,8,128]{2,1,0:T(8,128)S(1)}, f32[20,8,128]{2,1,0:T(8,128)S(1)}, u32[]{:S(2)}, u32[]{:S(2)}) collective-permute-start(f32[20,8,128]{2,1,0:T(8,128)S(1)} %get-tuple-element.41.face), channel_id=1, source_target_pairs={{1,506},{2,505},{3,508},{4,507},{5,510},{6,509},{505,2},{506,1},{5... | collective-permute-start | bytes 245768 | tf_op jit(solution)/shard_map/ppermute | solution.py:692
  55.1 10.0 %collective-permute-start.1 = (f32[2,5,72,128]{3,2,1,0:T(8,128)}, f32[2,5,72,128]{3,2,1,0:T(8,128)S(1)}, u32[]{:S(2)}, u32[]{:S(2)}) collective-permute-start(f32[2,5,72,128]{3,2,1,0:T(8,128)} %copy-done.9), channel_id=1, source_target_pairs={{0,8},{8,0},{16,24},{24,16},{32,40},{40,32},{48,56},{56,48},{64,72... | collective-permute-start | bytes 1105928 | tf_op jit(solution)/shard_map/ppermute | solution.py:690
  57.0 17.5 %collective-permute-start.2 = (f32[2,5,72,128]{3,2,1,0:T(8,128)S(1)}, f32[2,5,72,128]{3,2,1,0:T(8,128)S(1)}, u32[]{:S(2)}, u32[]{:S(2)}) collective-permute-start(f32[2,5,72,128]{3,2,1,0:T(8,128)S(1)} %get-tuple-element.34), channel_id=1, source_target_pairs={{0,504},{8,16},{16,8},{24,32},{32,24},{40,48},{48,40},{56,64},{64,... | collective-permute-start | bytes 1105928 | tf_op jit(solution)/shard_map/ppermute | solution.py:689
  59.0 18.9 %collective-permute-start.9 = (f32[40,8,128]{2,1,0:T(8,128)S(1)}, f32[40,8,128]{2,1,0:T(8,128)S(1)}, u32[]{:S(2)}, u32[]{:S(2)}) collective-permute-start(f32[40,8,128]{2,1,0:T(8,128)S(1)} %pad_maximum_fusion), channel_id=1, source_target_pairs={{8,16},{16,8},{24,32},{32,24},{40,48},{48,40},{56,64},{64,56},{72,... | collective-permute-start | bytes 491528 | tf_op jit(solution)/shard_map/ppermute | solution.py:701
  59.7 18.2 %collective-permute-start.8 = (f32[40,8,128]{2,1,0:T(8,128)S(1)}, f32[40,8,128]{2,1,0:T(8,128)S(1)}, u32[]{:S(2)}, u32[]{:S(2)}) collective-permute-start(f32[40,8,128]{2,1,0:T(8,128)S(1)} %pad_maximum_fusion), channel_id=1, source_target_pairs={{0,8},{8,0},{16,24},{24,16},{32,40},{40,32},{48,56},{56,48},{64,72... | collective-permute-start | bytes 491528 | tf_op jit(solution)/shard_map/ppermute | solution.py:700

commit v6 on v4

--- a/solution.py
+++ b/solution.py
@@ -57,104 +57,6 @@
             scaled = matrix[at] * term
             part = scaled if part is None else part + scaled
         totals[g] = part if totals[g] is None else totals[g] + part
-
-
-def axial_term(v, low_end, high_end, rates):
-    axial_low, axial_high = rates[2:4]
-    count = v.shape[0]
-    row = lax.broadcasted_iota(jnp.int32, v.shape, 0)
-    lower = jnp.where(row == 0, low_end, pltpu.roll(v, 1, 0))
-    upper = jnp.where(row == count - 1, high_end, pltpu.roll(v, count - 1, 0))
-    return axial_low * lower + axial_high * upper - (axial_low + axial_high) * v
-
-
-def theta_term(prior, v, later, rates):
-    theta_low, theta_high = rates[:2]
-    return theta_low * prior + theta_high * later - (theta_low + theta_high) * v
-
-
-def axial_term(v, low_end, high_end, rates):
-    axial_low, axial_high = rates[2:4]
-    count = v.shape[0]
-    row = lax.broadcasted_iota(jnp.int32, v.shape, 0)
-    lower = jnp.where(row == 0, low_end, pltpu.roll(v, 1, 0))
-    upper = jnp.where(row == count - 1, high_end, pltpu.roll(v, count - 1, 0))
-    return axial_low * lower + axial_high * upper - (axial_low + axial_high) * v
-
-
-def theta_term(prior, v, later, rates):
-    theta_low, theta_high = rates[:2]
-    return theta_low * prior + theta_high * later - (theta_low + theta_high) * v
-
-
-def axial_term(v, low_end, high_end, rates):
-    axial_low, axial_high = rates[2:4]
-    count = v.shape[0]
-    row = lax.broadcasted_iota(jnp.int32, v.shape, 0)
-    lower = jnp.where(row == 0, low_end, pltpu.roll(v, 1, 0))
-    upper = jnp.where(row == count - 1, high_end, pltpu.roll(v, count - 1, 0))
-    return axial_low * lower + axial_high * upper - (axial_low + axial_high) * v
-
-
-def theta_term(prior, v, later, rates):
-    theta_low, theta_high = rates[:2]
-    return theta_low * prior + theta_high * later - (theta_low + theta_high) * v
-
-
-def axial_term(v, low_end, high_end, rates):
-    axial_low, axial_high = rates[2:4]
-    count = v.shape[0]
-    row = lax.broadcasted_iota(jnp.int32, v.shape, 0)
-    lower = jnp.where(row == 0, low_end, pltpu.roll(v, 1, 0))
-    upper = jnp.where(row == count - 1, high_end, pltpu.roll(v, count - 1, 0))
-    return axial_low * lower + axial_high * upper - (axial_low + axial_high) * v
-
-
-def theta_term(prior, v, later, rates):
-    theta_low, theta_high = rates[:2]
-    return theta_low * prior + theta_high * later - (theta_low + theta_high) * v
-
-
-def axial_term(v, low_end, high_end, rates):
-    axial_low, axial_high = rates[2:4]
-    count = v.shape[0]
-    row = lax.broadcasted_iota(jnp.int32, v.shape, 0)
-    lower = jnp.where(row == 0, low_end, pltpu.roll(v, 1, 0))
-    upper = jnp.where(row == count - 1, high_end, pltpu.roll(v, count - 1, 0))
-    return axial_low * lower + axial_high * upper - (axial_low + axial_high) * v
-
-
-def theta_term(prior, v, later, rates):
-    theta_low, theta_high = rates[:2]
-    return theta_low * prior + theta_high * later - (theta_low + theta_high) * v
-
-
-def axial_term(v, low_end, high_end, rates):
-    axial_low, axial_high = rates[2:4]
-    count = v.shape[0]
-    row = lax.broadcasted_iota(jnp.int32, v.shape, 0)
-    lower = jnp.where(row == 0, low_end, pltpu.roll(v, 1, 0))
-    upper = jnp.where(row == count - 1, high_end, pltpu.roll(v, count - 1, 0))
-    return axial_low * lower + axial_high * upper - (axial_low + axial_high) * v
-
-
-def theta_term(prior, v, later, rates):
-    theta_low, theta_high = rates[:2]
-    return theta_low * prior + theta_high * later - (theta_low + theta_high) * v
-
-
-def axial_term(v, low_end, high_end, rates):
-    axial_low, axial_high = rates[2:4]
-    count = v.shape[0]
-    row = lax.broadcasted_iota(jnp.int32, v.shape, 0)
-    lower = jnp.where(row == 0, low_end, pltpu.roll(v, 1, 0))
-    upper = jnp.where(row == count - 1, high_end, pltpu.roll(v, count - 1, 0))
-    return axial_low * lower + axial_high * upper - (axial_low + axial_high) * v
-
-
-def theta_term(prior, v, later, rates):
-    theta_low, theta_high = rates[:2]
-    return theta_low * prior + theta_high * later - (theta_low + theta_high) * v
 
 
 def axial_term(v, low_end, high_end, rates):
@@ -233,7 +135,7 @@
     operator(adjoint, identity, reverse_rates, mixers, True, rows, sensitivity_at)
 
 
-def pack_axial_kernel(place, flow, cotangent, xsend, farsend):
+def pack_axial_kernel(place, flow, cotangent, xsend):
     fields, columns, layers, _ = flow.shape
     half = place[HALF]
     for n, source in enumerate((flow, cotangent)):
@@ -243,10 +145,7 @@
                 for depth in range(2):
                     low = source[f, t, depth : depth + 1, :]
                     high = source[f, t, layers - 1 - depth : layers - depth, :]
-                    value = jnp.where(half == 1, high, low)
-                    xsend[depth, n, f, rows, :] = value
-                    if depth == 0:
-                        farsend[n, f, rows, :] = value
+                    xsend[depth, n, f, rows, :] = jnp.where(half == 1, high, low)
 
 
 def pack_column(place, n, f, source, first, send):
@@ -262,7 +161,7 @@
         send[n, f, rows, :] = jnp.where(pick == 1, high, low)
 
 
-def pack_own_kernel(place, flow, cotangent, own, send_wrap):
+def pack_own_kernel(place, flow, cotangent, own, send_wrap, farsend):
     fields, columns, layers, _ = flow.shape
     half, even = place[HALF], place[EVEN]
     first = jnp.where(even == 1, 0, columns - 1)
@@ -274,6 +173,8 @@
                     low = source[f, t, depth : depth + 1, :]
                     high = source[f, t, layers - 1 - depth : layers - depth, :]
                     own[depth, n, f, t : t + 1, :] = jnp.where(half == 1, low, high)
+                    if depth == 0:
+                        farsend[n, f, t : t + 1, :] = jnp.where(half == 1, high, low)
 
 
 def pack_columns(place, flow, cotangent, send_a, send_b):
@@ -413,7 +314,7 @@
 
 
 def last_kernel(
-    place, mix_t, mix_a, mix_r, flow, cotangent, section, adjoint, ends, faces, pass_a, pass_b, far,
+    place, mix_t, mix_a, mix_r, flow, cotangent, section, adjoint, ends, faces, pass_a, pass_b, pass_wrap, far,
     got_a, got_b, got_wrap, weights, advanced_inner, sensitivity_inner, advanced_outer, sensitivity_outer,
     advanced, sensitivity,
     far_one, far_two, near, virtual, beyond, ends_two, tiles, section_ends,
@@ -450,13 +351,13 @@
             for f in range(fields):
                 lane = lanes[n][f]
                 k = spot(side, 0, n, f)
-                prior, later = prior_later(pass_a[k], pass_b[k])
+                prior, later = prior_later(pass_a[k], pass_b[k] + pass_wrap[k])
                 far_one[side, sector_rows(at_own), lane] = shaped(faces[k])
                 far_one[side, sector_rows(at_prior), lane] = shaped(prior)
                 far_one[side, sector_rows(at_later), lane] = shaped(later)
                 far_one[side, sector_rows(at_far), lane] = shaped(far[n, f])
                 k = spot(side, 1, n, f)
-                beside = prior_later(pass_a[k], pass_b[k])[side]
+                beside = prior_later(pass_a[k], pass_b[k] + pass_wrap[k])[side]
                 far_two[side, sector_rows(at_own - 1), lane] = shaped(faces[k])
                 far_two[side, sector_rows(2 - at_own), lane] = shaped(beside)
                 rows = slice(2 * layers, 2 * layers + columns)
@@ -499,7 +400,7 @@
             values.append(totals)
         for g in range(fields):
             k = spot(side, 0, 0, g)
-            parts = [faces[k], prior_later(pass_a[k], pass_b[k])[side]]
+            parts = [faces[k], prior_later(pass_a[k], pass_b[k] + pass_wrap[k])[side]]
             one = jnp.concatenate(parts if side else parts[::-1], axis=0) + time_step * values[0][g]
             reach_far = far_one[side, columns : columns + two, lanes[1][g]]
             beyond[side, :, lanes[0][g]] = shaping(one)
@@ -604,9 +505,7 @@
     pairs_near = [(i, j) for i, j in pairs_b if abs(i - j) == 1]
     pairs_x = [(b, b - 2) for b in range(2, n_block, 2)] + [(b, b + 2) for b in range(1, n_block - 2, 2)]
     pairs_long = [(b, b ^ 1) for b in blocks]
-    pairs_pass = [
-        (at(i, b), at(j, b ^ 1 if abs(i - j) > 1 else b)) for i, j in pairs_b for b in blocks
-    ]
+    pairs_pass = [(at(i, b), at(j, b ^ 1)) for i, j in pairs_wrap for b in blocks]
     pairs_far = []
     for s in sectors:
         inside = s + 2 < n_sector
@@ -614,7 +513,6 @@
         inside = s >= 2
         pairs_far.append((at(s, middle), at((s - 2) % n_sector, middle - 2 if inside else middle - 1)))
 
-    wrap = (sector == 0) | (sector == n_sector - 1)
     place = jnp.stack(
         [
             block % 2,
@@ -639,15 +537,12 @@
     far_face = shape(2, fields, columns, radii)
     work = 4 * 5 * 5 * 3 * columns * layers * radii
 
-    xsend, farsend = call(
-        pack_axial_kernel,
-        (place, flow_state, cotangent),
-        [face, far_face],
-        name="pack_axial",
-    )
+    (xsend,) = call(pack_axial_kernel, (place, flow_state, cotangent), [face], name="pack_axial")
     arrived = lax.ppermute(xsend, "block", pairs_x)
+    own, send_wrap, farsend = call(
+        pack_own_kernel, (place, flow_state, cotangent), [face, side, far_face], name="pack_own"
+    )
     far = lax.ppermute(farsend, ("azim", "block"), pairs_far)
-    own, send_wrap = call(pack_own_kernel, (place, flow_state, cotangent), [face, side], name="pack_own")
     got_wrap = lax.ppermute(send_wrap, "azim", pairs_wrap)
     (payload,) = call(
         payload_kernel,
@@ -666,13 +561,16 @@
         flops=20 * work,
         name="inner",
     )
-    send_a, slots, codes = lax.optimization_barrier((send_a, intersection_slot, intersection_code))
+    send_a, payload, slots, codes = lax.optimization_barrier(
+        (send_a, payload, intersection_slot, intersection_code)
+    )
+    pass_wrap = lax.ppermute(payload, ("azim", "block"), pairs_pass)
     weights = interface_weights(slots, codes, columns, sector, block, n_block)
     got_a = lax.ppermute(send_a, "azim", pairs_a)
     got_b = lax.ppermute(send_b, "azim", pairs_near)
-    faces, section, weights = lax.optimization_barrier((faces, section, weights))
+    faces, section, weights, pass_wrap = lax.optimization_barrier((faces, section, weights, pass_wrap))
     pass_a = lax.ppermute(faces, "azim", pairs_a)
-    pass_b = lax.ppermute(jnp.where(wrap, payload, faces), ("azim", "block"), pairs_pass)
+    pass_b = lax.ppermute(faces, "azim", pairs_near)
     section, adjoint, ends, advanced_outer, sensitivity_outer = call(
         outer_kernel,
         (place, *mixers, flow_state, cotangent, got_a, got_b, got_wrap, section, adjoint, reverse_ends),
@@ -685,7 +583,7 @@
     return tuple(
         call(
             last_kernel,
-            (place, *mixers, flow_state, cotangent, section, adjoint, ends, faces, pass_a, pass_b, far)
+            (place, *mixers, flow_state, cotangent, section, adjoint, ends, faces, pass_a, pass_b, pass_wrap, far)
             + (got_a, got_b, got_wrap, weights)
             + (advanced_inner, sensitivity_inner, advanced_outer, sensitivity_outer),
             [whole, whole],

time: 66.5 us -> 69.2 us (1.041)
  the two profiles are of different devices: /device:TPU:1 before, /device:TPU:5 now
where the time goes in v6:
time: 69.2 us; the launch traced here: 68.8 us
  starting transfers between devices  46 us (66%)
  Pallas kernels  14.8 us (21%)
  local copies, waits for them, and re-layouts  4.45 us (6%)
  waiting for transfers between devices  2.08 us (3%)
  between operations  0.96 us (1%)
    ppermute x1, starting transfers between devices, shards(): got_a = lax.ppermute(send_a, 'azim', pairs_a)  18 us
    pallas_call x6, Pallas kernels, call(): pl.pallas_call(kernel, out_shape=outs, in_specs=[SMEM if small(x) else VM...  14.8 us
    ppermute x1, starting transfers between devices, shards(): far = lax.ppermute(farsend, ('azim', 'block'), pairs_far)  14.5 us
    unnamed x24, local copies, waits for them, and re-layouts  3.9 us
    ppermute x1, starting transfers between devices, shards(): pass_b = lax.ppermute(faces, 'azim', pairs_near)  3.64 us
    ppermute x1, starting transfers between devices, shards(): faces = lax.ppermute(payload, 'block', pairs_long)  2.37 us
    ppermute x1, starting transfers between devices, shards(): arrived = lax.ppermute(xsend, 'block', pairs_x)  2.29 us
    ppermute x1, starting transfers between devices, shards(): pass_a = lax.ppermute(faces, 'azim', pairs_a)  1.92 us
  transfers between devices with their start and end apart: 9, of which 2 were waited for; matrix products, arithmetic and copies ran while one was open for 2% of the time, Pallas kernels for 14%

profile of v6, /device:TPU:5, one launch (start us, length us, event | category | flops | bytes accessed | tf_op | source)
XLA Modules:
  0.0 68.8 jit_solution(16491625370115105945)
XLA Ops:
  0.7 0.1 stack.48.place
  0.7 0.0 copy-start
  0.7 1.1 %copy-done = f32[5,8,32,128]{3,2,1,0:T(8,128)S(1)} copy-done((f32[5,8,32,128]{3,2,1,0:T(8,128)S(1)}, f32[5,8,32,128]{3,2,1,0:T(8,128)}, u32[]{:S(2)}) %copy-start) | copy-done | bytes 655384
  1.8 0.0 copy-start.2
  1.8 1.1 %copy-done.2 = f32[5,8,32,128]{3,2,1,0:T(8,128)S(1)} copy-done((f32[5,8,32,128]{3,2,1,0:T(8,128)S(1)}, f32[5,8,32,128]{3,2,1,0:T(8,128)}, u32[]{:S(2)}) %copy-start.2) | copy-done | bytes 655384
  2.9 0.6 pack_axial.1
  3.6 0.0 copy-start.1
  3.6 0.0 copy-start.3
  3.6 2.3 %collective-permute-start = (f32[2,2,5,8,128]{4,3,2,1,0:T(8,128)S(1)}, f32[2,2,5,8,128]{4,3,2,1,0:T(8,128)S(1)}, u32[]{:S(2)}, u32[]{:S(2)}) collective-permute-start(f32[2,2,5,8,128]{4,3,2,1,0:T(8,128)S(1)} %pack_axial.1), channel_id=1, source_target_pairs={{2,0},{4,2},{6,4},{1,3},{3,5},{5,7},{10,8},{12,10},{14,12},{9,11},... | collective-permute-start | bytes 245768 | tf_op jit(solution)/shard_map/ppermute | solution.py:541
  5.9 1.4 %pack_own.1 = (f32[2,2,5,8,128]{4,3,2,1,0:T(8,128)S(1)}, f32[2,5,72,128]{3,2,1,0:T(8,128)}, f32[2,5,8,128]{3,2,1,0:T(8,128)S(1)}) custom-call(s32[6]{0:T(128)S(1)} %stack.48.place, f32[5,8,32,128]{3,2,1,0:T(8,128)S(1)} %copy-done, f32[5,8,32,128]{3,2,1,0:T(8,128)S(1)} %copy-done.2), custom_call_target="tpu_custom_call" | custom-call | bytes 1802264 | tf_op jit(solution)/shard_map/pack_own/pallas_call | solution.py:31
  7.3 14.5 %collective-permute-start.1 = (f32[2,5,8,128]{3,2,1,0:T(8,128)S(1)}, f32[2,5,8,128]{3,2,1,0:T(8,128)S(1)}, u32[]{:S(2)}, u32[]{:S(2)}) collective-permute-start(f32[2,5,8,128]{3,2,1,0:T(8,128)S(1)} %get-tuple-element.28), channel_id=1, source_target_pairs={{3,21},{4,499},{11,29},{12,507},{19,37},{20,2},{27,45},{28,10},{35... | collective-permute-start | bytes 122888 | tf_op jit(solution)/shard_map/ppermute | solution.py:545
  21.8 0.7 collective-permute-start.4
  22.6 0.0 copy-start.5
  22.6 0.0 copy-start.4
  22.6 0.6 collective-permute-done.1.far
  23.2 0.0 collective-permute-done.arrived
  23.2 0.1 copy-done.5
  23.3 0.0 copy-done.4
  23.3 0.0 copy-start.6
  23.3 0.0 copy-start.7
  23.3 0.0 copy-start.8
  23.3 0.8 %payload.1 = f32[43,8,128]{2,1,0:T(8,128)S(1)} custom-call(s32[6]{0:T(128)S(1)} %stack.48.place, s32[3,512]{1,0:T(4,128)S(1)} %bitcast.19, s32[3,512]{1,0:T(4,128)S(1)} %bitcast.18, f32[2,2,5,8,128]{4,3,2,1,0:T(8,128)S(1)} %collective-permute-done.arrived, f32[2,2,5,8,128]{4,3,2,1,0:T(8,128)S(1)} %get-tuple-element.27.own, ...), custom_call_target="tpu_custom_call" | custom-call | bytes 393240 | tf_op jit(solution)/shard_map/payload/pallas_call | solution.py:31
  24.1 2.4 %collective-permute-start.5 = (f32[43,8,128]{2,1,0:T(8,128)S(1)}, f32[43,8,128]{2,1,0:T(8,128)S(1)}, u32[]{:S(2)}, u32[]{:S(2)}) collective-permute-start(f32[43,8,128]{2,1,0:T(8,128)S(1)} %payload.1), channel_id=1, source_target_pairs={{0,1},{1,0},{2,3},{3,2},{4,5},{5,4},{6,7},{7,6},{8,9},{9,8},{10,11... | collective-permute-start | bytes 528392 | tf_op jit(solution)/shard_map/ppermute | solution.py:553
  26.5 0.0 copy-done.1
  26.5 0.0 copy-done.3
  26.5 0.0 copy-done.6
  26.5 0.0 copy-done.7
  26.5 0.0 copy-done.8
  26.5 4.0 %inner.1 = (f32[5,6,32,128]{3,2,1,0:T(8,128)S(1)}, f32[5,6,32,128]{3,2,1,0:T(8,128)S(1)}, f32[2,5,8,128]{3,2,1,0:T(8,128)S(1)}, f32[5,4,16,128]{3,2,1,0:T(8,128)...) custom-call(s32[6]{0:T(128)S(1)} %stack.48.place, ...), custom_call_target="tpu_custom_call" | custom-call | flops 196608000 | bytes 3400004 | tf_op jit(solution)/shard_map/inner/pallas_call | solution.py:31
  30.5 0.0 copy-start.9
  30.5 0.7 %copy-done.9 = f32[2,5,72,128]{3,2,1,0:T(8,128)} copy-done((f32[2,5,72,128]{3,2,1,0:T(8,128)}, f32[2,5,72,128]{3,2,1,0:T(8,128)S(1)}, u32[]{:S(2)}) %copy-start.9) | copy-done | bytes 368664
  31.2 0.0 copy-start.10
  31.2 0.7 %copy-done.10 = f32[2,5,72,128]{3,2,1,0:T(8,128)} copy-done((f32[2,5,72,128]{3,2,1,0:T(8,128)}, f32[2,5,72,128]{3,2,1,0:T(8,128)S(1)}, u32[]{:S(2)}) %copy-start.10) | copy-done | bytes 368664
  32.0 0.1 slice.36
  32.1 0.1 slice.38
  32.1 0.1 fusion.14
  32.2 0.1 fusion.13
  32.3 0.1 select_reduce_fusion
  32.4 0.1 slice.49
  32.5 0.1 slice.51
  32.6 0.1 fusion.5
  32.6 0.1 slice.50
  32.7 0.1 copy.15
  32.8 0.1 copy.16
  32.9 0.1 slice_select_fusion
  32.9 0.1 fusion.6
  33.0 0.1 slice.53
  33.1 0.7 collective-permute-start.6
  33.8 18.0 %collective-permute-start.2 = (f32[2,5,72,128]{3,2,1,0:T(8,128)}, f32[2,5,72,128]{3,2,1,0:T(8,128)S(1)}, u32[]{:S(2)}, u32[]{:S(2)}) collective-permute-start(f32[2,5,72,128]{3,2,1,0:T(8,128)} %copy-done.10), channel_id=1, source_target_pairs={{0,8},{8,0},{16,24},{24,16},{32,40},{40,32},{48,56},{56,48},{64,72... | collective-permute-start | bytes 1105928 | tf_op jit(solution)/shard_map/ppermute | solution.py:569
  51.8 1.9 %collective-permute-start.3 = (f32[2,5,72,128]{3,2,1,0:T(8,128)}, f32[2,5,72,128]{3,2,1,0:T(8,128)S(1)}, u32[]{:S(2)}, u32[]{:S(2)}) collective-permute-start(f32[2,5,72,128]{3,2,1,0:T(8,128)} %copy-done.9), channel_id=1, source_target_pairs={{8,16},{16,8},{24,32},{32,24},{40,48},{48,40},{56,64},{64,56},{72,... | collective-permute-start | bytes 1105928 | tf_op jit(solution)/shard_map/ppermute | solution.py:570
  53.7 0.0 collective-permute-done.5.faces
  53.8 0.0 collective-permute-done.6.pass_wrap
  53.8 3.6 %collective-permute-start.8 = (f32[43,8,128]{2,1,0:T(8,128)S(1)}, f32[43,8,128]{2,1,0:T(8,128)S(1)}, u32[]{:S(2)}, u32[]{:S(2)}) collective-permute-start(f32[43,8,128]{2,1,0:T(8,128)S(1)} %collective-permute-done.5.faces), channel_id=1, source_target_pairs={{8,16},{16,8},{24,32},{32,24},{40,48},{48,40},{56,64},{64,56},{72,... | collective-permute-start | bytes 528392 | tf_op jit(solution)/shard_map/ppermute | solution.py:573
  57.4 1.9 %collective-permute-start.7 = (f32[43,8,128]{2,1,0:T(8,128)S(1)}, f32[43,8,128]{2,1,0:T(8,128)S(1)}, u32[]{:S(2)}, u32[]{:S(2)}) collective-permute-start(f32[43,8,128]{2,1,0:T(8,128)S(1)} %collective-permute-done.5.faces), channel_id=1, source_target_pairs={{0,8},{8,0},{16,24},{24,16},{32,40},{40,32},{48,56},{56,48},{64,72... | collective-permute-start | bytes 528392 | tf_op jit(solution)/shard_map/ppermute | solution.py:572
  59.3 0.0 collective-permute-done.4.got_wrap
  59.3 0.0 collective-permute-done.2.got_a
  59.4 1.5 %collective-permute-done.3.got_b = f32[2,5,72,128]{3,2,1,0:T(8,128)S(1)} collective-permute-done((f32[2,5,72,128]{3,2,1,0:T(8,128)}, f32[2,5,72,128]{3,2,1,0:T(8,128)S(1)}, u32[]{:S(2)}, u32[]{:S(2)}) %collective-permute-start.3) | collective-permute-done | bytes 368672 | tf_op jit(solution)/shard_map/ppermute | solution.py:570
  60.8 3.4 %outer.1 = (f32[5,10,32,128]{3,2,1,0:T(8,128)S(1)}, f32[5,10,32,128]{3,2,1,0:T(8,128)S(1)}, f32[2,3,5,16,128]{4,3,2,1,0:T(8,128)S(1)}, f32[5,4,16,128]{3,2,1,0:T(8,128)S(1)}, f32[5,4,16,128]{3,2,1,0:T(8,128)S(1)}) custom-call(s32[6]{0:T(128)S(1)} %stack.48.place, f32[5,5]{1,0:T(8,128)S(1)} %copy-done.6, f32[5,5]{1,0:T(8,128)S(1)} %copy-done.7, ...), custom_call_target="tpu_custom_call" | custom-call | bytes 5652804 | tf_op jit(solution)/shard_map/outer/pallas_call | solution.py:31
  64.2 0.0 collective-permute-done.8.pass_b
  64.2 0.0 collective-permute-done.7.pass_a
  64.2 4.6 %last.1 = (f32[5,8,32,128]{3,2,1,0:T(8,128)}, f32[5,8,32,128]{3,2,1,0:T(8,128)}) custom-call(s32[6]{0:T(128)S(1)} %stack.48.place, f32[5,5]{1,0:T(8,128)S(1)} %copy-done.6, f32[5,5]{1,0:T(8,128)S(1)} %copy-done.7, f32[5,5]{1,0:T(8,128)S(1)} %copy-done.8, f32[5,8,32,128]{3,2,1,0:T(8,128)S(1)} %copy-done.1, f32[5,8,32,128]{3,2,1,0:T(8,128)S(1)} %copy-done.3, ...), custom_call_target="tpu_custom_call" | custom-call | bytes 7022916 | tf_op jit(solution)/shard_map/last/pallas_call | solution.py:31
  (11 shorter events, 0.1 us)
Async XLA Ops:
  0.7 1.1 %copy-start = (f32[5,8,32,128]{3,2,1,0:T(8,128)S(1)}, f32[5,8,32,128]{3,2,1,0:T(8,128)}, u32[]{:S(2)}) copy-start(f32[5,8,32,128]{3,2,1,0:T(8,128)} %flow.9) | copy-start | bytes 1966084
  1.8 1.1 %copy-start.2 = (f32[5,8,32,128]{3,2,1,0:T(8,128)S(1)}, f32[5,8,32,128]{3,2,1,0:T(8,128)}, u32[]{:S(2)}) copy-start(f32[5,8,32,128]{3,2,1,0:T(8,128)} %cotangent.9) | copy-start | bytes 1966084
  3.6 22.9 %copy-start.1 = (f32[5,8,32,128]{3,2,1,0:T(8,128)S(1)}, f32[5,8,32,128]{3,2,1,0:T(8,128)}, u32[]{:S(2)}) copy-start(f32[5,8,32,128]{3,2,1,0:T(8,128)} %flow.9) | copy-start | bytes 1966084
  3.6 22.9 %copy-start.3 = (f32[5,8,32,128]{3,2,1,0:T(8,128)S(1)}, f32[5,8,32,128]{3,2,1,0:T(8,128)}, u32[]{:S(2)}) copy-start(f32[5,8,32,128]{3,2,1,0:T(8,128)} %cotangent.9) | copy-start | bytes 1966084
  3.6 19.6 %collective-permute-start = (f32[2,2,5,8,128]{4,3,2,1,0:T(8,128)S(1)}, f32[2,2,5,8,128]{4,3,2,1,0:T(8,128)S(1)}, u32[]{:S(2)}, u32[]{:S(2)}) collective-permute-start(f32[2,2,5,8,128]{4,3,2,1,0:T(8,128)S(1)} %pack_axial.1), channel_id=1, source_target_pairs={{2,0},{4,2},{6,4},{1,3},{3,5},{5,7},{10,8},{12,10},{14,12},{9,11},... | collective-permute-start | bytes 245768 | tf_op jit(solution)/shard_map/ppermute | solution.py:541
  7.3 15.9 %collective-permute-start.1 = (f32[2,5,8,128]{3,2,1,0:T(8,128)S(1)}, f32[2,5,8,128]{3,2,1,0:T(8,128)S(1)}, u32[]{:S(2)}, u32[]{:S(2)}) collective-permute-start(f32[2,5,8,128]{3,2,1,0:T(8,128)S(1)} %get-tuple-element.28), channel_id=1, source_target_pairs={{3,21},{4,499},{11,29},{12,507},{19,37},{20,2},{27,45},{28,10},{35... | collective-permute-start | bytes 122888 | tf_op jit(solution)/shard_map/ppermute | solution.py:545
  21.8 37.5 %collective-permute-start.4 = (f32[2,5,72,128]{3,2,1,0:T(8,128)}, f32[2,5,72,128]{3,2,1,0:T(8,128)S(1)}, u32[]{:S(2)}, u32[]{:S(2)}) collective-permute-start(f32[2,5,72,128]{3,2,1,0:T(8,128)} %get-tuple-element.34), channel_id=1, source_target_pairs={{0,504},{504,0},{1,505},{505,1},{2,506},{506,2},{3,507},{507,3},{4... | collective-permute-start | bytes 1105928 | tf_op jit(solution)/shard_map/ppermute | solution.py:546
  22.6 0.7 %copy-start.5 = (s32[512,3]{0,1:T(4,128)S(1)}, s32[512,3]{0,1:T(4,128)}, u32[]{:S(2)}) copy-start(s32[512,3]{0,1:T(4,128)} %param.12) | copy-start | bytes 18436
  22.6 0.7 %copy-start.4 = (s32[512,3]{0,1:T(4,128)S(1)}, s32[512,3]{0,1:T(4,128)}, u32[]{:S(2)}) copy-start(s32[512,3]{0,1:T(4,128)} %param.13) | copy-start | bytes 18436
  23.3 3.2 %copy-start.6 = (f32[5,5]{1,0:T(8,128)S(1)}, f32[5,5]{1,0:T(8,128)}, u32[]{:S(2)}) copy-start(f32[5,5]{1,0:T(8,128)} %mix_t.5) | copy-start | bytes 304
  23.3 3.3 %copy-start.7 = (f32[5,5]{1,0:T(8,128)S(1)}, f32[5,5]{1,0:T(8,128)}, u32[]{:S(2)}) copy-start(f32[5,5]{1,0:T(8,128)} %mix_a.5) | copy-start | bytes 304
  23.3 3.3 %copy-start.8 = (f32[5,5]{1,0:T(8,128)S(1)}, f32[5,5]{1,0:T(8,128)}, u32[]{:S(2)}) copy-start(f32[5,5]{1,0:T(8,128)} %mix_r.5) | copy-start | bytes 304
  24.1 29.6 %collective-permute-start.5 = (f32[43,8,128]{2,1,0:T(8,128)S(1)}, f32[43,8,128]{2,1,0:T(8,128)S(1)}, u32[]{:S(2)}, u32[]{:S(2)}) collective-permute-start(f32[43,8,128]{2,1,0:T(8,128)S(1)} %payload.1), channel_id=1, source_target_pairs={{0,1},{1,0},{2,3},{3,2},{4,5},{5,4},{6,7},{7,6},{8,9},{9,8},{10,11... | collective-permute-start | bytes 528392 | tf_op jit(solution)/shard_map/ppermute | solution.py:553
  30.5 0.7 %copy-start.9 = (f32[2,5,72,128]{3,2,1,0:T(8,128)}, f32[2,5,72,128]{3,2,1,0:T(8,128)S(1)}, u32[]{:S(2)}) copy-start(f32[2,5,72,128]{3,2,1,0:T(8,128)S(1)} %get-tuple-element.33) | copy-start | bytes 1105924
  31.2 0.7 %copy-start.10 = (f32[2,5,72,128]{3,2,1,0:T(8,128)}, f32[2,5,72,128]{3,2,1,0:T(8,128)S(1)}, u32[]{:S(2)}) copy-start(f32[2,5,72,128]{3,2,1,0:T(8,128)S(1)} %get-tuple-element.32) | copy-start | bytes 1105924
  33.1 20.6 %collective-permute-start.6 = (f32[43,8,128]{2,1,0:T(8,128)S(1)}, f32[43,8,128]{2,1,0:T(8,128)S(1)}, u32[]{:S(2)}, u32[]{:S(2)}) collective-permute-start(f32[43,8,128]{2,1,0:T(8,128)S(1)} %payload.1), channel_id=1, source_target_pairs={{0,505},{1,504},{2,507},{3,506},{4,509},{5,508},{6,511},{7,510},{5... | collective-permute-start | bytes 528392 | tf_op jit(solution)/shard_map/ppermute | solution.py:567
  33.8 25.6 %collective-permute-start.2 = (f32[2,5,72,128]{3,2,1,0:T(8,128)}, f32[2,5,72,128]{3,2,1,0:T(8,128)S(1)}, u32[]{:S(2)}, u32[]{:S(2)}) collective-permute-start(f32[2,5,72,128]{3,2,1,0:T(8,128)} %copy-done.10), channel_id=1, source_target_pairs={{0,8},{8,0},{16,24},{24,16},{32,40},{40,32},{48,56},{56,48},{64,72... | collective-permute-start | bytes 1105928 | tf_op jit(solution)/shard_map/ppermute | solution.py:569
  51.8 9.0 %collective-permute-start.3 = (f32[2,5,72,128]{3,2,1,0:T(8,128)}, f32[2,5,72,128]{3,2,1,0:T(8,128)S(1)}, u32[]{:S(2)}, u32[]{:S(2)}) collective-permute-start(f32[2,5,72,128]{3,2,1,0:T(8,128)} %copy-done.9), channel_id=1, source_target_pairs={{8,16},{16,8},{24,32},{32,24},{40,48},{48,40},{56,64},{64,56},{72,... | collective-permute-start | bytes 1105928 | tf_op jit(solution)/shard_map/ppermute | solution.py:570
  53.8 10.5 %collective-permute-start.8 = (f32[43,8,128]{2,1,0:T(8,128)S(1)}, f32[43,8,128]{2,1,0:T(8,128)S(1)}, u32[]{:S(2)}, u32[]{:S(2)}) collective-permute-start(f32[43,8,128]{2,1,0:T(8,128)S(1)} %collective-permute-done.5.faces), channel_id=1, source_target_pairs={{8,16},{16,8},{24,32},{32,24},{40,48},{48,40},{56,64},{64,56},{72,... | collective-permute-start | bytes 528392 | tf_op jit(solution)/shard_map/ppermute | solution.py:573
  57.4 6.8 %collective-permute-start.7 = (f32[43,8,128]{2,1,0:T(8,128)S(1)}, f32[43,8,128]{2,1,0:T(8,128)S(1)}, u32[]{:S(2)}, u32[]{:S(2)}) collective-permute-start(f32[43,8,128]{2,1,0:T(8,128)S(1)} %collective-permute-done.5.faces), channel_id=1, source_target_pairs={{0,8},{8,0},{16,24},{24,16},{32,40},{40,32},{48,56},{56,48},{64,72... | collective-permute-start | bytes 528392 | tf_op jit(solution)/shard_map/ppermute | solution.py:572

commit v7 on v6

--- a/solution.py
+++ b/solution.py
@@ -506,12 +506,13 @@
     pairs_x = [(b, b - 2) for b in range(2, n_block, 2)] + [(b, b + 2) for b in range(1, n_block - 2, 2)]
     pairs_long = [(b, b ^ 1) for b in blocks]
     pairs_pass = [(at(i, b), at(j, b ^ 1)) for i, j in pairs_wrap for b in blocks]
-    pairs_far = []
+    pairs_far, pairs_far_wrap = [], []
     for s in sectors:
-        inside = s + 2 < n_sector
-        pairs_far.append((at(s, middle - 1), at((s + 2) % n_sector, middle + 1 if inside else middle)))
-        inside = s >= 2
-        pairs_far.append((at(s, middle), at((s - 2) % n_sector, middle - 2 if inside else middle - 1)))
+        for b, shift, relay in ((middle - 1, 2, middle + 1), (middle, -2, middle - 2)):
+            if 0 <= s + shift < n_sector:
+                pairs_far.append((at(s, b), at(s + shift, relay)))
+            else:
+                pairs_far_wrap.append((at(s, b), at((s + shift) % n_sector, n_block - 1 - b)))
 
     place = jnp.stack(
         [
@@ -561,14 +562,17 @@
         flops=20 * work,
         name="inner",
     )
-    send_a, payload, slots, codes = lax.optimization_barrier(
-        (send_a, payload, intersection_slot, intersection_code)
+    send_a, payload, farsend, slots, codes = lax.optimization_barrier(
+        (send_a, payload, farsend, intersection_slot, intersection_code)
     )
     pass_wrap = lax.ppermute(payload, ("azim", "block"), pairs_pass)
+    far_wrap = lax.ppermute(farsend, ("azim", "block"), pairs_far_wrap)
     weights = interface_weights(slots, codes, columns, sector, block, n_block)
     got_a = lax.ppermute(send_a, "azim", pairs_a)
     got_b = lax.ppermute(send_b, "azim", pairs_near)
-    faces, section, weights, pass_wrap = lax.optimization_barrier((faces, section, weights, pass_wrap))
+    faces, section, weights, pass_wrap, far_wrap = lax.optimization_barrier(
+        (faces, section, weights, pass_wrap, far_wrap)
+    )
     pass_a = lax.ppermute(faces, "azim", pairs_a)
     pass_b = lax.ppermute(faces, "azim", pairs_near)
     section, adjoint, ends, advanced_outer, sensitivity_outer = call(
@@ -583,7 +587,7 @@
     return tuple(
         call(
             last_kernel,
-            (place, *mixers, flow_state, cotangent, section, adjoint, ends, faces, pass_a, pass_b, pass_wrap, far)
+            (place, *mixers, flow_state, cotangent, section, adjoint, ends, faces, pass_a, pass_b, pass_wrap, far_wrap)
             + (got_a, got_b, got_wrap, weights)
             + (advanced_inner, sensitivity_inner, advanced_outer, sensitivity_outer),
             [whole, whole],

time: 69.2 us -> 66.3 us (0.958)
  starting transfers between devices: 46 us -> 41.5 us
  waiting for transfers between devices: 2.08 us -> 3.17 us
    ppermute x1, starting transfers between devices: 18 us -> 3.53 us  [shards(): got_a = lax.ppermute(send_a, 'azim', pairs_a)]
    ppermute x1, starting transfers between devices: 2.37 us -> 16.2 us  [shards(): faces = lax.ppermute(payload, 'block', pairs_long)]
    ppermute x1, starting transfers between devices: 14.5 us -> 0.65 us  [shards(): far = lax.ppermute(farsend, ('azim', 'block'), pairs_far)]
    ppermute x0 -> x1, starting transfers between devices: none -> 9.99 us  [shards(): far_wrap = lax.ppermute(farsend, ('azim', 'block'), pairs_far_wrap)]
    ppermute x0 -> x1, waiting for transfers between devices: none -> 1.56 us  [shards(): far_wrap = lax.ppermute(farsend, ('azim', 'block'), pairs_far_wrap)]
  transfers between devices with their start and end apart: 9 -> 10, of which waited for: 2 -> 3; matrix products, arithmetic and copies ran while one was open for 2% -> 2% of each run, Pallas kernels for 14% -> 15%
where the time goes in v7:
time: 66.3 us; the launch traced here: 65.9 us
  starting transfers between devices  41.5 us (63%)
  Pallas kernels  14.8 us (22%)
  local copies, waits for them, and re-layouts  4.91 us (7%)
  waiting for transfers between devices  3.17 us (5%)
  between operations  0.98 us (1%)
    ppermute x1, starting transfers between devices, shards(): faces = lax.ppermute(payload, 'block', pairs_long)  16.2 us
    pallas_call x6, Pallas kernels, call(): pl.pallas_call(kernel, out_shape=outs, in_specs=[SMEM if small(x) else VM...  14.8 us
    ppermute x1, starting transfers between devices, shards(): far_wrap = lax.ppermute(farsend, ('azim', 'block'), pairs_far_wrap)  9.99 us
    unnamed x24, local copies, waits for them, and re-layouts  4.37 us
    ppermute x1, starting transfers between devices, shards(): pass_b = lax.ppermute(faces, 'azim', pairs_near)  3.64 us
    ppermute x1, starting transfers between devices, shards(): got_a = lax.ppermute(send_a, 'azim', pairs_a)  3.53 us
    ppermute x1, starting transfers between devices, shards(): arrived = lax.ppermute(xsend, 'block', pairs_x)  2.29 us
    ppermute x1, starting transfers between devices, shards(): pass_a = lax.ppermute(faces, 'azim', pairs_a)  1.92 us
  transfers between devices with their start and end apart: 10, of which 3 were waited for; matrix products, arithmetic and copies ran while one was open for 2% of the time, Pallas kernels for 15%

profile of v7, /device:TPU:5, one launch (start us, length us, event | category | flops | bytes accessed | tf_op | source)
XLA Modules:
  0.0 65.9 jit_solution(3291762669424061218)
XLA Ops:
  0.7 0.1 stack.48.place
  0.7 0.0 copy-start
  0.7 1.1 %copy-done = f32[5,8,32,128]{3,2,1,0:T(8,128)S(1)} copy-done((f32[5,8,32,128]{3,2,1,0:T(8,128)S(1)}, f32[5,8,32,128]{3,2,1,0:T(8,128)}, u32[]{:S(2)}) %copy-start) | copy-done | bytes 655384
  1.8 0.0 copy-start.2
  1.8 1.1 %copy-done.2 = f32[5,8,32,128]{3,2,1,0:T(8,128)S(1)} copy-done((f32[5,8,32,128]{3,2,1,0:T(8,128)S(1)}, f32[5,8,32,128]{3,2,1,0:T(8,128)}, u32[]{:S(2)}) %copy-start.2) | copy-done | bytes 655384
  2.9 0.6 pack_axial.1
  3.6 0.0 copy-start.1
  3.6 0.0 copy-start.3
  3.6 2.3 %collective-permute-start = (f32[2,2,5,8,128]{4,3,2,1,0:T(8,128)S(1)}, f32[2,2,5,8,128]{4,3,2,1,0:T(8,128)S(1)}, u32[]{:S(2)}, u32[]{:S(2)}) collective-permute-start(f32[2,2,5,8,128]{4,3,2,1,0:T(8,128)S(1)} %pack_axial.1), channel_id=1, source_target_pairs={{2,0},{4,2},{6,4},{1,3},{3,5},{5,7},{10,8},{12,10},{14,12},{9,11},... | collective-permute-start | bytes 245768 | tf_op jit(solution)/shard_map/ppermute | solution.py:542
  5.9 1.4 %pack_own.1 = (f32[2,2,5,8,128]{4,3,2,1,0:T(8,128)S(1)}, f32[2,5,72,128]{3,2,1,0:T(8,128)}, f32[2,5,8,128]{3,2,1,0:T(8,128)S(1)}) custom-call(s32[6]{0:T(128)S(1)} %stack.48.place, f32[5,8,32,128]{3,2,1,0:T(8,128)S(1)} %copy-done, f32[5,8,32,128]{3,2,1,0:T(8,128)S(1)} %copy-done.2), custom_call_target="tpu_custom_call" | custom-call | bytes 1802264 | tf_op jit(solution)/shard_map/pack_own/pallas_call | solution.py:31
  7.3 0.7 collective-permute-start.1
  8.0 0.7 %collective-permute-start.4 = (f32[2,5,72,128]{3,2,1,0:T(8,128)}, f32[2,5,72,128]{3,2,1,0:T(8,128)S(1)}, u32[]{:S(2)}, u32[]{:S(2)}) collective-permute-start(f32[2,5,72,128]{3,2,1,0:T(8,128)} %get-tuple-element.36), channel_id=1, source_target_pairs={{0,504},{504,0},{1,505},{505,1},{2,506},{506,2},{3,507},{507,3},{4... | collective-permute-start | bytes 1105928 | tf_op jit(solution)/shard_map/ppermute | solution.py:547
  8.7 0.0 copy-start.5
  8.7 0.0 copy-start.4
  8.8 0.0 collective-permute-done.1.far
  8.8 0.1 collective-permute-done.arrived
  8.9 0.5 copy-done.5
  9.4 0.0 copy-done.4
  9.4 0.0 copy-start.6
  9.4 0.0 copy-start.7
  9.4 0.0 copy-start.8
  9.4 0.8 %payload.1 = f32[43,8,128]{2,1,0:T(8,128)S(1)} custom-call(s32[6]{0:T(128)S(1)} %stack.48.place, s32[3,512]{1,0:T(4,128)S(1)} %bitcast.19, s32[3,512]{1,0:T(4,128)S(1)} %bitcast.18, f32[2,2,5,8,128]{4,3,2,1,0:T(8,128)S(1)} %collective-permute-done.arrived, f32[2,2,5,8,128]{4,3,2,1,0:T(8,128)S(1)} %get-tuple-element.29.own, ...), custom_call_target="tpu_custom_call" | custom-call | bytes 393240 | tf_op jit(solution)/shard_map/payload/pallas_call | solution.py:31
  10.3 16.2 %collective-permute-start.5 = (f32[43,8,128]{2,1,0:T(8,128)S(1)}, f32[43,8,128]{2,1,0:T(8,128)S(1)}, u32[]{:S(2)}, u32[]{:S(2)}) collective-permute-start(f32[43,8,128]{2,1,0:T(8,128)S(1)} %payload.1), channel_id=1, source_target_pairs={{0,1},{1,0},{2,3},{3,2},{4,5},{5,4},{6,7},{7,6},{8,9},{9,8},{10,11... | collective-permute-start | bytes 528392 | tf_op jit(solution)/shard_map/ppermute | solution.py:554
  26.5 0.0 copy-done.1
  26.5 0.0 copy-done.3
  26.5 0.0 copy-done.6
  26.5 0.0 copy-done.7
  26.5 0.0 copy-done.8
  26.6 4.0 %inner.1 = (f32[5,6,32,128]{3,2,1,0:T(8,128)S(1)}, f32[5,6,32,128]{3,2,1,0:T(8,128)S(1)}, f32[2,5,8,128]{3,2,1,0:T(8,128)S(1)}, f32[5,4,16,128]{3,2,1,0:T(8,128)...) custom-call(s32[6]{0:T(128)S(1)} %stack.48.place, ...), custom_call_target="tpu_custom_call" | custom-call | flops 196608000 | bytes 3400004 | tf_op jit(solution)/shard_map/inner/pallas_call | solution.py:31
  30.5 0.0 copy-start.9
  30.5 0.7 %copy-done.9 = f32[2,5,72,128]{3,2,1,0:T(8,128)} copy-done((f32[2,5,72,128]{3,2,1,0:T(8,128)}, f32[2,5,72,128]{3,2,1,0:T(8,128)S(1)}, u32[]{:S(2)}) %copy-start.9) | copy-done | bytes 368664
  31.2 0.0 copy-start.10
  31.3 0.7 %copy-done.10 = f32[2,5,72,128]{3,2,1,0:T(8,128)} copy-done((f32[2,5,72,128]{3,2,1,0:T(8,128)}, f32[2,5,72,128]{3,2,1,0:T(8,128)S(1)}, u32[]{:S(2)}) %copy-start.10) | copy-done | bytes 368664
  32.0 0.1 slice.36
  32.1 0.1 slice.38
  32.1 0.1 fusion.14
  32.2 0.1 fusion.13
  32.3 0.1 select_reduce_fusion
  32.4 0.1 slice.49
  32.5 0.1 slice.51
  32.6 0.1 fusion.5
  32.6 0.1 slice.50
  32.7 0.1 copy.15
  32.8 0.1 copy.16
  32.9 0.1 slice_select_fusion
  32.9 0.1 fusion.6
  33.0 0.1 slice.53
  33.1 10.0 %collective-permute-start.7 = (f32[2,5,8,128]{3,2,1,0:T(8,128)S(1)}, f32[2,5,8,128]{3,2,1,0:T(8,128)S(1)}, u32[]{:S(2)}, u32[]{:S(2)}) collective-permute-start(f32[2,5,8,128]{3,2,1,0:T(8,128)S(1)} %get-tuple-element.41), channel_id=1, source_target_pairs={{4,499},{12,507},{499,4},{507,12}} | collective-permute-start | bytes 122888 | tf_op jit(solution)/shard_map/ppermute | solution.py:569
  43.1 0.7 %collective-permute-start.6 = (f32[43,8,128]{2,1,0:T(8,128)S(1)}, f32[43,8,128]{2,1,0:T(8,128)S(1)}, u32[]{:S(2)}, u32[]{:S(2)}) collective-permute-start(f32[43,8,128]{2,1,0:T(8,128)S(1)} %payload.1), channel_id=1, source_target_pairs={{0,505},{1,504},{2,507},{3,506},{4,509},{5,508},{6,511},{7,510},{5... | collective-permute-start | bytes 528392 | tf_op jit(solution)/shard_map/ppermute | solution.py:568
  43.8 3.5 %collective-permute-start.2 = (f32[2,5,72,128]{3,2,1,0:T(8,128)}, f32[2,5,72,128]{3,2,1,0:T(8,128)S(1)}, u32[]{:S(2)}, u32[]{:S(2)}) collective-permute-start(f32[2,5,72,128]{3,2,1,0:T(8,128)} %copy-done.10), channel_id=1, source_target_pairs={{0,8},{8,0},{16,24},{24,16},{32,40},{40,32},{48,56},{56,48},{64,72... | collective-permute-start | bytes 1105928 | tf_op jit(solution)/shard_map/ppermute | solution.py:571
  47.3 1.6 %collective-permute-done.7.far = f32[2,5,8,128]{3,2,1,0:T(8,128)S(1)} collective-permute-done((f32[2,5,8,128]{3,2,1,0:T(8,128)S(1)}, f32[2,5,8,128]{3,2,1,0:T(8,128)S(1)}, u32[]{:S(2)}, u32[]{:S(2)}) %collective-permute-start.7) | collective-permute-done | bytes 40992 | tf_op jit(solution)/shard_map/ppermute | solution.py:569
  48.9 1.9 %collective-permute-start.3 = (f32[2,5,72,128]{3,2,1,0:T(8,128)}, f32[2,5,72,128]{3,2,1,0:T(8,128)S(1)}, u32[]{:S(2)}, u32[]{:S(2)}) collective-permute-start(f32[2,5,72,128]{3,2,1,0:T(8,128)} %copy-done.9), channel_id=1, source_target_pairs={{8,16},{16,8},{24,32},{32,24},{40,48},{48,40},{56,64},{64,56},{72,... | collective-permute-start | bytes 1105928 | tf_op jit(solution)/shard_map/ppermute | solution.py:572
  50.8 0.0 collective-permute-done.5.faces
  50.8 0.0 collective-permute-done.6.pass_wrap
  50.9 3.6 %collective-permute-start.9 = (f32[43,8,128]{2,1,0:T(8,128)S(1)}, f32[43,8,128]{2,1,0:T(8,128)S(1)}, u32[]{:S(2)}, u32[]{:S(2)}) collective-permute-start(f32[43,8,128]{2,1,0:T(8,128)S(1)} %collective-permute-done.5.faces), channel_id=1, source_target_pairs={{8,16},{16,8},{24,32},{32,24},{40,48},{48,40},{56,64},{64,56},{72,... | collective-permute-start | bytes 528392 | tf_op jit(solution)/shard_map/ppermute | solution.py:577
  54.5 1.9 %collective-permute-start.8 = (f32[43,8,128]{2,1,0:T(8,128)S(1)}, f32[43,8,128]{2,1,0:T(8,128)S(1)}, u32[]{:S(2)}, u32[]{:S(2)}) collective-permute-start(f32[43,8,128]{2,1,0:T(8,128)S(1)} %collective-permute-done.5.faces), channel_id=1, source_target_pairs={{0,8},{8,0},{16,24},{24,16},{32,40},{40,32},{48,56},{56,48},{64,72... | collective-permute-start | bytes 528392 | tf_op jit(solution)/shard_map/ppermute | solution.py:576
  56.4 0.0 collective-permute-done.4.got_wrap
  56.4 0.0 collective-permute-done.2.got_a
  56.5 1.5 %collective-permute-done.3.got_b = f32[2,5,72,128]{3,2,1,0:T(8,128)S(1)} collective-permute-done((f32[2,5,72,128]{3,2,1,0:T(8,128)}, f32[2,5,72,128]{3,2,1,0:T(8,128)S(1)}, u32[]{:S(2)}, u32[]{:S(2)}) %collective-permute-start.3) | collective-permute-done | bytes 368672 | tf_op jit(solution)/shard_map/ppermute | solution.py:572
  57.9 3.4 %outer.1 = (f32[5,10,32,128]{3,2,1,0:T(8,128)S(1)}, f32[5,10,32,128]{3,2,1,0:T(8,128)S(1)}, f32[2,3,5,16,128]{4,3,2,1,0:T(8,128)S(1)}, f32[5,4,16,128]{3,2,1,0:T(8,128)S(1)}, f32[5,4,16,128]{3,2,1,0:T(8,128)S(1)}) custom-call(s32[6]{0:T(128)S(1)} %stack.48.place, f32[5,5]{1,0:T(8,128)S(1)} %copy-done.6, f32[5,5]{1,0:T(8,128)S(1)} %copy-done.7, ...), custom_call_target="tpu_custom_call" | custom-call | bytes 5652804 | tf_op jit(solution)/shard_map/outer/pallas_call | solution.py:31
  61.3 0.0 collective-permute-done.9.pass_b
  61.3 0.0 collective-permute-done.8.pass_a
  61.3 4.6 %last.1 = (f32[5,8,32,128]{3,2,1,0:T(8,128)}, f32[5,8,32,128]{3,2,1,0:T(8,128)}) custom-call(s32[6]{0:T(128)S(1)} %stack.48.place, f32[5,5]{1,0:T(8,128)S(1)} %copy-done.6, f32[5,5]{1,0:T(8,128)S(1)} %copy-done.7, f32[5,5]{1,0:T(8,128)S(1)} %copy-done.8, f32[5,8,32,128]{3,2,1,0:T(8,128)S(1)} %copy-done.1, f32[5,8,32,128]{3,2,1,0:T(8,128)S(1)} %copy-done.3, ...), custom_call_target="tpu_custom_call" | custom-call | bytes 7022916 | tf_op jit(solution)/shard_map/last/pallas_call | solution.py:31
  (11 shorter events, 0.1 us)
Async XLA Ops:
  0.7 1.1 %copy-start = (f32[5,8,32,128]{3,2,1,0:T(8,128)S(1)}, f32[5,8,32,128]{3,2,1,0:T(8,128)}, u32[]{:S(2)}) copy-start(f32[5,8,32,128]{3,2,1,0:T(8,128)} %flow.9) | copy-start | bytes 1966084
  1.8 1.1 %copy-start.2 = (f32[5,8,32,128]{3,2,1,0:T(8,128)S(1)}, f32[5,8,32,128]{3,2,1,0:T(8,128)}, u32[]{:S(2)}) copy-start(f32[5,8,32,128]{3,2,1,0:T(8,128)} %cotangent.9) | copy-start | bytes 1966084
  3.6 22.9 %copy-start.1 = (f32[5,8,32,128]{3,2,1,0:T(8,128)S(1)}, f32[5,8,32,128]{3,2,1,0:T(8,128)}, u32[]{:S(2)}) copy-start(f32[5,8,32,128]{3,2,1,0:T(8,128)} %flow.9) | copy-start | bytes 1966084
  3.6 22.9 %copy-start.3 = (f32[5,8,32,128]{3,2,1,0:T(8,128)S(1)}, f32[5,8,32,128]{3,2,1,0:T(8,128)}, u32[]{:S(2)}) copy-start(f32[5,8,32,128]{3,2,1,0:T(8,128)} %cotangent.9) | copy-start | bytes 1966084
  3.6 5.3 %collective-permute-start = (f32[2,2,5,8,128]{4,3,2,1,0:T(8,128)S(1)}, f32[2,2,5,8,128]{4,3,2,1,0:T(8,128)S(1)}, u32[]{:S(2)}, u32[]{:S(2)}) collective-permute-start(f32[2,2,5,8,128]{4,3,2,1,0:T(8,128)S(1)} %pack_axial.1), channel_id=1, source_target_pairs={{2,0},{4,2},{6,4},{1,3},{3,5},{5,7},{10,8},{12,10},{14,12},{9,11},... | collective-permute-start | bytes 245768 | tf_op jit(solution)/shard_map/ppermute | solution.py:542
  7.3 1.4 %collective-permute-start.1 = (f32[2,5,8,128]{3,2,1,0:T(8,128)S(1)}, f32[2,5,8,128]{3,2,1,0:T(8,128)S(1)}, u32[]{:S(2)}, u32[]{:S(2)}) collective-permute-start(f32[2,5,8,128]{3,2,1,0:T(8,128)S(1)} %get-tuple-element.41), channel_id=1, source_target_pairs={{3,21},{11,29},{19,37},{20,2},{27,45},{28,10},{35,53},{36,18},{43,... | collective-permute-start | bytes 122888 | tf_op jit(solution)/shard_map/ppermute | solution.py:546
  8.0 48.5 %collective-permute-start.4 = (f32[2,5,72,128]{3,2,1,0:T(8,128)}, f32[2,5,72,128]{3,2,1,0:T(8,128)S(1)}, u32[]{:S(2)}, u32[]{:S(2)}) collective-permute-start(f32[2,5,72,128]{3,2,1,0:T(8,128)} %get-tuple-element.36), channel_id=1, source_target_pairs={{0,504},{504,0},{1,505},{505,1},{2,506},{506,2},{3,507},{507,3},{4... | collective-permute-start | bytes 1105928 | tf_op jit(solution)/shard_map/ppermute | solution.py:547
  8.7 0.7 %copy-start.5 = (s32[512,3]{0,1:T(4,128)S(1)}, s32[512,3]{0,1:T(4,128)}, u32[]{:S(2)}) copy-start(s32[512,3]{0,1:T(4,128)} %param.12) | copy-start | bytes 18436
  8.7 0.7 %copy-start.4 = (s32[512,3]{0,1:T(4,128)S(1)}, s32[512,3]{0,1:T(4,128)}, u32[]{:S(2)}) copy-start(s32[512,3]{0,1:T(4,128)} %param.13) | copy-start | bytes 18436
  9.4 17.1 %copy-start.6 = (f32[5,5]{1,0:T(8,128)S(1)}, f32[5,5]{1,0:T(8,128)}, u32[]{:S(2)}) copy-start(f32[5,5]{1,0:T(8,128)} %mix_t.5) | copy-start | bytes 304
  9.4 17.1 %copy-start.7 = (f32[5,5]{1,0:T(8,128)S(1)}, f32[5,5]{1,0:T(8,128)}, u32[]{:S(2)}) copy-start(f32[5,5]{1,0:T(8,128)} %mix_a.5) | copy-start | bytes 304
  9.4 17.1 %copy-start.8 = (f32[5,5]{1,0:T(8,128)S(1)}, f32[5,5]{1,0:T(8,128)}, u32[]{:S(2)}) copy-start(f32[5,5]{1,0:T(8,128)} %mix_r.5) | copy-start | bytes 304
  10.3 40.6 %collective-permute-start.5 = (f32[43,8,128]{2,1,0:T(8,128)S(1)}, f32[43,8,128]{2,1,0:T(8,128)S(1)}, u32[]{:S(2)}, u32[]{:S(2)}) collective-permute-start(f32[43,8,128]{2,1,0:T(8,128)S(1)} %payload.1), channel_id=1, source_target_pairs={{0,1},{1,0},{2,3},{3,2},{4,5},{5,4},{6,7},{7,6},{8,9},{9,8},{10,11... | collective-permute-start | bytes 528392 | tf_op jit(solution)/shard_map/ppermute | solution.py:554
  30.5 0.7 %copy-start.9 = (f32[2,5,72,128]{3,2,1,0:T(8,128)}, f32[2,5,72,128]{3,2,1,0:T(8,128)S(1)}, u32[]{:S(2)}) copy-start(f32[2,5,72,128]{3,2,1,0:T(8,128)S(1)} %get-tuple-element.35) | copy-start | bytes 1105924
  31.2 0.7 %copy-start.10 = (f32[2,5,72,128]{3,2,1,0:T(8,128)}, f32[2,5,72,128]{3,2,1,0:T(8,128)S(1)}, u32[]{:S(2)}) copy-start(f32[2,5,72,128]{3,2,1,0:T(8,128)S(1)} %get-tuple-element.34) | copy-start | bytes 1105924
  33.1 15.8 %collective-permute-start.7 = (f32[2,5,8,128]{3,2,1,0:T(8,128)S(1)}, f32[2,5,8,128]{3,2,1,0:T(8,128)S(1)}, u32[]{:S(2)}, u32[]{:S(2)}) collective-permute-start(f32[2,5,8,128]{3,2,1,0:T(8,128)S(1)} %get-tuple-element.41), channel_id=1, source_target_pairs={{4,499},{12,507},{499,4},{507,12}} | collective-permute-start | bytes 122888 | tf_op jit(solution)/shard_map/ppermute | solution.py:569
  43.1 7.7 %collective-permute-start.6 = (f32[43,8,128]{2,1,0:T(8,128)S(1)}, f32[43,8,128]{2,1,0:T(8,128)S(1)}, u32[]{:S(2)}, u32[]{:S(2)}) collective-permute-start(f32[43,8,128]{2,1,0:T(8,128)S(1)} %payload.1), channel_id=1, source_target_pairs={{0,505},{1,504},{2,507},{3,506},{4,509},{5,508},{6,511},{7,510},{5... | collective-permute-start | bytes 528392 | tf_op jit(solution)/shard_map/ppermute | solution.py:568
  43.8 12.7 %collective-permute-start.2 = (f32[2,5,72,128]{3,2,1,0:T(8,128)}, f32[2,5,72,128]{3,2,1,0:T(8,128)S(1)}, u32[]{:S(2)}, u32[]{:S(2)}) collective-permute-start(f32[2,5,72,128]{3,2,1,0:T(8,128)} %copy-done.10), channel_id=1, source_target_pairs={{0,8},{8,0},{16,24},{24,16},{32,40},{40,32},{48,56},{56,48},{64,72... | collective-permute-start | bytes 1105928 | tf_op jit(solution)/shard_map/ppermute | solution.py:571
  48.9 9.0 %collective-permute-start.3 = (f32[2,5,72,128]{3,2,1,0:T(8,128)}, f32[2,5,72,128]{3,2,1,0:T(8,128)S(1)}, u32[]{:S(2)}, u32[]{:S(2)}) collective-permute-start(f32[2,5,72,128]{3,2,1,0:T(8,128)} %copy-done.9), channel_id=1, source_target_pairs={{8,16},{16,8},{24,32},{32,24},{40,48},{48,40},{56,64},{64,56},{72,... | collective-permute-start | bytes 1105928 | tf_op jit(solution)/shard_map/ppermute | solution.py:572
  50.9 10.4 %collective-permute-start.9 = (f32[43,8,128]{2,1,0:T(8,128)S(1)}, f32[43,8,128]{2,1,0:T(8,128)S(1)}, u32[]{:S(2)}, u32[]{:S(2)}) collective-permute-start(f32[43,8,128]{2,1,0:T(8,128)S(1)} %collective-permute-done.5.faces), channel_id=1, source_target_pairs={{8,16},{16,8},{24,32},{32,24},{40,48},{48,40},{56,64},{64,56},{72,... | collective-permute-start | bytes 528392 | tf_op jit(solution)/shard_map/ppermute | solution.py:577
  54.5 6.8 %collective-permute-start.8 = (f32[43,8,128]{2,1,0:T(8,128)S(1)}, f32[43,8,128]{2,1,0:T(8,128)S(1)}, u32[]{:S(2)}, u32[]{:S(2)}) collective-permute-start(f32[43,8,128]{2,1,0:T(8,128)S(1)} %collective-permute-done.5.faces), channel_id=1, source_target_pairs={{0,8},{8,0},{16,24},{24,16},{32,40},{40,32},{48,56},{56,48},{64,72... | collective-permute-start | bytes 528392 | tf_op jit(solution)/shard_map/ppermute | solution.py:576

commit v8 on v7

--- a/solution.py
+++ b/solution.py
@@ -562,19 +562,19 @@
         flops=20 * work,
         name="inner",
     )
-    send_a, payload, farsend, slots, codes = lax.optimization_barrier(
-        (send_a, payload, farsend, intersection_slot, intersection_code)
+    send_a, payload, slots, codes = lax.optimization_barrier(
+        (send_a, payload, intersection_slot, intersection_code)
     )
     pass_wrap = lax.ppermute(payload, ("azim", "block"), pairs_pass)
-    far_wrap = lax.ppermute(farsend, ("azim", "block"), pairs_far_wrap)
     weights = interface_weights(slots, codes, columns, sector, block, n_block)
     got_a = lax.ppermute(send_a, "azim", pairs_a)
     got_b = lax.ppermute(send_b, "azim", pairs_near)
-    faces, section, weights, pass_wrap, far_wrap = lax.optimization_barrier(
-        (faces, section, weights, pass_wrap, far_wrap)
+    faces, section, weights, pass_wrap, farsend = lax.optimization_barrier(
+        (faces, section, weights, pass_wrap, farsend)
     )
     pass_a = lax.ppermute(faces, "azim", pairs_a)
     pass_b = lax.ppermute(faces, "azim", pairs_near)
+    far_wrap = lax.ppermute(farsend, ("azim", "block"), pairs_far_wrap)
     section, adjoint, ends, advanced_outer, sensitivity_outer = call(
         outer_kernel,
         (place, *mixers, flow_state, cotangent, got_a, got_b, got_wrap, section, adjoint, reverse_ends),

time: 66.3 us -> 68.7 us (1.036)
  starting transfers between devices: 41.5 us -> 46.2 us
  waiting for transfers between devices: 3.17 us -> 0.39 us
    ppermute x1, starting transfers between devices: 3.53 us -> 11.6 us  [shards(): got_a = lax.ppermute(send_a, 'azim', pairs_a)]
    ppermute x1, starting transfers between devices: 9.99 us -> 5.33 us  [shards(): far_wrap = lax.ppermute(farsend, ('azim', 'block'), pairs_far_wrap)]
    ppermute x1, waiting for transfers between devices: 1.46 us -> 0.01 us  [shards(): got_b = lax.ppermute(send_b, 'azim', pairs_near)]
    ppermute x1, waiting for transfers between devices: 1.56 us -> 0.24 us  [shards(): far_wrap = lax.ppermute(farsend, ('azim', 'block'), pairs_far_wrap)]
    ppermute x1, starting transfers between devices: 1.92 us -> 3.19 us  [shards(): pass_a = lax.ppermute(faces, 'azim', pairs_a)]
  transfers between devices with their start and end apart: 10 -> 10, of which waited for: 3 -> 2; matrix products, arithmetic and copies ran while one was open for 2% -> 2% of each run, Pallas kernels for 15% -> 14%
where the time goes in v8:
time: 68.7 us; the launch traced here: 67.8 us
  starting transfers between devices  46.2 us (67%)
  Pallas kernels  14.8 us (22%)
  local copies, waits for them, and re-layouts  4.91 us (7%)
  between operations  0.97 us (1%)
    ppermute x1, starting transfers between devices, shards(): faces = lax.ppermute(payload, 'block', pairs_long)  16.2 us
    pallas_call x6, Pallas kernels, call(): pl.pallas_call(kernel, out_shape=outs, in_specs=[SMEM if small(x) else VM...  14.8 us
    ppermute x1, starting transfers between devices, shards(): got_a = lax.ppermute(send_a, 'azim', pairs_a)  11.6 us
    ppermute x1, starting transfers between devices, shards(): far_wrap = lax.ppermute(farsend, ('azim', 'block'), pairs_far_wrap)  5.33 us
    unnamed x24, local copies, waits for them, and re-layouts  4.37 us
    ppermute x1, starting transfers between devices, shards(): pass_b = lax.ppermute(faces, 'azim', pairs_near)  3.64 us
    ppermute x1, starting transfers between devices, shards(): pass_a = lax.ppermute(faces, 'azim', pairs_a)  3.19 us
    ppermute x1, starting transfers between devices, shards(): arrived = lax.ppermute(xsend, 'block', pairs_x)  2.29 us
  transfers between devices with their start and end apart: 10, of which 2 were waited for; matrix products, arithmetic and copies ran while one was open for 2% of the time, Pallas kernels for 14%

profile of v8, /device:TPU:5, one launch (start us, length us, event | category | flops | bytes accessed | tf_op | source)
XLA Modules:
  0.0 67.8 jit_solution(13420171257945783985)
XLA Ops:
  0.7 0.1 stack.48.place
  0.7 0.0 copy-start
  0.7 1.1 %copy-done = f32[5,8,32,128]{3,2,1,0:T(8,128)S(1)} copy-done((f32[5,8,32,128]{3,2,1,0:T(8,128)S(1)}, f32[5,8,32,128]{3,2,1,0:T(8,128)}, u32[]{:S(2)}) %copy-start) | copy-done | bytes 655384
  1.8 0.0 copy-start.2
  1.8 1.1 %copy-done.2 = f32[5,8,32,128]{3,2,1,0:T(8,128)S(1)} copy-done((f32[5,8,32,128]{3,2,1,0:T(8,128)S(1)}, f32[5,8,32,128]{3,2,1,0:T(8,128)}, u32[]{:S(2)}) %copy-start.2) | copy-done | bytes 655384
  2.9 0.6 pack_axial.1
  3.6 0.0 copy-start.1
  3.6 0.0 copy-start.3
  3.6 2.3 %collective-permute-start = (f32[2,2,5,8,128]{4,3,2,1,0:T(8,128)S(1)}, f32[2,2,5,8,128]{4,3,2,1,0:T(8,128)S(1)}, u32[]{:S(2)}, u32[]{:S(2)}) collective-permute-start(f32[2,2,5,8,128]{4,3,2,1,0:T(8,128)S(1)} %pack_axial.1), channel_id=1, source_target_pairs={{2,0},{4,2},{6,4},{1,3},{3,5},{5,7},{10,8},{12,10},{14,12},{9,11},... | collective-permute-start | bytes 245768 | tf_op jit(solution)/shard_map/ppermute | solution.py:542
  5.9 1.4 %pack_own.1 = (f32[2,2,5,8,128]{4,3,2,1,0:T(8,128)S(1)}, f32[2,5,72,128]{3,2,1,0:T(8,128)}, f32[2,5,8,128]{3,2,1,0:T(8,128)S(1)}) custom-call(s32[6]{0:T(128)S(1)} %stack.48.place, f32[5,8,32,128]{3,2,1,0:T(8,128)S(1)} %copy-done, f32[5,8,32,128]{3,2,1,0:T(8,128)S(1)} %copy-done.2), custom_call_target="tpu_custom_call" | custom-call | bytes 1802264 | tf_op jit(solution)/shard_map/pack_own/pallas_call | solution.py:31
  7.3 0.7 collective-permute-start.1
  8.0 0.7 %collective-permute-start.4 = (f32[2,5,72,128]{3,2,1,0:T(8,128)}, f32[2,5,72,128]{3,2,1,0:T(8,128)S(1)}, u32[]{:S(2)}, u32[]{:S(2)}) collective-permute-start(f32[2,5,72,128]{3,2,1,0:T(8,128)} %get-tuple-element.35), channel_id=1, source_target_pairs={{0,504},{504,0},{1,505},{505,1},{2,506},{506,2},{3,507},{507,3},{4... | collective-permute-start | bytes 1105928 | tf_op jit(solution)/shard_map/ppermute | solution.py:547
  8.7 0.0 copy-start.5
  8.7 0.0 copy-start.4
  8.8 0.0 collective-permute-done.1.far
  8.8 0.1 collective-permute-done.arrived
  8.9 0.5 copy-done.5
  9.4 0.0 copy-done.4
  9.4 0.0 copy-start.6
  9.4 0.0 copy-start.7
  9.4 0.0 copy-start.8
  9.4 0.8 %payload.1 = f32[43,8,128]{2,1,0:T(8,128)S(1)} custom-call(s32[6]{0:T(128)S(1)} %stack.48.place, s32[3,512]{1,0:T(4,128)S(1)} %bitcast.19, s32[3,512]{1,0:T(4,128)S(1)} %bitcast.18, f32[2,2,5,8,128]{4,3,2,1,0:T(8,128)S(1)} %collective-permute-done.arrived, f32[2,2,5,8,128]{4,3,2,1,0:T(8,128)S(1)} %get-tuple-element.28.own, ...), custom_call_target="tpu_custom_call" | custom-call | bytes 393240 | tf_op jit(solution)/shard_map/payload/pallas_call | solution.py:31
  10.3 16.2 %collective-permute-start.5 = (f32[43,8,128]{2,1,0:T(8,128)S(1)}, f32[43,8,128]{2,1,0:T(8,128)S(1)}, u32[]{:S(2)}, u32[]{:S(2)}) collective-permute-start(f32[43,8,128]{2,1,0:T(8,128)S(1)} %payload.1), channel_id=1, source_target_pairs={{0,1},{1,0},{2,3},{3,2},{4,5},{5,4},{6,7},{7,6},{8,9},{9,8},{10,11... | collective-permute-start | bytes 528392 | tf_op jit(solution)/shard_map/ppermute | solution.py:554
  26.5 0.0 copy-done.1
  26.5 0.0 copy-done.3
  26.5 0.0 copy-done.6
  26.5 0.0 copy-done.7
  26.5 0.0 copy-done.8
  26.6 4.0 %inner.1 = (f32[5,6,32,128]{3,2,1,0:T(8,128)S(1)}, f32[5,6,32,128]{3,2,1,0:T(8,128)S(1)}, f32[2,5,8,128]{3,2,1,0:T(8,128)S(1)}, f32[5,4,16,128]{3,2,1,0:T(8,128)...) custom-call(s32[6]{0:T(128)S(1)} %stack.48.place, ...), custom_call_target="tpu_custom_call" | custom-call | flops 196608000 | bytes 3400004 | tf_op jit(solution)/shard_map/inner/pallas_call | solution.py:31
  30.5 0.0 copy-start.9
  30.5 0.7 %copy-done.9 = f32[2,5,72,128]{3,2,1,0:T(8,128)} copy-done((f32[2,5,72,128]{3,2,1,0:T(8,128)}, f32[2,5,72,128]{3,2,1,0:T(8,128)S(1)}, u32[]{:S(2)}) %copy-start.9) | copy-done | bytes 368664
  31.2 0.0 copy-start.10
  31.3 0.7 %copy-done.10 = f32[2,5,72,128]{3,2,1,0:T(8,128)} copy-done((f32[2,5,72,128]{3,2,1,0:T(8,128)}, f32[2,5,72,128]{3,2,1,0:T(8,128)S(1)}, u32[]{:S(2)}) %copy-start.10) | copy-done | bytes 368664
  32.0 0.1 slice.36
  32.1 0.1 slice.38
  32.1 0.1 fusion.14
  32.2 0.1 fusion.13
  32.3 0.1 select_reduce_fusion
  32.4 0.1 slice.49
  32.5 0.1 slice.51
  32.6 0.1 fusion.5
  32.6 0.1 slice.50
  32.7 0.1 copy.15
  32.8 0.1 copy.16
  32.9 0.1 slice_select_fusion
  32.9 0.1 fusion.6
  33.0 0.1 slice.53
  33.1 0.7 collective-permute-start.6
  33.8 11.6 %collective-permute-start.2 = (f32[2,5,72,128]{3,2,1,0:T(8,128)}, f32[2,5,72,128]{3,2,1,0:T(8,128)S(1)}, u32[]{:S(2)}, u32[]{:S(2)}) collective-permute-start(f32[2,5,72,128]{3,2,1,0:T(8,128)} %copy-done.10), channel_id=1, source_target_pairs={{0,8},{8,0},{16,24},{24,16},{32,40},{40,32},{48,56},{56,48},{64,72... | collective-permute-start | bytes 1105928 | tf_op jit(solution)/shard_map/ppermute | solution.py:570
  45.4 1.9 %collective-permute-start.3 = (f32[2,5,72,128]{3,2,1,0:T(8,128)}, f32[2,5,72,128]{3,2,1,0:T(8,128)S(1)}, u32[]{:S(2)}, u32[]{:S(2)}) collective-permute-start(f32[2,5,72,128]{3,2,1,0:T(8,128)} %copy-done.9), channel_id=1, source_target_pairs={{8,16},{16,8},{24,32},{32,24},{40,48},{48,40},{56,64},{64,56},{72,... | collective-permute-start | bytes 1105928 | tf_op jit(solution)/shard_map/ppermute | solution.py:571
  47.4 0.0 collective-permute-done.5.faces
  47.4 0.0 collective-permute-done.6.pass_wrap
  47.4 3.6 %collective-permute-start.8 = (f32[43,8,128]{2,1,0:T(8,128)S(1)}, f32[43,8,128]{2,1,0:T(8,128)S(1)}, u32[]{:S(2)}, u32[]{:S(2)}) collective-permute-start(f32[43,8,128]{2,1,0:T(8,128)S(1)} %collective-permute-done.5.faces), channel_id=1, source_target_pairs={{8,16},{16,8},{24,32},{32,24},{40,48},{48,40},{56,64},{64,56},{72,... | collective-permute-start | bytes 528392 | tf_op jit(solution)/shard_map/ppermute | solution.py:576
  51.0 3.2 %collective-permute-start.7 = (f32[43,8,128]{2,1,0:T(8,128)S(1)}, f32[43,8,128]{2,1,0:T(8,128)S(1)}, u32[]{:S(2)}, u32[]{:S(2)}) collective-permute-start(f32[43,8,128]{2,1,0:T(8,128)S(1)} %collective-permute-done.5.faces), channel_id=1, source_target_pairs={{0,8},{8,0},{16,24},{24,16},{32,40},{40,32},{48,56},{56,48},{64,72... | collective-permute-start | bytes 528392 | tf_op jit(solution)/shard_map/ppermute | solution.py:575
  54.2 0.0 collective-permute-done.4.got_wrap
  54.2 5.3 %collective-permute-start.9 = (f32[2,5,8,128]{3,2,1,0:T(8,128)S(1)}, f32[2,5,8,128]{3,2,1,0:T(8,128)S(1)}, u32[]{:S(2)}, u32[]{:S(2)}) collective-permute-start(f32[2,5,8,128]{3,2,1,0:T(8,128)S(1)} %get-tuple-element.48), channel_id=1, source_target_pairs={{4,499},{12,507},{499,4},{507,12}} | collective-permute-start | bytes 122888 | tf_op jit(solution)/shard_map/ppermute | solution.py:577
  59.6 0.0 collective-permute-done.2.got_a
  59.6 0.0 collective-permute-done.3.got_b
  59.6 3.4 %outer.1 = (f32[5,10,32,128]{3,2,1,0:T(8,128)S(1)}, f32[5,10,32,128]{3,2,1,0:T(8,128)S(1)}, f32[2,3,5,16,128]{4,3,2,1,0:T(8,128)S(1)}, f32[5,4,16,128]{3,2,1,0:T(8,128)S(1)}, f32[5,4,16,128]{3,2,1,0:T(8,128)S(1)}) custom-call(s32[6]{0:T(128)S(1)} %stack.48.place, f32[5,5]{1,0:T(8,128)S(1)} %copy-done.6, f32[5,5]{1,0:T(8,128)S(1)} %copy-done.7, ...), custom_call_target="tpu_custom_call" | custom-call | bytes 5652804 | tf_op jit(solution)/shard_map/outer/pallas_call | solution.py:31
  63.0 0.2 collective-permute-done.9.far
  63.2 0.0 collective-permute-done.8.pass_b
  63.2 0.0 collective-permute-done.7.pass_a
  63.2 4.6 %last.1 = (f32[5,8,32,128]{3,2,1,0:T(8,128)}, f32[5,8,32,128]{3,2,1,0:T(8,128)}) custom-call(s32[6]{0:T(128)S(1)} %stack.48.place, f32[5,5]{1,0:T(8,128)S(1)} %copy-done.6, f32[5,5]{1,0:T(8,128)S(1)} %copy-done.7, f32[5,5]{1,0:T(8,128)S(1)} %copy-done.8, f32[5,8,32,128]{3,2,1,0:T(8,128)S(1)} %copy-done.1, f32[5,8,32,128]{3,2,1,0:T(8,128)S(1)} %copy-done.3, ...), custom_call_target="tpu_custom_call" | custom-call | bytes 7022916 | tf_op jit(solution)/shard_map/last/pallas_call | solution.py:31
  (11 shorter events, 0.1 us)
Async XLA Ops:
  0.7 1.1 %copy-start = (f32[5,8,32,128]{3,2,1,0:T(8,128)S(1)}, f32[5,8,32,128]{3,2,1,0:T(8,128)}, u32[]{:S(2)}) copy-start(f32[5,8,32,128]{3,2,1,0:T(8,128)} %flow.9) | copy-start | bytes 1966084
  1.8 1.1 %copy-start.2 = (f32[5,8,32,128]{3,2,1,0:T(8,128)S(1)}, f32[5,8,32,128]{3,2,1,0:T(8,128)}, u32[]{:S(2)}) copy-start(f32[5,8,32,128]{3,2,1,0:T(8,128)} %cotangent.9) | copy-start | bytes 1966084
  3.6 22.9 %copy-start.1 = (f32[5,8,32,128]{3,2,1,0:T(8,128)S(1)}, f32[5,8,32,128]{3,2,1,0:T(8,128)}, u32[]{:S(2)}) copy-start(f32[5,8,32,128]{3,2,1,0:T(8,128)} %flow.9) | copy-start | bytes 1966084
  3.6 22.9 %copy-start.3 = (f32[5,8,32,128]{3,2,1,0:T(8,128)S(1)}, f32[5,8,32,128]{3,2,1,0:T(8,128)}, u32[]{:S(2)}) copy-start(f32[5,8,32,128]{3,2,1,0:T(8,128)} %cotangent.9) | copy-start | bytes 1966084
  3.6 5.3 %collective-permute-start = (f32[2,2,5,8,128]{4,3,2,1,0:T(8,128)S(1)}, f32[2,2,5,8,128]{4,3,2,1,0:T(8,128)S(1)}, u32[]{:S(2)}, u32[]{:S(2)}) collective-permute-start(f32[2,2,5,8,128]{4,3,2,1,0:T(8,128)S(1)} %pack_axial.1), channel_id=1, source_target_pairs={{2,0},{4,2},{6,4},{1,3},{3,5},{5,7},{10,8},{12,10},{14,12},{9,11},... | collective-permute-start | bytes 245768 | tf_op jit(solution)/shard_map/ppermute | solution.py:542
  7.3 1.4 %collective-permute-start.1 = (f32[2,5,8,128]{3,2,1,0:T(8,128)S(1)}, f32[2,5,8,128]{3,2,1,0:T(8,128)S(1)}, u32[]{:S(2)}, u32[]{:S(2)}) collective-permute-start(f32[2,5,8,128]{3,2,1,0:T(8,128)S(1)} %get-tuple-element.48), channel_id=1, source_target_pairs={{3,21},{11,29},{19,37},{20,2},{27,45},{28,10},{35,53},{36,18},{43,... | collective-permute-start | bytes 122888 | tf_op jit(solution)/shard_map/ppermute | solution.py:546
  8.0 46.2 %collective-permute-start.4 = (f32[2,5,72,128]{3,2,1,0:T(8,128)}, f32[2,5,72,128]{3,2,1,0:T(8,128)S(1)}, u32[]{:S(2)}, u32[]{:S(2)}) collective-permute-start(f32[2,5,72,128]{3,2,1,0:T(8,128)} %get-tuple-element.35), channel_id=1, source_target_pairs={{0,504},{504,0},{1,505},{505,1},{2,506},{506,2},{3,507},{507,3},{4... | collective-permute-start | bytes 1105928 | tf_op jit(solution)/shard_map/ppermute | solution.py:547
  8.7 0.7 %copy-start.5 = (s32[512,3]{0,1:T(4,128)S(1)}, s32[512,3]{0,1:T(4,128)}, u32[]{:S(2)}) copy-start(s32[512,3]{0,1:T(4,128)} %param.12) | copy-start | bytes 18436
  8.7 0.7 %copy-start.4 = (s32[512,3]{0,1:T(4,128)S(1)}, s32[512,3]{0,1:T(4,128)}, u32[]{:S(2)}) copy-start(s32[512,3]{0,1:T(4,128)} %param.13) | copy-start | bytes 18436
  9.4 17.1 %copy-start.6 = (f32[5,5]{1,0:T(8,128)S(1)}, f32[5,5]{1,0:T(8,128)}, u32[]{:S(2)}) copy-start(f32[5,5]{1,0:T(8,128)} %mix_t.5) | copy-start | bytes 304
  9.4 17.1 %copy-start.7 = (f32[5,5]{1,0:T(8,128)S(1)}, f32[5,5]{1,0:T(8,128)}, u32[]{:S(2)}) copy-start(f32[5,5]{1,0:T(8,128)} %mix_a.5) | copy-start | bytes 304
  9.4 17.1 %copy-start.8 = (f32[5,5]{1,0:T(8,128)S(1)}, f32[5,5]{1,0:T(8,128)}, u32[]{:S(2)}) copy-start(f32[5,5]{1,0:T(8,128)} %mix_r.5) | copy-start | bytes 304
  10.3 37.1 %collective-permute-start.5 = (f32[43,8,128]{2,1,0:T(8,128)S(1)}, f32[43,8,128]{2,1,0:T(8,128)S(1)}, u32[]{:S(2)}, u32[]{:S(2)}) collective-permute-start(f32[43,8,128]{2,1,0:T(8,128)S(1)} %payload.1), channel_id=1, source_target_pairs={{0,1},{1,0},{2,3},{3,2},{4,5},{5,4},{6,7},{7,6},{8,9},{9,8},{10,11... | collective-permute-start | bytes 528392 | tf_op jit(solution)/shard_map/ppermute | solution.py:554
  30.5 0.7 %copy-start.9 = (f32[2,5,72,128]{3,2,1,0:T(8,128)}, f32[2,5,72,128]{3,2,1,0:T(8,128)S(1)}, u32[]{:S(2)}) copy-start(f32[2,5,72,128]{3,2,1,0:T(8,128)S(1)} %get-tuple-element.34) | copy-start | bytes 1105924
  31.2 0.7 %copy-start.10 = (f32[2,5,72,128]{3,2,1,0:T(8,128)}, f32[2,5,72,128]{3,2,1,0:T(8,128)S(1)}, u32[]{:S(2)}) copy-start(f32[2,5,72,128]{3,2,1,0:T(8,128)S(1)} %get-tuple-element.33) | copy-start | bytes 1105924
  33.1 14.3 %collective-permute-start.6 = (f32[43,8,128]{2,1,0:T(8,128)S(1)}, f32[43,8,128]{2,1,0:T(8,128)S(1)}, u32[]{:S(2)}, u32[]{:S(2)}) collective-permute-start(f32[43,8,128]{2,1,0:T(8,128)S(1)} %payload.1), channel_id=1, source_target_pairs={{0,505},{1,504},{2,507},{3,506},{4,509},{5,508},{6,511},{7,510},{5... | collective-permute-start | bytes 528392 | tf_op jit(solution)/shard_map/ppermute | solution.py:568
  33.8 25.8 %collective-permute-start.2 = (f32[2,5,72,128]{3,2,1,0:T(8,128)}, f32[2,5,72,128]{3,2,1,0:T(8,128)S(1)}, u32[]{:S(2)}, u32[]{:S(2)}) collective-permute-start(f32[2,5,72,128]{3,2,1,0:T(8,128)} %copy-done.10), channel_id=1, source_target_pairs={{0,8},{8,0},{16,24},{24,16},{32,40},{40,32},{48,56},{56,48},{64,72... | collective-permute-start | bytes 1105928 | tf_op jit(solution)/shard_map/ppermute | solution.py:570
  45.4 14.2 %collective-permute-start.3 = (f32[2,5,72,128]{3,2,1,0:T(8,128)}, f32[2,5,72,128]{3,2,1,0:T(8,128)S(1)}, u32[]{:S(2)}, u32[]{:S(2)}) collective-permute-start(f32[2,5,72,128]{3,2,1,0:T(8,128)} %copy-done.9), channel_id=1, source_target_pairs={{8,16},{16,8},{24,32},{32,24},{40,48},{48,40},{56,64},{64,56},{72,... | collective-permute-start | bytes 1105928 | tf_op jit(solution)/shard_map/ppermute | solution.py:571
  47.4 15.8 %collective-permute-start.8 = (f32[43,8,128]{2,1,0:T(8,128)S(1)}, f32[43,8,128]{2,1,0:T(8,128)S(1)}, u32[]{:S(2)}, u32[]{:S(2)}) collective-permute-start(f32[43,8,128]{2,1,0:T(8,128)S(1)} %collective-permute-done.5.faces), channel_id=1, source_target_pairs={{8,16},{16,8},{24,32},{32,24},{40,48},{48,40},{56,64},{64,56},{72,... | collective-permute-start | bytes 528392 | tf_op jit(solution)/shard_map/ppermute | solution.py:576
  51.0 12.2 %collective-permute-start.7 = (f32[43,8,128]{2,1,0:T(8,128)S(1)}, f32[43,8,128]{2,1,0:T(8,128)S(1)}, u32[]{:S(2)}, u32[]{:S(2)}) collective-permute-start(f32[43,8,128]{2,1,0:T(8,128)S(1)} %collective-permute-done.5.faces), channel_id=1, source_target_pairs={{0,8},{8,0},{16,24},{24,16},{32,40},{40,32},{48,56},{56,48},{64,72... | collective-permute-start | bytes 528392 | tf_op jit(solution)/shard_map/ppermute | solution.py:575
  54.2 9.0 %collective-permute-start.9 = (f32[2,5,8,128]{3,2,1,0:T(8,128)S(1)}, f32[2,5,8,128]{3,2,1,0:T(8,128)S(1)}, u32[]{:S(2)}, u32[]{:S(2)}) collective-permute-start(f32[2,5,8,128]{3,2,1,0:T(8,128)S(1)} %get-tuple-element.48), channel_id=1, source_target_pairs={{4,499},{12,507},{499,4},{507,12}} | collective-permute-start | bytes 122888 | tf_op jit(solution)/shard_map/ppermute | solution.py:577
